TPU v7x, 128 devices: a whole 4x4x4 slice. The times are simulated.
128 devices in a mesh: node: 16 (over z, y), local: 8 (over x, core).
Axes of the slice: x: 4, y: 4, z: 4, core: 2. Of those that a mesh axis runs over, the one named last changes fastest.
Arguments:
- hidden: bfloat16 [16384, 3584], P(('node', 'local')), may hold values from -6 to 6
- latent_weight: bfloat16 [3584, 576], P('node'), may hold values from -0.09375 to 0.09375
- latent_gain: float32 [512], replicated, may hold values from 0.1 to 1.9
- queries: bfloat16 [16384, 12288], P(('node', 'local')), may hold values from -200 to 200
- kv_weight: bfloat16 [512, 16384], P('node', 'local'), may hold values from -0.25 to 0.25
- expert_ids: int32 [16384, 8], P(('node', 'local')), may hold values from 0 to 255, as said below
- route_weights: float32 [16384, 8], P(('node', 'local')), may hold values from 0.05 to 0.6
- gate_proj: bfloat16 [128, 3584, 512], P(('node', 'local')), may hold values from -0.09375 to 0.09375
- up_proj: bfloat16 [128, 3584, 512], P(('node', 'local')), may hold values from -0.09375 to 0.09375
- down_proj: bfloat16 [128, 512, 3584], P(('node', 'local')), may hold values from -0.1875 to 0.1875
Outputs:
- attention: bfloat16 [16384, 8192], P(('node', 'local'))
- routed: bfloat16 [16384, 3584], P(('node', 'local'))
Inputs may be any that keep to these rules, and one draw needn't show every extreme that they name: `expert_ids`: each row names 8 different experts, all of them in at most 4 of the 8 groups of 32 consecutive expert numbers.
All inputs are finite; a program needn't handle non-finite values.
Results may differ from a plain program's by a relative error of at most 0.014.
The roundings to bfloat16 on the way count: a program that leaves them out, or rounds other values in their place, can miss the bound.
Values may be sent and summed in bfloat16 or wider, within the bound.
No kernel may reach another device: no remote copies, remote signals or barrier semaphores. Data moves between devices by JAX's collectives and lax.ppermute only.
A program may use at most 128 MiB of HBM per device.

v0:
```python
import math

import jax
import jax.numpy as jnp
from jax import lax
from jax.sharding import PartitionSpec as P

NOPE = 128
ROPE = 64
VDIM = 128
LAT = 512
EXPERTS = 256
TOPK = 8
CAP = 8


def normalize(columns, latent_gain):
    mean_square = jnp.mean(columns * columns, axis=1, keepdims=True)
    return (columns * lax.rsqrt(mean_square + 1e-06) * latent_gain[None, :]).astype(jnp.bfloat16)


def rotate_keys(rope_part, position):
    half_width = ROPE // 2
    freqs = 10000.0 ** (-2.0 * jnp.arange(half_width, dtype=jnp.float32) / ROPE)
    angles = position.astype(jnp.float32)[:, None] * freqs[None, :]
    cosine = jnp.cos(angles)
    sine = jnp.sin(angles)
    first_half = rope_part[:, :half_width]
    second_half = rope_part[:, half_width:]
    return jnp.concatenate(
        [first_half * cosine - second_half * sine, second_half * cosine + first_half * sine], axis=1
    )


def attend_head(query_rows, keyval, keys_rope):
    length = query_rows.shape[0]
    q_block = min(length, 512)
    keys_nope = keyval[:, :NOPE]
    values = keyval[:, NOPE:]
    scale = 1.0 / math.sqrt(NOPE + ROPE)

    def one_block(block_index):
        offset = block_index * q_block
        block_rows = lax.dynamic_slice_in_dim(query_rows, offset, q_block, 0)
        scores = jnp.einsum(
            "qd,kd->qk", block_rows[:, :NOPE], keys_nope, preferred_element_type=jnp.float32
        )
        scores = scores + jnp.einsum(
            "qd,kd->qk", block_rows[:, NOPE:], keys_rope, preferred_element_type=jnp.float32
        )
        scores = scores * scale
        query_pos = offset + jnp.arange(q_block, dtype=jnp.int32)[:, None]
        key_pos = jnp.arange(length, dtype=jnp.int32)[None, :]
        scores = jnp.where(key_pos <= query_pos, scores, -1e30)
        row_max = jnp.max(scores, axis=1, keepdims=True)
        weights = jnp.exp(scores - row_max)
        probs = (weights / jnp.sum(weights, axis=1, keepdims=True)).astype(jnp.bfloat16)
        return jnp.dot(probs, values, preferred_element_type=jnp.float32).astype(jnp.bfloat16)

    blocks = lax.map(one_block, jnp.arange(length // q_block, dtype=jnp.int32))
    return blocks.reshape(length, values.shape[1])


def send_rows(buffer):
    return lax.all_to_all(buffer, ("node", "local"), split_axis=0, concat_axis=0, tiled=True)


def return_rows(buffer):
    return lax.all_to_all(buffer, ("node", "local"), split_axis=0, concat_axis=0, tiled=True)


def expert_half(row_block, gate_proj, up_proj, down_proj):
    stacked = row_block.reshape(-1, row_block.shape[-1])
    gate = jnp.dot(stacked, gate_proj[0], preferred_element_type=jnp.float32)
    upper = jnp.dot(stacked, up_proj[0], preferred_element_type=jnp.float32)
    inner = (jax.nn.silu(gate) * upper).astype(jnp.bfloat16)
    return (
        jnp.dot(inner, down_proj[0], preferred_element_type=jnp.float32)
        .astype(jnp.bfloat16)
        .reshape(row_block.shape)
    )


def shards(
    hidden,
    latent_weight,
    latent_gain,
    queries,
    kv_weight,
    expert_ids,
    route_weights,
    gate_proj,
    up_proj,
    down_proj,
):
    tok_rows = hidden.shape[0]
    width = hidden.shape[1]
    devices = lax.axis_size("node") * lax.axis_size("local")
    columns = hidden
    latent = jnp.dot(
        columns,
        lax.all_gather(latent_weight, "node", axis=0, tiled=True),
        preferred_element_type=jnp.float32,
    )
    position = lax.axis_index("local") * tok_rows + jnp.arange(tok_rows, dtype=jnp.int32)
    compressed = normalize(latent[:, :LAT], latent_gain)
    rope_keys = rotate_keys(latent[:, LAT:], position).astype(jnp.bfloat16)
    sequence = lax.all_gather(
        jnp.concatenate([compressed, rope_keys], axis=1), "local", axis=0, tiled=True
    )
    length = sequence.shape[0]
    head_queries = lax.all_to_all(queries, "local", split_axis=1, concat_axis=0, tiled=True)
    heads_here = head_queries.shape[1] // (NOPE + ROPE)
    portion = lax.all_gather(kv_weight, "node", axis=0, tiled=True)
    columns = lax.slice_in_dim(sequence, 0, portion.shape[0], axis=1)
    keyval = jnp.dot(columns, portion, preferred_element_type=jnp.float32).astype(jnp.bfloat16)
    keys_rope = sequence[:, LAT:]
    query_stack = head_queries.reshape(length, heads_here, NOPE + ROPE).transpose(1, 0, 2)
    keyval_stack = keyval.reshape(length, heads_here, NOPE + VDIM).transpose(1, 0, 2)
    outputs = lax.map(
        lambda head_pair: attend_head(head_pair[0], head_pair[1], keys_rope),
        (query_stack, keyval_stack),
    )
    merged = outputs.transpose(1, 0, 2).reshape(length, heads_here * VDIM)
    attention = lax.all_to_all(merged, "local", split_axis=0, concat_axis=1, tiled=True)
    flight = devices // 2
    stride = EXPERTS // flight
    routes_flat = expert_ids.reshape(-1)
    in_flight = routes_flat % stride == 0
    target = routes_flat // stride
    onehot = (
        (target[:, None] == jnp.arange(flight, dtype=jnp.int32)[None, :]) & in_flight[:, None]
    ).astype(jnp.int32)
    slot_index = jnp.sum((jnp.cumsum(onehot, axis=0) - onehot) * onehot, axis=1)
    kept_mask = in_flight & (slot_index < CAP)
    dump_slot = flight * CAP
    place_index = jnp.where(kept_mask, target * CAP + slot_index, dump_slot)
    token_index = jnp.arange(routes_flat.shape[0], dtype=jnp.int32) // TOPK
    row_table = (
        jnp.full((dump_slot + 1,), tok_rows, jnp.int32).at[place_index].set(token_index)[:dump_slot]
    )
    padded = jnp.concatenate([hidden, jnp.zeros((1, width), jnp.bfloat16)], axis=0)
    outgoing = padded[row_table].reshape(flight, CAP, width)
    doubled = jnp.broadcast_to(outgoing[:, None], (flight, 2, CAP, width)).reshape(
        devices, CAP, width
    )
    arrived = send_rows(doubled)
    partial_value = expert_half(arrived, gate_proj, up_proj, down_proj)
    returned = return_rows(partial_value).reshape(flight, 2, CAP, width)
    results = (returned[:, 0].astype(jnp.float32) + returned[:, 1].astype(jnp.float32)).astype(
        jnp.bfloat16
    )
    results = results.reshape(flight * CAP, width)
    results = jnp.concatenate([results, jnp.zeros((1, width), jnp.bfloat16)], axis=0)
    route_index = place_index.reshape(tok_rows, TOPK)
    routed = jnp.zeros((tok_rows, width), jnp.float32)
    for column in range(TOPK):
        routed = routed + route_weights[:, column : column + 1] * results[
            route_index[:, column]
        ].astype(jnp.float32)
    return (attention, routed.astype(jnp.bfloat16))


def solution(mesh):
    placed = (
        P(("node", "local"), None),
        P("node", None),
        P(),
        P(("node", "local"), None),
        P("node", "local"),
        P(("node", "local"), None),
        P(("node", "local"), None),
        P(("node", "local"), None, None),
        P(("node", "local"), None, None),
        P(("node", "local"), None, None),
    )
    return jax.shard_map(
        shards,
        mesh=mesh,
        in_specs=placed,
        out_specs=(P(("node", "local"), None), P(("node", "local"), None)),
        check_vma=False,
    )
```

profile of v0, /device:TPU:0, one launch (start us, length us, event | category | flops | bytes accessed | tf_op | source)
XLA Modules:
  0.0 450.6 jit_solution(15767828511904910385)
XLA Ops:
  8.6 4.7 %copy.50 = bf16[128,12288]{0,1:T(8,128)(2,1)} copy(bf16[128,12288]{1,0:T(8,128)(2,1)} %param.17) | data formatting | bytes 6291456 | tf_op args[3]
  13.3 4.6 %all-to-all-start = ((bf16[128,8,1536]{0,2,1:T(8,128)(2,1)}), bf16[128,8,1536]{0,2,1:T(8,128)(2,1)}, u32[]{:S(2)}, u32[]{:S(2)}) async-start(bf16[128,8,1536]{0,2,1:T(8,128)(2,1)} %bitcast.5), calls=%async_computation | async-start | bytes 6291456 | tf_op jit(solution)/shard_map/all_to_all | solution.py:112
  18.4 47.7 %all-gather.4.cloned.1.call-done = bf16[3584,576]{1,0:T(8,128)(2,1)} async-done(((bf16[224,576]{1,0:T(8,128)(2,1)}), bf16[3584,576]{1,0:T(8,128)(2,1)}) %all-gather.4.cloned.1.call-update) | async-done | bytes 4128784 | tf_op jit(solution)/shard_map/all_gather | solution.py:102
  66.1 4.1 fusion.69
  71.4 18.0 %reduce-window.6 = s32[64,8,128]{2,1,0:T(8,128)S(1)} reduce-window(s32[64,8,128]{2,1,0:T(8,128)S(1)} %fusion.31, s32[]{:T(128)} %constant.101.clone.1), window={size=1x1x128 pad=0_0x0_0x127_0}, to_apply=%region_7.8 | reduce-window | flops 8323072 | bytes 524292 | tf_op jit(solution)/shard_map/reduce-window
  90.8 4.3 scatter_custom_fusion
  95.1 4.2 gather_fusion
  99.4 5.6 %broadcast_in_dim.37 = bf16[64,2,8,3584]{3,2,1,0:T(8,128)(2,1)} broadcast(bf16[64,8,3584]{2,1,0:T(8,128)(2,1)} %bitcast.123), dimensions={0,2,3} | broadcast | bytes 11010048 | tf_op jit(solution)/shard_map/broadcast_in_dim | solution.py:144
  105.0 9.1 %all-to-all-start.2 = ((bf16[128,8,3584]{2,1,0:T(8,128)(2,1)}), bf16[128,8,3584]{2,1,0:T(8,128)(2,1)}, u32[]{:S(2)}, u32[]{:S(2)}) async-start(bf16[128,8,3584]{2,1,0:T(8,128)(2,1)} %bitcast.122), calls=%async_computation.2 | async-start | bytes 14680064 | tf_op jit(solution)/shard_map/all_to_all | solution.py:65
  114.1 9.6 %copy.51 = bf16[8,128,1536]{1,0,2:T(8,128)(2,1)S(1)} copy(bf16[8,128,1536]{1,2,0:T(8,128)(2,1)} %bitcast.6) | data formatting | bytes 6291456 | tf_op jit(solution)/shard_map/all_to_all | solution.py:112
  123.7 3.3 reshape.248
  127.1 21.4 %all-gather.6.cloned.1.call-done = bf16[1024,576]{0,1:T(8,128)(2,1)} async-done(((bf16[128,576]{0,1:T(8,128)(2,1)}), bf16[1024,576]{0,1:T(8,128)(2,1)}) %all-gather.6.cloned.1.call-update) | async-done | bytes 1179664 | tf_op jit(solution)/shard_map/all_gather | solution.py:108
  148.4 4.3 convolution_convert_fusion.2
  152.7 2.3 copy.76
  155.2 92.4 %while.21 = (s32[]{:T(128)}, bf16[8,1024,128]{2,1,0:T(8,128)(2,1)}, bf16[8,1024,192]{1,2,0:T(8,128)(2,1)}, bf16[8,1024,256]{2,1,0:T(8,128)(2,1)}, bf16[1024,64]{...) while((s32[]{:T(128)}, bf16[8,1024,128]{2,1,0:T(8,128)(2,1)}, ...), condition=%wide.region_6.7_spmd, body=%wide.region_1.6_spmd.sunk | while | flops 340852224 | bytes 16923608 | solution.py:120
  155.2 1.1 dynamic-slice_bitcast_fusion.2
  156.3 0.7 fusion.85
  157.0 1.0 constant_dynamic-slice_fusion.2
  158.3 7.7 %while.22 = (s32[]{:T(128)}, bf16[2,512,128]{2,1,0:T(8,128)(2,1)S(1)}, s32[2]{0:T(128)S(1)}, bf16[1024,192]{1,0:T(8,128)(2,1)S(1)}, bf16[1024,128]{1,0:T(8,128)(...) while((s32[]{:T(128)}, ...), condition=%wide.region_5.5_spmd, body=%wide.region_2.4_spmd.sunk | while | flops 340852224 | bytes 12728555 | solution.py:60
  166.7 1.1 dynamic-slice_bitcast_fusion.2
  168.5 1.0 constant_dynamic-slice_fusion.2
  169.8 7.7 %while.22 = (s32[]{:T(128)}, bf16[2,512,128]{2,1,0:T(8,128)(2,1)S(1)}, s32[2]{0:T(128)S(1)}, bf16[1024,192]{1,0:T(8,128)(2,1)S(1)}, bf16[1024,128]{1,0:T(8,128)(...) while((s32[]{:T(128)}, ...), condition=%wide.region_5.5_spmd, body=%wide.region_2.4_spmd.sunk | while | flops 340852224 | bytes 12728555 | solution.py:60
  178.3 1.1 dynamic-slice_bitcast_fusion.2
  179.4 0.7 fusion.85
  180.1 1.0 constant_dynamic-slice_fusion.2
  181.3 7.7 %while.22 = (s32[]{:T(128)}, bf16[2,512,128]{2,1,0:T(8,128)(2,1)S(1)}, s32[2]{0:T(128)S(1)}, bf16[1024,192]{1,0:T(8,128)(2,1)S(1)}, bf16[1024,128]{1,0:T(8,128)(...) while((s32[]{:T(128)}, ...), condition=%wide.region_5.5_spmd, body=%wide.region_2.4_spmd.sunk | while | flops 340852224 | bytes 12728555 | solution.py:60
  189.8 1.1 dynamic-slice_bitcast_fusion.2
  190.9 0.7 fusion.85
  191.6 1.0 constant_dynamic-slice_fusion.2
  192.9 7.7 %while.22 = (s32[]{:T(128)}, bf16[2,512,128]{2,1,0:T(8,128)(2,1)S(1)}, s32[2]{0:T(128)S(1)}, bf16[1024,192]{1,0:T(8,128)(2,1)S(1)}, bf16[1024,128]{1,0:T(8,128)(...) while((s32[]{:T(128)}, ...), condition=%wide.region_5.5_spmd, body=%wide.region_2.4_spmd.sunk | while | flops 340852224 | bytes 12728555 | solution.py:60
  201.4 1.1 dynamic-slice_bitcast_fusion.2
  202.4 0.7 fusion.85
  203.2 1.0 constant_dynamic-slice_fusion.2
  204.4 7.7 %while.22 = (s32[]{:T(128)}, bf16[2,512,128]{2,1,0:T(8,128)(2,1)S(1)}, s32[2]{0:T(128)S(1)}, bf16[1024,192]{1,0:T(8,128)(2,1)S(1)}, bf16[1024,128]{1,0:T(8,128)(...) while((s32[]{:T(128)}, ...), condition=%wide.region_5.5_spmd, body=%wide.region_2.4_spmd.sunk | while | flops 340852224 | bytes 12728555 | solution.py:60
  212.9 1.1 dynamic-slice_bitcast_fusion.2
  214.7 1.0 constant_dynamic-slice_fusion.2
  216.0 7.7 %while.22 = (s32[]{:T(128)}, bf16[2,512,128]{2,1,0:T(8,128)(2,1)S(1)}, s32[2]{0:T(128)S(1)}, bf16[1024,192]{1,0:T(8,128)(2,1)S(1)}, bf16[1024,128]{1,0:T(8,128)(...) while((s32[]{:T(128)}, ...), condition=%wide.region_5.5_spmd, body=%wide.region_2.4_spmd.sunk | while | flops 340852224 | bytes 12728555 | solution.py:60
  224.5 1.1 dynamic-slice_bitcast_fusion.2
  226.3 1.0 constant_dynamic-slice_fusion.2
  227.5 7.7 %while.22 = (s32[]{:T(128)}, bf16[2,512,128]{2,1,0:T(8,128)(2,1)S(1)}, s32[2]{0:T(128)S(1)}, bf16[1024,192]{1,0:T(8,128)(2,1)S(1)}, bf16[1024,128]{1,0:T(8,128)(...) while((s32[]{:T(128)}, ...), condition=%wide.region_5.5_spmd, body=%wide.region_2.4_spmd.sunk | while | flops 340852224 | bytes 12728555 | solution.py:60
  236.0 1.1 dynamic-slice_bitcast_fusion.2
  237.8 1.0 constant_dynamic-slice_fusion.2
  239.1 7.7 %while.22 = (s32[]{:T(128)}, bf16[2,512,128]{2,1,0:T(8,128)(2,1)S(1)}, s32[2]{0:T(128)S(1)}, bf16[1024,192]{1,0:T(8,128)(2,1)S(1)}, bf16[1024,128]{1,0:T(8,128)(...) while((s32[]{:T(128)}, ...), condition=%wide.region_5.5_spmd, body=%wide.region_2.4_spmd.sunk | while | flops 340852224 | bytes 12728555 | solution.py:60
  247.5 2.9 copy.55
  250.5 2.3 all_to_all.35
  252.8 16.4 %all-to-all-start.1 = ((bf16[8,128,1024]{2,1,0:T(8,128)(2,1)}), bf16[8,128,1024]{2,1,0:T(8,128)(2,1)S(1)}, u32[]{:S(2)}, u32[]{:S(2)}) async-start(bf16[8,128,1024]{2,1,0:T(8,128)(2,1)} %all_to_all.35), calls=%async_computation.1 | async-start | bytes 4194304 | tf_op jit(solution)/shard_map/all_to_all | solution.py:125
  269.2 9.4 %fusion.7 = f32[1024,512]{1,0:T(8,128)} fusion(bf16[128,8,3584]{2,1,0:T(8,128)(2,1)} %all-to-all-done.2, bf16[1,3584,512]{2,1,0:T(8,128)(2,1)} %param.22), kind=kOutput, calls=%fused_computation.27 | convolution fusion | flops 3758096384 | bytes 13107200 | tf_op jit(solution)/shard_map/dot_general | solution.py:75
  278.6 14.7 %fusion.11 = bf16[128,8,3584]{2,1,0:T(8,128)(2,1)} fusion(bf16[1,512,3584]{2,1,0:T(8,128)(2,1)} %param.23, f32[1024,512]{1,0:T(8,128)} %fusion.7, bf16[1,3584,512]{2,1,0:T(8,128)(2,1)} %param.21, bf16[128,8,3584]{2,1,0:T(8,128)(2,1)} %all-to-all-done.2), kind=kOutput, calls=%fused_computation.32 | convolution fusion | flops 7523008512 | bytes 24117248 | tf_op jit(solution)/shard_map/dot_general | solution.py:78
  293.3 3.1 all-to-all-done.1
  296.3 8.6 %all-to-all-start.3 = ((bf16[128,8,3584]{2,1,0:T(8,128)(2,1)}), bf16[128,8,3584]{2,1,0:T(8,128)(2,1)}, u32[]{:S(2)}, u32[]{:S(2)}) async-start(bf16[128,8,3584]{2,1,0:T(8,128)(2,1)} %fusion.11), calls=%async_computation.3 | async-start | bytes 14680064 | tf_op jit(solution)/shard_map/all_to_all | solution.py:69
  305.6 2.4 copy.56
  308.0 4.1 copy.68
  312.1 79.4 %all-to-all-done.3 = bf16[128,8,3584]{2,1,0:T(8,128)(2,1)} async-done(((bf16[128,8,3584]{2,1,0:T(8,128)(2,1)}), bf16[128,8,3584]{2,1,0:T(8,128)(2,1)}, u32[]{:S(2)}, u32[]{:S(2)}) %all-to-all-start.3) | async-done | bytes 7340064 | tf_op jit(solution)/shard_map/all_to_all | solution.py:69
  391.4 4.0 fusion.12
  395.5 2.0 concatenate.14
  397.5 4.6 %gather_fusion.1 = bf16[128,3584]{1,0:T(8,128)(2,1)S(1)} fusion(bf16[513,3584]{1,0:T(8,128)(2,1)} %concatenate.14, s32[1024]{0:T(1024)S(1)} %get-tuple-element.144), kind=kCustom, calls=%fused_computation.1 | custom fusion | bytes 1835520 | tf_op jit(solution)/shard_map/gather | solution.py:158
  402.1 4.6 %gather_fusion.2 = bf16[128,3584]{1,0:T(8,128)(2,1)S(1)} fusion(bf16[513,3584]{1,0:T(8,128)(2,1)} %concatenate.14, s32[1024]{0:T(1024)S(1)} %get-tuple-element.143), kind=kCustom, calls=%fused_computation.2 | custom fusion | bytes 1835520 | tf_op jit(solution)/shard_map/gather | solution.py:158
  406.6 4.6 %gather_fusion.3 = bf16[128,3584]{1,0:T(8,128)(2,1)S(1)} fusion(bf16[513,3584]{1,0:T(8,128)(2,1)} %concatenate.14, s32[1024]{0:T(1024)S(1)} %get-tuple-element.142), kind=kCustom, calls=%fused_computation.3 | custom fusion | bytes 1835520 | tf_op jit(solution)/shard_map/gather | solution.py:158
  411.2 5.5 %gather_fusion.4 = bf16[128,3584]{1,0:T(8,128)(2,1)} fusion(bf16[513,3584]{1,0:T(8,128)(2,1)} %concatenate.14, s32[1024]{0:T(1024)S(1)} %get-tuple-element.141), kind=kCustom, calls=%fused_computation.4 | custom fusion | bytes 1835520 | tf_op jit(solution)/shard_map/gather | solution.py:158
  416.7 5.5 %gather_fusion.5 = bf16[128,3584]{1,0:T(8,128)(2,1)} fusion(bf16[513,3584]{1,0:T(8,128)(2,1)} %concatenate.14, s32[1024]{0:T(1024)S(1)} %get-tuple-element.140), kind=kCustom, calls=%fused_computation.5 | custom fusion | bytes 1835520 | tf_op jit(solution)/shard_map/gather | solution.py:158
  422.2 5.7 %gather_fusion.6 = bf16[128,3584]{1,0:T(8,128)(2,1)} fusion(bf16[513,3584]{1,0:T(8,128)(2,1)} %concatenate.14, s32[1024]{0:T(1024)S(1)} %get-tuple-element.139), kind=kCustom, calls=%fused_computation.6 | custom fusion | bytes 1835520 | tf_op jit(solution)/shard_map/gather | solution.py:158
  427.9 5.5 %gather_fusion.7 = bf16[128,3584]{1,0:T(8,128)(2,1)} fusion(bf16[513,3584]{1,0:T(8,128)(2,1)} %concatenate.14, s32[1024]{0:T(1024)S(1)} %get-tuple-element.138), kind=kCustom, calls=%fused_computation.7 | custom fusion | bytes 1835520 | tf_op jit(solution)/shard_map/gather | solution.py:158
  433.4 5.5 %gather_fusion.8 = bf16[128,3584]{1,0:T(8,128)(2,1)} fusion(bf16[513,3584]{1,0:T(8,128)(2,1)} %concatenate.14, s32[1024]{0:T(1024)S(1)} %get-tuple-element.137), kind=kCustom, calls=%fused_computation.8 | custom fusion | bytes 1835520 | tf_op jit(solution)/shard_map/gather | solution.py:158
  438.9 4.9 %add_convert_fusion.1 = bf16[128,3584]{1,0:T(8,128)(2,1)} fusion(bf16[128,3584]{1,0:T(8,128)(2,1)} %gather_fusion.8, bf16[128,3584]{1,0:T(8,128)(2,1)} %gather_fusion.7, bf16[128,3584]{1,0:T(8,128)(2,1)} %gather_fusion.6, bf16[128,3584]{1,0:T(8,128)(2,1)} %gather_fusion.5, bf16[128,3584]{1,0:T(8,128)(2,1)} %gather_fusion.4, ...), kind=kLoop, calls=%fused_computation.42 | loop fusion | flops 11010048 | bytes 8261632 | tf_op jit(solution)/shard_map/convert_element_type | solution.py:161
  (229 shorter events, 67.6 us)
Async XLA Ops:
  7.2 58.9 %all-gather.4.cloned.1.call-start = ((), (), s32[]{:S(2)}) async-start(), calls=%async_computation.4 | async-start | bytes 4874240 | tf_op jit(solution)/shard_map/all_gather | solution.py:102
  7.9 119.2 %all-gather.8.cloned.1.call-start = ((), (), s32[]{:S(2)}) async-start(), calls=%async_computation.6 | async-start | bytes 2228224 | tf_op jit(solution)/shard_map/all_gather | solution.py:114
  13.3 4.7 %copy-start.6 = (s32[128,8]{0,1:T(8,128)S(1)}, s32[128,8]{0,1:T(8,128)}, u32[]{:S(2)}) copy-start(s32[128,8]{0,1:T(8,128)} %param.19) | copy-start | bytes 12292
  13.3 52.8 %copy-start.1 = (bf16[128,3584]{1,0:T(8,128)(2,1)S(1)}, bf16[128,3584]{1,0:T(8,128)(2,1)}, u32[]{:S(2)}) copy-start(bf16[128,3584]{1,0:T(8,128)(2,1)} %param.14) | copy-start | bytes 2752516
  13.3 86.1 %all-to-all-start = ((bf16[128,8,1536]{0,2,1:T(8,128)(2,1)}), bf16[128,8,1536]{0,2,1:T(8,128)(2,1)}, u32[]{:S(2)}, u32[]{:S(2)}) async-start(bf16[128,8,1536]{0,2,1:T(8,128)(2,1)} %bitcast.5), calls=%async_computation | async-start | bytes 6291456 | tf_op jit(solution)/shard_map/all_to_all | solution.py:112
  17.9 130.5 %all-gather.6.cloned.1.call-start = ((), (), s32[]{:S(2)}) async-start(), calls=%async_computation.5 | async-start | bytes 1327104 | tf_op jit(solution)/shard_map/all_gather | solution.py:108
  18.1 52.2 %copy-start.2 = (s32[128,8]{1,0:T(8,128)}, s32[128,8]{1,0:T(8,128)S(1)}, u32[]{:S(2)}) copy-start(s32[128,8]{1,0:T(8,128)S(1)} %copy.57) | copy-start | bytes 12292
  18.4 52.1 %copy-start.8 = (f32[512]{0:T(512)S(1)}, f32[512]{0:T(512)}, u32[]{:S(2)}) copy-start(f32[512]{0:T(512)} %param.16) | copy-start | bytes 6148
  90.2 0.6 copy-start.4
  105.0 147.8 %all-to-all-start.2 = ((bf16[128,8,3584]{2,1,0:T(8,128)(2,1)}), bf16[128,8,3584]{2,1,0:T(8,128)(2,1)}, u32[]{:S(2)}, u32[]{:S(2)}) async-start(bf16[128,8,3584]{2,1,0:T(8,128)(2,1)} %bitcast.122), calls=%async_computation.2 | async-start | bytes 14680064 | tf_op jit(solution)/shard_map/all_to_all | solution.py:65
  152.7 2.3 slice-start
  160.6 1.0 copy-start
  164.4 1.0 copy-start
  172.1 1.0 copy-start
  176.0 1.0 copy-start
  183.7 1.0 copy-start
  187.5 1.0 copy-start
  195.2 1.0 copy-start
  199.1 1.0 copy-start
  206.7 1.0 copy-start
  210.6 1.0 copy-start
  218.3 1.0 copy-start
  222.2 1.0 copy-start
  229.8 1.0 copy-start
  233.7 1.0 copy-start
  241.4 1.0 copy-start
  245.3 1.0 copy-start
  252.8 43.6 %all-to-all-start.1 = ((bf16[8,128,1024]{2,1,0:T(8,128)(2,1)}), bf16[8,128,1024]{2,1,0:T(8,128)(2,1)S(1)}, u32[]{:S(2)}, u32[]{:S(2)}) async-start(bf16[8,128,1024]{2,1,0:T(8,128)(2,1)} %all_to_all.35), calls=%async_computation.1 | async-start | bytes 4194304 | tf_op jit(solution)/shard_map/all_to_all | solution.py:125
  293.2 11.7 %copy-start.5 = (s32[1024]{0:T(1024)S(1)}, s32[1024]{0:T(1024)}, u32[]{:S(2)}) copy-start(s32[1024]{0:T(1024)} %copy-done.4) | copy-start | bytes 12292
  293.2 11.8 %copy-start.3 = (s32[128,8]{1,0:T(8,128)S(1)}, s32[128,8]{1,0:T(8,128)}, u32[]{:S(2)}) copy-start(s32[128,8]{1,0:T(8,128)} %copy-done.2) | copy-start | bytes 12292
  293.2 12.3 %copy-start.7 = (f32[128,8]{0,1:T(8,128)S(1)}, f32[128,8]{0,1:T(8,128)}, u32[]{:S(2)}) copy-start(f32[128,8]{0,1:T(8,128)} %param.20) | copy-start | bytes 12292
  296.3 95.1 %all-to-all-start.3 = ((bf16[128,8,3584]{2,1,0:T(8,128)(2,1)}), bf16[128,8,3584]{2,1,0:T(8,128)(2,1)}, u32[]{:S(2)}, u32[]{:S(2)}) async-start(bf16[128,8,3584]{2,1,0:T(8,128)(2,1)} %fusion.11), calls=%async_computation.3 | async-start | bytes 14680064 | tf_op jit(solution)/shard_map/all_to_all | solution.py:69
Sparse Core Ops, SparseCore 0:
  10.1 55.9 all-gather.3
  68.2 44.9 all-gather.7
  115.5 32.8 all-gather.5
where the time goes:
time: 459 us; the launch traced here: 451 us
  waiting for transfers between devices  153 us (33%)
  local copies, waits for them, and re-layouts  137 us (30%)
  matrix products  59.8 us (13%)
  starting transfers between devices  38.8 us (8%)
  other arithmetic  37.1 us (8%)
  between operations  14.3 us (3%)
  loops' own time  10.2 us (2%)
    all_to_all x1, waiting for transfers between devices, return_rows(): lax.all_to_all(buffer, ('node', 'local'), split_axis=0, concat_axis=0, ti...  79.4 us
    all_gather x1, waiting for transfers between devices, shards(): lax.all_gather(latent_weight, 'node', axis=0, tiled=True)  47.7 us
    gather x8, local copies, waits for them, and re-layouts, shards(): results[route_index[:, column]].astype(jnp.float32)  41.3 us
    all_gather x1, waiting for transfers between devices, shards(): lax.all_gather(jnp.concatenate([compressed, rope_keys], axis=1), 'local',...  21.4 us
    another operation x12, other arithmetic  18.3 us
    all_to_all x1, starting transfers between devices, shards(): lax.all_to_all(merged, 'local', split_axis=0, concat_axis=1, tiled=True)  16.4 us
    dot_general x1, matrix products, expert_half(): jnp.dot(inner, down_proj[0], preferred_element_type=jnp.float32)  14.7 us
    dot_general x16, matrix products, one_block(): jnp.einsum('qd,kd->qk', block_rows[:, NOPE:], keys_rope, preferred_elemen...  10.8 us
  transfers between devices with their start and end apart: 7, of which 4 were waited for; matrix products, arithmetic and copies ran while one was open for 38% of the time, Pallas kernels for 0%

commit v1 on v0

v1 whole, which is shorter than its diff:
```python
import functools
import math

import jax
import jax.numpy as jnp
from jax import lax
from jax.experimental import pallas as pl
from jax.experimental.pallas import tpu as pltpu
from jax.sharding import Mesh
from jax.sharding import PartitionSpec as P

NOPE = 128
ROPE = 64
VDIM = 128
LAT = 512
EXPERTS = 256
TOPK = 8
CAP = 8
HEAD = NOPE + ROPE
KV = NOPE + VDIM
CHIPS = ("z", "y", "x")
ALL = ("z", "y", "x", "c")
BF16 = jnp.bfloat16
F32 = jnp.float32
MIB = 1 << 20


def call(kernel, **options):
    limit = options.pop("vmem", 32)
    flops, moved = options.pop("cost")
    return pl.pallas_call(
        kernel,
        compiler_params=pltpu.CompilerParams(vmem_limit_bytes=limit * MIB),
        cost_estimate=pl.CostEstimate(flops=flops, bytes_accessed=moved, transcendentals=0),
        **options,
    )


def dispatch_kernel(ids_ref, weights_ref, hidden_ref, rows_ref, gate_ref, pick):
    slots, tokens = pick.shape

    @pl.when(pl.program_id(0) == 0)
    def _():
        row = lax.broadcasted_iota(jnp.int32, (slots, tokens), 0)
        number = (row // CAP) * (EXPERTS * CAP // slots)
        named = jnp.zeros((slots, tokens), F32)
        weight = jnp.zeros((slots, tokens), F32)
        for k in range(TOPK):
            here = ids_ref[k : k + 1, :] == number
            named = jnp.where(here, 1.0, named)
            weight = jnp.where(here, weights_ref[k : k + 1, :], weight)
        before = lax.broadcasted_iota(jnp.int32, (tokens, tokens), 0) < lax.broadcasted_iota(
            jnp.int32, (tokens, tokens), 1
        )
        earlier = jnp.dot(
            named.astype(BF16), before.astype(F32).astype(BF16), preferred_element_type=F32
        )
        kept = (named > 0.5) & (earlier.astype(jnp.int32) == row % CAP)
        pick[...] = jnp.where(kept, 1.0, 0.0).astype(BF16)
        gate_ref[...] = jnp.where(kept, weight, 0.0)

    rows_ref[...] = jnp.dot(pick[...], hidden_ref[...], preferred_element_type=F32).astype(BF16)


def dispatch(ids, weights, hidden, slots):
    tokens, width = hidden.shape
    block = 512
    return call(
        dispatch_kernel,
        cost=(2 * slots * tokens * width, 2 * (slots + tokens) * width),
        grid=(width // block,),
        in_specs=[
            pl.BlockSpec((TOPK, tokens), lambda j: (0, 0)),
            pl.BlockSpec((TOPK, tokens), lambda j: (0, 0)),
            pl.BlockSpec((tokens, block), lambda j: (0, j)),
        ],
        out_specs=[
            pl.BlockSpec((slots, block), lambda j: (0, j)),
            pl.BlockSpec((slots, tokens), lambda j: (0, 0)),
        ],
        out_shape=[
            jax.ShapeDtypeStruct((slots, width), BF16),
            jax.ShapeDtypeStruct((slots, tokens), F32),
        ],
        scratch_shapes=[pltpu.VMEM((slots, tokens), BF16)],
    )(ids, weights, hidden)


def combine_kernel(gate_ref, rows_ref, out_ref, terms):
    tokens = out_ref.shape[0]

    @pl.when(pl.program_id(0) == 0)
    def _():
        rest = gate_ref[...]
        for term in range(3):
            part = rest.astype(BF16)
            terms[:, term * tokens : (term + 1) * tokens] = part
            rest = rest - part.astype(F32)

    total = lax.dot_general(
        terms[...], rows_ref[...], (((0,), (0,)), ((), ())), preferred_element_type=F32
    )
    out_ref[...] = (total[:tokens] + total[tokens : 2 * tokens] + total[2 * tokens :]).astype(BF16)


def combine(gate, rows):
    slots, tokens = gate.shape
    width = rows.shape[1]
    block = 512
    return call(
        combine_kernel,
        cost=(6 * slots * tokens * width, 2 * (slots + tokens) * width),
        grid=(width // block,),
        in_specs=[
            pl.BlockSpec((slots, tokens), lambda j: (0, 0)),
            pl.BlockSpec((slots, block), lambda j: (0, j)),
        ],
        out_specs=pl.BlockSpec((tokens, block), lambda j: (0, j)),
        out_shape=jax.ShapeDtypeStruct((tokens, width), BF16),
        scratch_shapes=[pltpu.VMEM((slots, 3 * tokens), BF16)],
    )(gate, rows)


def expert_kernel(
    rows_ref, gate0, up0, down0, gate1, up1, down1, out_ref, inner, *, steps
):
    step = pl.program_id(0)

    def hidden_block(gate_ref, up_ref):
        rows = rows_ref[...]
        gate = jnp.dot(rows, gate_ref[0], preferred_element_type=F32)
        upper = jnp.dot(rows, up_ref[0], preferred_element_type=F32)
        inner[step] = (gate / (1.0 + jnp.exp(-gate)) * upper).astype(BF16)

    pl.when(step < steps)(lambda: hidden_block(gate0, up0))
    pl.when((step >= steps) & (step < 2 * steps))(lambda: hidden_block(gate1, up1))

    @pl.when(step >= 2 * steps)
    def _():
        wide = inner.shape[2]
        total = None
        for half, down in enumerate((down0, down1)):
            partial = None
            for part in range(steps):
                term = jnp.dot(
                    inner[half * steps + part],
                    down[0, part * wide : (part + 1) * wide, :],
                    preferred_element_type=F32,
                )
                partial = term if partial is None else partial + term
            partial = partial.astype(BF16).astype(F32)
            total = partial if total is None else total + partial
        out_ref[...] = total.astype(BF16)


def experts(rows, own, other):
    count, width = rows.shape
    half = own[0].shape[2]
    wide, block = 256, 512
    steps = half // wide
    first = 2 * steps

    def column(start):
        return lambda j: (0, 0, jnp.clip(j - start, 0, steps - 1))

    def late(j):
        return (0, 0, jnp.maximum(j - first, 0))

    specs = []
    for start in (0, steps):
        specs += [
            pl.BlockSpec((1, width, wide), column(start)),
            pl.BlockSpec((1, width, wide), column(start)),
            pl.BlockSpec((1, half, block), late),
        ]
    return call(
        functools.partial(expert_kernel, steps=steps),
        vmem=56,
        cost=(12 * count * width * half, 2 * (2 * count * width + 6 * width * half)),
        grid=(first + width // block,),
        in_specs=[pl.BlockSpec((count, width), lambda j: (0, 0))] + specs,
        out_specs=pl.BlockSpec((count, block), lambda j: (0, jnp.maximum(j - first, 0))),
        out_shape=jax.ShapeDtypeStruct((count, width), BF16),
        scratch_shapes=[pltpu.VMEM((first, count, wide), BF16)],
    )(rows, *own, *other)


def attention_kernel(
    where_ref, latent_ref, kv_ref, mine_ref, other_ref, out_ref, send_ref, bias
):
    tokens = mine_ref.shape[0]
    length = latent_ref.shape[0]
    chips = length // (2 * tokens)

    @pl.when(pl.program_id(0) == 0)
    def _():
        core, chip = where_ref[0], where_ref[1]
        row = lax.broadcasted_iota(jnp.int32, (2 * tokens, length), 0)
        col = lax.broadcasted_iota(jnp.int32, (2 * tokens, length), 1)
        row_core = jnp.where(row < tokens, core, 1 - core)
        row_at = (2 * chip + row_core) * tokens + row % tokens
        block = col // tokens
        col_core = jnp.where(block < chips, core, 1 - core)
        col_chip = (chip + chips - block % chips) % chips
        col_at = (2 * col_chip + col_core) * tokens + col % tokens
        bias[...] = jnp.where(col_at <= row_at, 0.0, -1e30)

    compressed = latent_ref[:, :LAT]
    rope = latent_ref[:, LAT:]
    weight = kv_ref[...].reshape(LAT, 2 * KV)
    keyval = jnp.dot(compressed, weight, preferred_element_type=F32).astype(BF16)
    factor = math.log2(math.e) / math.sqrt(HEAD)
    for head in range(2):
        keys = jnp.concatenate([keyval[:, head * KV : head * KV + NOPE], rope], axis=1)
        values = keyval[:, head * KV + NOPE : (head + 1) * KV]
        span = slice(head * HEAD, (head + 1) * HEAD)
        query = jnp.concatenate([mine_ref[:, span], other_ref[:, span]], axis=0)
        score = lax.dot_general(
            query, keys, (((1,), (1,)), ((), ())), preferred_element_type=F32
        )
        score = score + bias[...]
        top = jnp.max(score, axis=1, keepdims=True)
        weights = jnp.exp2((score - top) * factor)
        inverse = 1.0 / jnp.sum(weights, axis=1, keepdims=True)
        probs = (weights * inverse).astype(BF16)
        result = jnp.dot(probs, values, preferred_element_type=F32).astype(BF16)
        span = slice(head * VDIM, (head + 1) * VDIM)
        out_ref[:, span] = result[:tokens]
        send_ref[:, span] = result[tokens:]


def attend(where, latent, kv_weight, mine, other):
    tokens = mine.shape[0]
    length = latent.shape[0]
    nodes, chips, rows, columns = kv_weight.shape
    pairs = columns // (2 * KV)
    heads = 2 * pairs * chips
    spec = pltpu.PrefetchScalarGridSpec(
        num_scalar_prefetch=1,
        grid=(chips * pairs,),
        in_specs=[
            pl.BlockSpec((length, LAT + ROPE), lambda i, w: (0, 0)),
            pl.BlockSpec((nodes, 1, rows, 2 * KV), lambda i, w: (0, i // pairs, 0, i % pairs)),
            pl.BlockSpec(
                (tokens, 2 * HEAD), lambda i, w: (0, (2 * (i // pairs) + w[0]) * pairs + i % pairs)
            ),
            pl.BlockSpec((tokens, 2 * HEAD), lambda i, w: (0, i)),
        ],
        out_specs=[
            pl.BlockSpec(
                (tokens, 2 * VDIM), lambda i, w: (0, (2 * (i // pairs) + w[0]) * pairs + i % pairs)
            ),
            pl.BlockSpec((tokens, 2 * VDIM), lambda i, w: (0, i)),
        ],
        scratch_shapes=[pltpu.VMEM((2 * tokens, length), F32)],
    )
    flops = 2 * heads * length * (LAT * KV + 2 * tokens * (HEAD + VDIM))
    return call(
        attention_kernel,
        vmem=48,
        cost=(2 * flops, 2 * (LAT * heads * KV + 4 * tokens * heads * HEAD)),
        grid_spec=spec,
        out_shape=[
            jax.ShapeDtypeStruct((tokens, 2 * heads * VDIM), BF16),
            jax.ShapeDtypeStruct((tokens, heads * VDIM), BF16),
        ],
    )(where, latent, kv_weight, mine, other)


def merge_kernel(where_ref, part_ref, whole_ref, out_ref):
    out_ref[...] = part_ref[...]


def merge(where, part, whole, chips):
    tokens, columns = part.shape
    block = columns // chips
    spec = pltpu.PrefetchScalarGridSpec(
        num_scalar_prefetch=1,
        grid=(chips,),
        in_specs=[
            pl.BlockSpec((tokens, block), lambda i, w: (0, i)),
            pl.BlockSpec(memory_space=pl.ANY),
        ],
        out_specs=pl.BlockSpec((tokens, block), lambda i, w: (0, 2 * i + 1 - w[0])),
    )
    return call(
        merge_kernel,
        cost=(0, 4 * tokens * columns),
        grid_spec=spec,
        out_shape=jax.ShapeDtypeStruct(whole.shape, BF16),
        input_output_aliases={2: 0},
    )(where, part, whole)


def normalize(columns, latent_gain):
    mean_square = jnp.mean(columns * columns, axis=1, keepdims=True)
    return (columns * lax.rsqrt(mean_square + 1e-06) * latent_gain[None, :]).astype(BF16)


def rotate_keys(rope_part, position):
    half_width = ROPE // 2
    freqs = 10000.0 ** (-2.0 * jnp.arange(half_width, dtype=F32) / ROPE)
    angles = position.astype(F32)[:, None] * freqs[None, :]
    cosine = jnp.cos(angles)
    sine = jnp.sin(angles)
    first_half = rope_part[:, :half_width]
    second_half = rope_part[:, half_width:]
    return jnp.concatenate(
        [first_half * cosine - second_half * sine, second_half * cosine + first_half * sine], axis=1
    ).astype(BF16)


def swap(array):
    return lax.ppermute(array, "c", [(0, 1), (1, 0)])


def along_x(array, distance):
    size = lax.axis_size("x")
    return lax.ppermute(array, "x", [(i, (i + distance) % size) for i in range(size)])


def exchange(rows):
    return lax.all_to_all(rows, CHIPS, split_axis=0, concat_axis=0, tiled=True)


def shards(
    hidden,
    latent_weight,
    latent_gain,
    queries,
    kv_weight,
    expert_ids,
    route_weights,
    gate_proj,
    up_proj,
    down_proj,
):
    tokens = hidden.shape[0]
    core = lax.axis_index("c")
    chip = lax.axis_index("x")
    chips = lax.axis_size("x")
    nodes = lax.axis_size("z") * lax.axis_size("y")
    where = jnp.stack([core, chip]).astype(jnp.int32)

    slots = nodes * chips * CAP
    rows, gate = dispatch(expert_ids.T, route_weights.T, hidden, slots)
    arrived = exchange(rows)

    own = (gate_proj, up_proj, down_proj)
    other = tuple(swap(array) for array in own)

    portion = lax.all_gather(latent_weight, ("z", "y"), axis=0, tiled=True)
    latent = jnp.dot(hidden, portion, preferred_element_type=F32)
    position = (2 * chip + core) * tokens + jnp.arange(tokens, dtype=jnp.int32)
    mine = jnp.concatenate(
        [normalize(latent[:, :LAT], latent_gain), rotate_keys(latent[:, LAT:], position)], axis=1
    )
    line = jnp.concatenate([mine] + [along_x(mine, d) for d in range(1, chips)], axis=0)
    sequence = jnp.concatenate([line, swap(line)], axis=0)

    kv_rows, kv_columns = kv_weight.shape
    kv_all = lax.all_gather(kv_weight, CHIPS, axis=0, tiled=True)
    kv_all = kv_all.reshape(nodes, chips, kv_rows, kv_columns)

    split = queries.reshape(tokens, chips, 2, -1)
    sent = lax.dynamic_index_in_dim(split, 1 - core, axis=2, keepdims=False)
    other_queries = swap(sent.reshape(tokens, -1))

    results = experts(arrived, own, other)
    sequence, results = lax.optimization_barrier((sequence, results))
    returned = exchange(results)

    whole, send = attend(where, sequence, kv_all, queries, other_queries)
    attention = merge(where, swap(send), whole, chips)
    routed = combine(gate, returned)
    return (attention, routed)


def solution(mesh):
    grid = Mesh(mesh.devices.reshape(4, 4, 4, 2), ALL)
    token = P(ALL, None)
    placed = (
        token,
        P(("z", "y"), None),
        P(),
        token,
        P(("z", "y"), ("x", "c")),
        token,
        token,
        P(ALL, None, None),
        P(ALL, None, None),
        P(ALL, None, None),
    )
    return jax.shard_map(
        shards, mesh=grid, in_specs=placed, out_specs=(token, token), check_vma=False
    )
```

time: 459 us -> 276 us (0.60)
  the two profiles are of different devices: /device:TPU:0 before, /device:TPU:23 now
where the time goes in v1:
time: 276 us; the launch traced here: 275 us
  waiting for transfers between devices  124 us (45%)
  Pallas kernels  69.6 us (25%)
  local copies, waits for them, and re-layouts  33.3 us (12%)
  starting transfers between devices  26.6 us (10%)
  between operations  14.2 us (5%)
  other arithmetic  3.31 us (1%)
  matrix products  3.19 us (1%)
    all_gather x1, waiting for transfers between devices, shards(): portion = lax.all_gather(latent_weight, ('z', 'y'), axis=0, tiled=True)  73.9 us
    all_gather x1, waiting for transfers between devices, shards(): kv_all = lax.all_gather(kv_weight, CHIPS, axis=0, tiled=True)  49.2 us
    pallas_call x1, Pallas kernels, attend(): call(attention_kernel, vmem=48, cost=(2 * flops, 2 * (LAT * heads * KV +...  35.4 us
    pallas_call x1, Pallas kernels, experts(): call(functools.partial(expert_kernel, steps=steps), vmem=56, cost=(12 * c...  22.6 us
    all_to_all x2, starting transfers between devices, exchange(): return lax.all_to_all(rows, CHIPS, split_axis=0, concat_axis=0, tiled=True)  19.7 us
    dynamic_slice x1, local copies, waits for them, and re-layouts, shards(): sent = lax.dynamic_index_in_dim(split, 1 - core, axis=2, keepdims=False)  11.9 us
    reshape x1, local copies, waits for them, and re-layouts, shards(): split = queries.reshape(tokens, chips, 2, -1)  8.04 us
    unnamed x16, local copies, waits for them, and re-layouts  7.82 us
  transfers between devices with their start and end apart: 13, of which 2 were waited for; matrix products, arithmetic and copies ran while one was open for 13% of the time, Pallas kernels for 25%

profile of v1, /device:TPU:23, one launch (start us, length us, event | category | flops | bytes accessed | tf_op | source)
XLA Modules:
  0.0 274.7 jit_solution(2619770739012104171)
XLA Ops:
  7.2 0.0 all-gather.3.cloned.1.call-start
  7.2 0.7 all-gather.3.cloned.1.call-update
  7.9 0.0 all-gather.5.cloned.1.call-start
  7.9 0.7 all-gather.5.cloned.1.call-update
  8.6 0.8 collective-permute-start.4
  9.4 0.1 collective-permute-start.5
  9.5 0.4 collective-permute-start.6
  9.9 0.0 copy-start.1
  9.9 1.2 copy-done.1
  11.1 0.0 copy-start.3
  11.1 0.7 copy-done.3
  11.8 0.0 copy-start.4
  11.8 0.7 copy-done.4
  12.5 2.7 shard_map.113
  15.2 0.0 copy-start
  15.2 1.8 copy-done
  17.0 0.0 copy-start.2
  17.0 10.9 %all-to-all-start = ((bf16[64,8,3584]{2,1,0:T(8,128)(2,1)}), bf16[64,8,3584]{2,1,0:T(8,128)(2,1)}, u32[]{:S(2)}, u32[]{:S(2)}) async-start(bf16[64,8,3584]{2,1,0:T(8,128)(2,1)} %bitcast.13), calls=%async_computation | async-start | bytes 7340032 | tf_op jit(solution)/shard_map/all_to_all | solution.py:323
  28.0 0.0 copy-start.5
  28.0 73.9 %all-gather.3.cloned.1.call-done = bf16[3584,576]{1,0:T(8,128)(2,1)} async-done(((bf16[224,576]{1,0:T(8,128)(2,1)}), bf16[3584,576]{1,0:T(8,128)(2,1)}) %all-gather.3.cloned.1.call-update) | async-done | bytes 4128784 | tf_op jit(solution)/shard_map/all_gather | solution.py:352
  101.9 0.0 copy-done.2
  101.9 3.2 %fusion.8 = f32[128,576]{1,0:T(8,128)S(1)} fusion(bf16[128,3584]{1,0:T(8,128)(2,1)S(1)} %copy-done.2, bf16[3584,576]{1,0:T(8,128)(2,1)} %all-gather.3.cloned.1.call-done), kind=kOutput, calls=%fused_computation.24 | convolution fusion | flops 528482304 | bytes 5341184 | tf_op jit(solution)/shard_map/dot_general | solution.py:353
  105.1 0.1 multiply_reduce_fusion
  105.2 0.3 fusion.5
  105.5 0.0 copy-done.5
  105.5 0.1 multiply_convert_fusion
  105.6 0.8 constant_dynamic-update-slice_fusion.4
  106.4 0.3 collective-permute-start
  106.6 8.0 %reshape.38 = bf16[128,4,2,1536]{3,2,1,0:T(2,128)(2,1)} reshape(bf16[128,12288]{1,0:T(8,128)(2,1)} %mine_ref.1) | data formatting | bytes 6291456 | tf_op jit(solution)/shard_map/reshape | solution.py:365
  114.7 2.1 collective-permute-start.1
  116.8 0.0 collective-permute-done
  116.8 0.0 collective-permute-start.2
  116.8 11.9 %dynamic-slice_reduce_fusion = bf16[128,4,1536]{2,1,0:T(4,128)(2,1)S(1)} fusion(bf16[128,4,2,1536]{3,2,1,0:T(2,128)(2,1)} %reshape.38, s32[]{:T(128)S(6)} %select_n.4), kind=kLoop, calls=%fused_computation | loop fusion | bytes 3145732 | tf_op jit(solution)/shard_map/jit(dynamic_index_in_dim)/dynamic_slice | solution.py:366
  128.7 1.4 copy.32
  130.2 0.0 collective-permute-done.1
  130.2 1.2 collective-permute-start.7
  131.4 0.0 collective-permute-done.2
  131.4 1.9 pad_maximum_fusion
  133.3 2.1 copy.27
  135.5 0.0 collective-permute-start.3
  135.5 0.0 all-to-all-done
  135.5 0.0 collective-permute-done.4.gate1
  135.5 0.0 collective-permute-done.5.up1
  135.5 0.0 collective-permute-done.6.down1
  135.5 22.6 %shard_map.114 = bf16[512,3584]{1,0:T(8,128)(2,1)} custom-call(bf16[512,3584]{1,0:T(8,128)(2,1)} %bitcast.5.rows_ref, bf16[1,3584,512]{2,1,0:T(8,128)(2,1)} %gate0.1, bf16[1,3584,512]{2,1,0:T(8,128)(2,1)} %up0.1, bf16[1,512,3584]{2,1,0:T(8,128)(2,1)} %down0.1, bf16[1,3584,512]{2,1,0:T(8,128)(2,1)} %collective-permute-done.4.gate1, ...), custom_call_target="tpu_custom_call" | custom-call | flops 11274289152 | bytes 29360128 | tf_op jit(solution)/shard_map/pallas_call | solution.py:176
  158.2 1.0 constant_dynamic-update-slice_fusion.2
  159.2 0.9 constant_dynamic-update-slice_fusion.1
  160.1 0.0 collective-permute-done.3
  160.1 2.1 copy.28
  162.3 1.2 constant_dynamic-update-slice_fusion.latent_ref
  163.5 8.7 %all-to-all-start.1 = ((bf16[64,8,3584]{2,1,0:T(8,128)(2,1)}), bf16[64,8,3584]{2,1,0:T(8,128)(2,1)}, u32[]{:S(2)}, u32[]{:S(2)}) async-start(bf16[64,8,3584]{2,1,0:T(8,128)(2,1)} %bitcast.17), calls=%async_computation.1 | async-start | bytes 7340032 | tf_op jit(solution)/shard_map/all_to_all | solution.py:323
  172.2 0.1 pad_add_fusion.where_ref
  172.3 0.0 collective-permute-done.7.other_ref
  172.3 49.2 %all-gather.5.cloned.1.call-done = bf16[2048,2048]{1,0:T(8,128)(2,1)} async-done(((bf16[32,2048]{1,0:T(8,128)(2,1)}), bf16[2048,2048]{1,0:T(8,128)(2,1)}) %all-gather.5.cloned.1.call-update) | async-done | bytes 8388624 | tf_op jit(solution)/shard_map/all_gather | solution.py:362
  221.5 35.4 %shard_map.115 = (bf16[128,8192]{1,0:T(8,128)(2,1)}, bf16[128,4096]{1,0:T(8,128)(2,1)}) custom-call(s32[2]{0:T(128)S(1)} %pad_add_fusion.where_ref, bf16[1024,576]{1,0:T(8,128)(2,1)S(1)} %constant_dynamic-update-slice_fusion.latent_ref, bf16[16,4,32,2048]{3,2,1,0:T(8,128)(2,1)} %bitcast.18, bf16[128,12288]{1,0:T(8,128)(2,1)} %mine_ref.1, ...), custom_call_target="tpu_custom_call" | custom-call | flops 27917287424 | bytes 14680064 | tf_op jit(solution)/shard_map/pallas_call | solution.py:258
  256.9 2.0 collective-permute-start.8
  258.9 0.0 all-to-all-done.1
  258.9 6.7 %shard_map.117 = bf16[128,3584]{1,0:T(8,128)(2,1)} custom-call(f32[512,128]{1,0:T(8,128)S(1)} %get-tuple-element.12.gate_ref, bf16[512,3584]{1,0:T(8,128)(2,1)} %bitcast.8.rows_ref), custom_call_target="tpu_custom_call" | custom-call | flops 1409286144 | bytes 4587520 | tf_op jit(solution)/shard_map/pallas_call | solution.py:110
  265.7 0.0 collective-permute-done.8.part_ref
  265.7 2.2 shard_map.116
  (4 shorter events, 0.0 us)
Async XLA Ops:
  7.2 94.7 %all-gather.3.cloned.1.call-start = ((), (), s32[]{:S(2)}) async-start(), calls=%async_computation.2 | async-start | bytes 4874240 | tf_op jit(solution)/shard_map/all_gather | solution.py:352
  7.9 213.6 %all-gather.5.cloned.1.call-start = ((), (), s32[]{:S(2)}) async-start(), calls=%async_computation.3 | async-start | bytes 8519680 | tf_op jit(solution)/shard_map/all_gather | solution.py:362
  8.6 126.8 %collective-permute-start.4 = (bf16[1,3584,512]{2,1,0:T(8,128)(2,1)}, bf16[1,3584,512]{2,1,0:T(8,128)(2,1)}, u32[]{:S(2)}, u32[]{:S(2)}) collective-permute-start(bf16[1,3584,512]{2,1,0:T(8,128)(2,1)} %gate0.1), channel_id=1, source_target_pairs={{0,1},{1,0},{2,3},{3,2},{4,5},{5,4},{6,7},{7,6},{8,9},{9,8},{10,11... | collective-permute-start | bytes 11010056 | tf_op jit(solution)/shard_map/ppermute | solution.py:314
  9.4 126.1 %collective-permute-start.5 = (bf16[1,3584,512]{2,1,0:T(8,128)(2,1)}, bf16[1,3584,512]{2,1,0:T(8,128)(2,1)}, u32[]{:S(2)}, u32[]{:S(2)}) collective-permute-start(bf16[1,3584,512]{2,1,0:T(8,128)(2,1)} %up0.1), channel_id=1, source_target_pairs={{0,1},{1,0},{2,3},{3,2},{4,5},{5,4},{6,7},{7,6},{8,9},{9,8},{10,11... | collective-permute-start | bytes 11010056 | tf_op jit(solution)/shard_map/ppermute | solution.py:314
  9.5 126.0 %collective-permute-start.6 = (bf16[1,512,3584]{2,1,0:T(8,128)(2,1)}, bf16[1,512,3584]{2,1,0:T(8,128)(2,1)}, u32[]{:S(2)}, u32[]{:S(2)}) collective-permute-start(bf16[1,512,3584]{2,1,0:T(8,128)(2,1)} %down0.1), channel_id=1, source_target_pairs={{0,1},{1,0},{2,3},{3,2},{4,5},{5,4},{6,7},{7,6},{8,9},{9,8},{10,11... | collective-permute-start | bytes 11010056 | tf_op jit(solution)/shard_map/ppermute | solution.py:314
  9.9 1.2 copy-start.1
  11.1 0.7 copy-start.3
  11.8 0.7 copy-start.4
  15.2 1.9 copy-start
  17.0 84.8 %copy-start.2 = (bf16[128,3584]{1,0:T(8,128)(2,1)S(1)}, bf16[128,3584]{1,0:T(8,128)(2,1)}, u32[]{:S(2)}) copy-start(bf16[128,3584]{1,0:T(8,128)(2,1)} %hidden_ref.1) | copy-start | bytes 2752516
  17.0 118.5 %all-to-all-start = ((bf16[64,8,3584]{2,1,0:T(8,128)(2,1)}), bf16[64,8,3584]{2,1,0:T(8,128)(2,1)}, u32[]{:S(2)}, u32[]{:S(2)}) async-start(bf16[64,8,3584]{2,1,0:T(8,128)(2,1)} %bitcast.13), calls=%async_computation | async-start | bytes 7340032 | tf_op jit(solution)/shard_map/all_to_all | solution.py:323
  28.0 77.5 %copy-start.5 = (f32[512]{0:T(512)S(1)}, f32[512]{0:T(512)}, u32[]{:S(2)}) copy-start(f32[512]{0:T(512)} %param.12) | copy-start | bytes 6148
  106.4 10.4 %collective-permute-start = (bf16[128,576]{1,0:T(8,128)(2,1)}, bf16[128,576]{1,0:T(8,128)(2,1)S(1)}, u32[]{:S(2)}, u32[]{:S(2)}) collective-permute-start(bf16[128,576]{1,0:T(8,128)(2,1)} %get-tuple-element.15), channel_id=1, source_target_pairs={{0,2},{2,4},{4,6},{6,0},{1,3},{3,5},{5,7},{7,1},{8,10},{10,12},{12... | collective-permute-start | bytes 442376 | tf_op jit(solution)/shard_map/ppermute | solution.py:319
  114.7 15.5 %collective-permute-start.1 = (bf16[128,576]{1,0:T(8,128)(2,1)}, bf16[128,576]{1,0:T(8,128)(2,1)}, u32[]{:S(2)}, u32[]{:S(2)}) collective-permute-start(bf16[128,576]{1,0:T(8,128)(2,1)} %get-tuple-element.15), channel_id=1, source_target_pairs={{0,4},{2,6},{4,0},{6,2},{1,5},{3,7},{5,1},{7,3},{8,12},{10,14},{12... | collective-permute-start | bytes 442376 | tf_op jit(solution)/shard_map/ppermute | solution.py:319
  116.8 14.6 %collective-permute-start.2 = (bf16[128,576]{1,0:T(8,128)(2,1)}, bf16[128,576]{1,0:T(8,128)(2,1)}, u32[]{:S(2)}, u32[]{:S(2)}) collective-permute-start(bf16[128,576]{1,0:T(8,128)(2,1)} %get-tuple-element.15), channel_id=1, source_target_pairs={{0,6},{2,0},{4,2},{6,4},{1,7},{3,1},{5,3},{7,5},{8,14},{10,8},{12,... | collective-permute-start | bytes 442376 | tf_op jit(solution)/shard_map/ppermute | solution.py:319
  130.2 42.1 %collective-permute-start.7 = (bf16[128,6144]{1,0:T(8,128)(2,1)}, bf16[128,6144]{1,0:T(8,128)(2,1)S(1)}, u32[]{:S(2)}, u32[]{:S(2)}) collective-permute-start(bf16[128,6144]{1,0:T(8,128)(2,1)} %bitcast.10), channel_id=1, source_target_pairs={{0,1},{1,0},{2,3},{3,2},{4,5},{5,4},{6,7},{7,6},{8,9},{9,8},{10,11... | collective-permute-start | bytes 4718600 | tf_op jit(solution)/shard_map/ppermute | solution.py:314
  135.5 24.7 %collective-permute-start.3 = (bf16[512,576]{0,1:T(8,128)(2,1)}, bf16[512,576]{0,1:T(8,128)(2,1)}, u32[]{:S(2)}, u32[]{:S(2)}) collective-permute-start(bf16[512,576]{0,1:T(8,128)(2,1)} %copy.27), channel_id=1, source_target_pairs={{0,1},{1,0},{2,3},{3,2},{4,5},{5,4},{6,7},{7,6},{8,9},{9,8},{10,11... | collective-permute-start | bytes 1769480 | tf_op jit(solution)/shard_map/ppermute | solution.py:314
  163.5 95.4 %all-to-all-start.1 = ((bf16[64,8,3584]{2,1,0:T(8,128)(2,1)}), bf16[64,8,3584]{2,1,0:T(8,128)(2,1)}, u32[]{:S(2)}, u32[]{:S(2)}) async-start(bf16[64,8,3584]{2,1,0:T(8,128)(2,1)} %bitcast.17), calls=%async_computation.1 | async-start | bytes 7340032 | tf_op jit(solution)/shard_map/all_to_all | solution.py:323
  256.9 8.8 %collective-permute-start.8 = (bf16[128,4096]{1,0:T(8,128)(2,1)}, bf16[128,4096]{1,0:T(8,128)(2,1)S(1)}, u32[]{:S(2)}, u32[]{:S(2)}) collective-permute-start(bf16[128,4096]{1,0:T(8,128)(2,1)} %get-tuple-element.10), channel_id=1, source_target_pairs={{0,1},{1,0},{2,3},{3,2},{4,5},{5,4},{6,7},{7,6},{8,9},{9,8},{10,11... | collective-permute-start | bytes 3145736 | tf_op jit(solution)/shard_map/ppermute | solution.py:314
Sparse Core Ops, SparseCore 0:
  10.1 91.6 all-gather.2
  104.7 116.7 all-gather.4

commit v2 on v1

--- a/solution.py
+++ b/solution.py
@@ -106,7 +106,7 @@
 def combine(gate, rows):
     slots, tokens = gate.shape
     width = rows.shape[1]
-    block = 512
+    block = 1792
     return call(
         combine_kernel,
         cost=(6 * slots * tokens * width, 2 * (slots + tokens) * width),
@@ -156,7 +156,7 @@
 def experts(rows, own, other):
     count, width = rows.shape
     half = own[0].shape[2]
-    wide, block = 256, 512
+    wide, block = 256, 1792
     steps = half // wide
     first = 2 * steps
 
@@ -258,7 +258,7 @@
     return call(
         attention_kernel,
         vmem=48,
-        cost=(2 * flops, 2 * (LAT * heads * KV + 4 * tokens * heads * HEAD)),
+        cost=(flops // 4, 2 * (LAT * heads * KV + 4 * tokens * heads * HEAD)),
         grid_spec=spec,
         out_shape=[
             jax.ShapeDtypeStruct((tokens, 2 * heads * VDIM), BF16),
@@ -292,22 +292,82 @@
     )(where, part, whole)
 
 
-def normalize(columns, latent_gain):
+def latent_kernel(
+    where_ref, hidden_ref, mine_ref, other_ref, gain_ref, cosine_ref, sine_ref, out_ref
+):
+    core, _, row, col = (where_ref[i] for i in range(4))
+    side, blocks, depth = 4, mine_ref.shape[0], mine_ref.shape[1]
+    latent = None
+    for node in range(blocks):
+        by_row = (row + side - node // side) % side
+        by_col = (col + side - node % side) % side
+        along = by_col * side + by_row
+        across = by_row * side + by_col
+        start = 2 * depth * node
+        lower = hidden_ref[:, start : start + depth]
+        upper = hidden_ref[:, start + depth : start + 2 * depth]
+        first = core == 0
+        for held, block, picked in (
+            (mine_ref, jnp.where(first, along, across), jnp.where(first, lower, upper)),
+            (other_ref, jnp.where(first, across, along), jnp.where(first, upper, lower)),
+        ):
+            term = jnp.dot(picked, held[block], preferred_element_type=F32)
+            latent = term if latent is None else latent + term
+    columns = latent[:, :LAT]
     mean_square = jnp.mean(columns * columns, axis=1, keepdims=True)
-    return (columns * lax.rsqrt(mean_square + 1e-06) * latent_gain[None, :]).astype(BF16)
-
-
-def rotate_keys(rope_part, position):
-    half_width = ROPE // 2
-    freqs = 10000.0 ** (-2.0 * jnp.arange(half_width, dtype=F32) / ROPE)
+    out_ref[:, :LAT] = (columns * lax.rsqrt(mean_square + 1e-06) * gain_ref[...]).astype(BF16)
+    keys = latent[:, LAT:]
+    half = ROPE // 2
+    turned = jnp.concatenate([keys[:, half:], keys[:, :half]], axis=1)
+    out_ref[:, LAT:] = (keys * cosine_ref[...] + turned * sine_ref[...]).astype(BF16)
+
+
+def latents(where, hidden, mine, other, gain, cosine, sine):
+    tokens, width = hidden.shape
+    spec = pltpu.PrefetchScalarGridSpec(
+        num_scalar_prefetch=1,
+        grid=(1,),
+        in_specs=[
+            pl.BlockSpec(array.shape, functools.partial(lambda n, i, w: (0,) * n, array.ndim))
+            for array in (hidden, mine, other, gain, cosine, sine)
+        ],
+        out_specs=pl.BlockSpec((tokens, LAT + ROPE), lambda i, w: (0, 0)),
+    )
+    return call(
+        latent_kernel,
+        cost=(2 * tokens * width * (LAT + ROPE), 2 * width * (LAT + ROPE)),
+        grid_spec=spec,
+        out_shape=jax.ShapeDtypeStruct((tokens, LAT + ROPE), BF16),
+    )(where, hidden, mine, other, gain, cosine, sine)
+
+
+def rotation(position):
+    freqs = 10000.0 ** (-2.0 * jnp.arange(ROPE // 2, dtype=F32) / ROPE)
     angles = position.astype(F32)[:, None] * freqs[None, :]
     cosine = jnp.cos(angles)
     sine = jnp.sin(angles)
-    first_half = rope_part[:, :half_width]
-    second_half = rope_part[:, half_width:]
-    return jnp.concatenate(
-        [first_half * cosine - second_half * sine, second_half * cosine + first_half * sine], axis=1
-    ).astype(BF16)
+    return jnp.concatenate([cosine, cosine], axis=1), jnp.concatenate([-sine, sine], axis=1)
+
+
+def pick_kernel(where_ref, whole_ref, part_ref):
+    part_ref[...] = whole_ref[...]
+
+
+def other_groups(where, queries, groups):
+    tokens, columns = queries.shape
+    block = columns // groups
+    spec = pltpu.PrefetchScalarGridSpec(
+        num_scalar_prefetch=1,
+        grid=(groups // 2,),
+        in_specs=[pl.BlockSpec((tokens, block), lambda i, w: (0, 2 * i + 1 - w[0]))],
+        out_specs=pl.BlockSpec((tokens, block), lambda i, w: (0, i)),
+    )
+    return call(
+        pick_kernel,
+        cost=(0, 2 * tokens * columns),
+        grid_spec=spec,
+        out_shape=jax.ShapeDtypeStruct((tokens, columns // 2), BF16),
+    )(where, queries)
 
 
 def swap(array):
@@ -317,6 +377,29 @@
 def along_x(array, distance):
     size = lax.axis_size("x")
     return lax.ppermute(array, "x", [(i, (i + distance) % size) for i in range(size)])
+
+
+def turn(array, distance, swapped):
+    side = lax.axis_size("z")
+    pairs = []
+    for row in range(side):
+        for col in range(side):
+            for core in range(2):
+                if (core == 0) != swapped:
+                    to = ((row + distance) % side, col)
+                else:
+                    to = (row, (col + distance) % side)
+                pairs.append(((row * side + col) * 2 + core, (to[0] * side + to[1]) * 2 + core))
+    return lax.ppermute(array, ("z", "y", "c"), pairs)
+
+
+def ring(block, swapped):
+    return [block] + [turn(block, d, swapped) for d in (1, 3, 2)]
+
+
+def spread(pieces):
+    near, right, left, far = pieces
+    return jnp.concatenate([near, right, far, left], axis=0)
 
 
 def exchange(rows):
@@ -340,35 +423,39 @@
     chip = lax.axis_index("x")
     chips = lax.axis_size("x")
     nodes = lax.axis_size("z") * lax.axis_size("y")
-    where = jnp.stack([core, chip]).astype(jnp.int32)
-
-    slots = nodes * chips * CAP
-    rows, gate = dispatch(expert_ids.T, route_weights.T, hidden, slots)
-    arrived = exchange(rows)
-
-    own = (gate_proj, up_proj, down_proj)
-    other = tuple(swap(array) for array in own)
-
-    portion = lax.all_gather(latent_weight, ("z", "y"), axis=0, tiled=True)
-    latent = jnp.dot(hidden, portion, preferred_element_type=F32)
-    position = (2 * chip + core) * tokens + jnp.arange(tokens, dtype=jnp.int32)
-    mine = jnp.concatenate(
-        [normalize(latent[:, :LAT], latent_gain), rotate_keys(latent[:, LAT:], position)], axis=1
-    )
-    line = jnp.concatenate([mine] + [along_x(mine, d) for d in range(1, chips)], axis=0)
-    sequence = jnp.concatenate([line, swap(line)], axis=0)
+    where = jnp.stack([core, chip, lax.axis_index("z"), lax.axis_index("y")]).astype(jnp.int32)
 
     kv_rows, kv_columns = kv_weight.shape
     kv_all = lax.all_gather(kv_weight, CHIPS, axis=0, tiled=True)
     kv_all = kv_all.reshape(nodes, chips, kv_rows, kv_columns)
 
-    split = queries.reshape(tokens, chips, 2, -1)
-    sent = lax.dynamic_index_in_dim(split, 1 - core, axis=2, keepdims=False)
-    other_queries = swap(sent.reshape(tokens, -1))
+    slots = nodes * chips * CAP
+    rows, gate = dispatch(expert_ids.T, route_weights.T, hidden, slots)
+
+    depth = latent_weight.shape[0] // 2
+    part = lax.dynamic_slice_in_dim(latent_weight, core * depth, depth, axis=0)
+    pieces = ring(spread(ring(part[None], False)), True)
+    own = (gate_proj, up_proj, down_proj)
+    pieces, rows, own, queries = lax.optimization_barrier((pieces, rows, own, queries))
+    arrived = exchange(rows)
+    mine_weight = spread(pieces)
+    other = tuple(swap(array) for array in own)
+
+    position = (2 * chip + core) * tokens + jnp.arange(tokens, dtype=jnp.int32)
+    cosine, sine = rotation(position)
+    mine = latents(
+        where, hidden, mine_weight, swap(mine_weight), latent_gain[None], cosine, sine
+    )
+    pieces = [mine] + [along_x(mine, d) for d in range(1, chips)]
 
     results = experts(arrived, own, other)
-    sequence, results = lax.optimization_barrier((sequence, results))
+    pieces, results = lax.optimization_barrier((pieces, results))
     returned = exchange(results)
+
+    line = jnp.concatenate(pieces, axis=0)
+    sequence = jnp.concatenate([line, swap(line)], axis=0)
+
+    other_queries = swap(other_groups(where, queries, 2 * chips))
 
     whole, send = attend(where, sequence, kv_all, queries, other_queries)
     attention = merge(where, swap(send), whole, chips)

time: 276 us -> 217 us (0.79)
  the two profiles are of different devices: /device:TPU:23 before, /device:TPU:95 now
where the time goes in v2:
time: 217 us
  Pallas kernels  72.4 us (33%)
  waiting for transfers between devices  66.2 us (31%)
  starting transfers between devices  49.1 us (23%)
  between operations  14.3 us (7%)
  local copies, waits for them, and re-layouts  13.2 us (6%)
    pallas_call x1, Pallas kernels, attend(): call(attention_kernel, vmem=48, cost=(flops // 4, 2 * (LAT * heads * KV +...  35.2 us
    all_to_all x2, waiting for transfers between devices, exchange(): return lax.all_to_all(rows, CHIPS, split_axis=0, concat_axis=0, tiled=True)  30.8 us
    all_to_all x2, starting transfers between devices, exchange(): return lax.all_to_all(rows, CHIPS, split_axis=0, concat_axis=0, tiled=True)  21.1 us
    pallas_call x1, Pallas kernels, experts(): call(functools.partial(expert_kernel, steps=steps), vmem=56, cost=(12 * c...  20.8 us
    ppermute x7, starting transfers between devices, swap(): return lax.ppermute(array, 'c', [(0, 1), (1, 0)])  19.2 us
    all_gather x1, waiting for transfers between devices, shards(): kv_all = lax.all_gather(kv_weight, CHIPS, axis=0, tiled=True)  17.2 us
    ppermute x6, waiting for transfers between devices, turn(): return lax.ppermute(array, ('z', 'y', 'c'), pairs)  10 us
    unnamed x55, local copies, waits for them, and re-layouts  8.72 us
  transfers between devices with their start and end apart: 19, of which 7 were waited for; matrix products, arithmetic and copies ran while one was open for 4% of the time, Pallas kernels for 32%

profile of v2, /device:TPU:95, one launch (start us, length us, event | category | flops | bytes accessed | tf_op | source)
XLA Modules:
  0.0 216.8 jit_solution(3504584106041592077)
XLA Ops:
  7.2 0.0 copy-start
  7.2 0.0 all-gather.2.cloned.1.call-start
  7.2 0.7 all-gather.2.cloned.1.call-update
  7.9 0.2 copy-done
  8.1 0.5 collective-permute-start.2
  8.7 0.7 collective-permute-start.1
  9.3 1.9 collective-permute-start
  11.2 3.8 %collective-permute-done.2 = bf16[1,112,576]{2,1,0:T(8,128)(2,1)S(1)} collective-permute-done((bf16[1,112,576]{2,1,0:T(8,128)(2,1)S(1)}, bf16[1,112,576]{2,1,0:T(8,128)(2,1)S(1)}, u32[]{:S(2)}, u32[]{:S(2)}) %collective-permute-start.2) | collective-permute-done | bytes 129056 | tf_op jit(solution)/shard_map/ppermute | solution.py:393
  15.1 0.7 collective-permute-done
  15.8 0.1 pad_maximum_fusion.1
  15.9 1.4 collective-permute-start.3
  17.3 0.1 collective-permute-start.4
  17.4 1.7 collective-permute-start.5
  19.2 1.2 copy-done.6
  20.4 0.7 copy-done.9
  21.1 0.7 copy-done.10
  21.7 2.7 %shard_map.113 = (bf16[512,3584]{1,0:T(8,128)(2,1)S(1)}, f32[512,128]{1,0:T(8,128)S(1)}) custom-call(s32[8,128]{1,0:T(8,128)S(1)} %bitcast.16, f32[8,128]{1,0:T(8,128)S(1)} %bitcast.17, bf16[128,3584]{1,0:T(8,128)(2,1)S(1)} %copy-done.6), custom_call_target="tpu_custom_call" | custom-call | flops 469762048 | bytes 4587520 | tf_op jit(solution)/shard_map/pallas_call | solution.py:68
  24.4 1.8 copy-done.3
  26.2 5.5 %collective-permute-done.3 = bf16[4,112,576]{2,1,0:T(8,128)(2,1)S(1)} collective-permute-done((bf16[4,112,576]{2,1,0:T(8,128)(2,1)S(1)}, bf16[4,112,576]{2,1,0:T(8,128)(2,1)S(1)}, u32[]{:S(2)}, u32[]{:S(2)}) %collective-permute-start.3) | collective-permute-done | bytes 516128 | tf_op jit(solution)/shard_map/ppermute | solution.py:393
  31.7 0.0 collective-permute-done.4
  31.7 0.0 collective-permute-done.5
  31.7 0.8 copy-done.19
  32.6 0.1 copy-done.21
  32.7 3.8 %collective-permute-start.10 = (bf16[1,3584,512]{2,1,0:T(8,128)(2,1)}, bf16[1,3584,512]{2,1,0:T(8,128)(2,1)}, u32[]{:S(2)}, u32[]{:S(2)}) collective-permute-start(bf16[1,3584,512]{2,1,0:T(8,128)(2,1)} %gate0), channel_id=1, source_target_pairs={{0,1},{1,0},{2,3},{3,2},{4,5},{5,4},{6,7},{7,6},{8,9},{9,8},{10,11... | collective-permute-start | bytes 11010056 | tf_op jit(solution)/shard_map/ppermute | solution.py:374
  36.5 0.7 collective-permute-start.11
  37.2 9.7 %all-to-all-start = ((bf16[64,8,3584]{2,1,0:T(8,128)(2,1)}), bf16[64,8,3584]{2,1,0:T(8,128)(2,1)}, u32[]{:S(2)}, u32[]{:S(2)}) async-start(bf16[64,8,3584]{2,1,0:T(8,128)(2,1)} %bitcast.14), calls=%async_computation | async-start | bytes 7340032 | tf_op jit(solution)/shard_map/all_to_all | solution.py:406
  46.9 0.0 copy-start.23
  46.9 0.1 constant_dynamic-update-slice_fusion.3
  47.0 0.0 copy-start.7
  47.0 0.0 copy-start.8
  47.0 1.3 constant_dynamic-update-slice_fusion.2
  48.3 0.1 constant_dynamic-update-slice_fusion.1
  48.4 0.1 constant_dynamic-update-slice_fusion.mine_ref
  48.5 1.2 collective-permute-start.6
  49.7 0.1 pad_add_fusion.where_ref
  49.7 0.3 fusion
  50.1 0.1 pad_maximum_fusion.2
  50.2 6.3 %collective-permute-done.6.other_ref = bf16[16,112,576]{2,1,0:T(8,128)(2,1)} collective-permute-done((bf16[16,112,576]{2,1,0:T(8,128)(2,1)S(1)}, bf16[16,112,576]{2,1,0:T(8,128)(2,1)}, u32[]{:S(2)}, u32[]{:S(2)}) %collective-permute-start.6) | collective-permute-done | bytes 2064416 | tf_op jit(solution)/shard_map/ppermute | solution.py:374
  56.5 5.0 %shard_map.114 = bf16[128,576]{1,0:T(8,128)(2,1)S(1)} custom-call(s32[4]{0:T(128)S(1)} %pad_add_fusion.where_ref, bf16[128,3584]{1,0:T(8,128)(2,1)S(1)} %copy-done.7, bf16[16,112,576]{2,1,0:T(8,128)(2,1)S(1)} %constant_dynamic-update-slice_fusion.mine_ref, bf16[16,112,576]{2,1,0:T(8,128)(2,1)} %collective-permute-done.6.other_ref, f32[1,512]{1,0:T(1,128)S(1)} %bitcast.15, ...), custom_call_target="tpu_custom_call" | custom-call | flops 528482304 | bytes 4128768 | tf_op jit(solution)/shard_map/pallas_call | solution.py:336
  61.5 0.0 copy-start.4
  61.5 0.1 collective-permute-start.7
  61.6 2.3 %collective-permute-start.8 = (bf16[128,576]{1,0:T(8,128)(2,1)S(1)}, bf16[128,576]{1,0:T(8,128)(2,1)S(1)}, u32[]{:S(2)}, u32[]{:S(2)}) collective-permute-start(bf16[128,576]{1,0:T(8,128)(2,1)S(1)} %shard_map.114), channel_id=1, source_target_pairs={{0,4},{2,6},{4,0},{6,2},{1,5},{3,7},{5,1},{7,3},{8,12},{10,14},{12... | collective-permute-start | bytes 442376 | tf_op jit(solution)/shard_map/ppermute | solution.py:379
  63.9 0.0 collective-permute-start.9
  63.9 30.7 %all-to-all-done = bf16[64,8,3584]{2,1,0:T(8,128)(2,1)} async-done(((bf16[64,8,3584]{2,1,0:T(8,128)(2,1)}), bf16[64,8,3584]{2,1,0:T(8,128)(2,1)}, u32[]{:S(2)}, u32[]{:S(2)}) %all-to-all-start) | async-done | bytes 3670048 | tf_op jit(solution)/shard_map/all_to_all | solution.py:406
  94.6 20.8 %shard_map.115 = bf16[512,3584]{1,0:T(8,128)(2,1)} custom-call(bf16[512,3584]{1,0:T(8,128)(2,1)} %bitcast.9.rows_ref, bf16[1,3584,512]{2,1,0:T(8,128)(2,1)} %gate0, bf16[1,3584,512]{2,1,0:T(8,128)(2,1)} %up0, bf16[1,512,3584]{2,1,0:T(8,128)(2,1)} %down0, bf16[1,3584,512]{2,1,0:T(8,128)(2,1)} %collective-permute-done.10.gate1, ...), custom_call_target="tpu_custom_call" | custom-call | flops 11274289152 | bytes 29360128 | tf_op jit(solution)/shard_map/pallas_call | solution.py:176
  115.4 0.0 collective-permute-done.7
  115.5 0.6 copy-done.13
  116.1 0.1 copy-done.16
  116.2 11.4 %all-to-all-start.1 = ((bf16[64,8,3584]{2,1,0:T(8,128)(2,1)}), bf16[64,8,3584]{2,1,0:T(8,128)(2,1)}, u32[]{:S(2)}, u32[]{:S(2)}) async-start(bf16[64,8,3584]{2,1,0:T(8,128)(2,1)} %bitcast.19), calls=%async_computation.1 | async-start | bytes 7340032 | tf_op jit(solution)/shard_map/all_to_all | solution.py:406
  127.6 0.0 copy-start.5
  127.6 2.3 %shard_map.116 = bf16[128,6144]{1,0:T(8,128)(2,1)} custom-call(s32[4]{0:T(128)S(1)} %pad_add_fusion.where_ref, bf16[128,12288]{1,0:T(8,128)(2,1)S(1)} %copy-done.2), custom_call_target="tpu_custom_call" | custom-call | bytes 3145728 | tf_op jit(solution)/shard_map/pallas_call | solution.py:365
  129.9 1.9 collective-permute-start.14
  131.9 1.0 pad_maximum_fusion
  132.8 1.1 copy.16
  133.9 0.1 collective-permute-start.13
  134.1 0.9 constant_dynamic-update-slice_fusion.5
  135.0 1.2 collective-permute-done.13
  136.3 2.1 copy.17
  138.4 1.2 constant_dynamic-update-slice_fusion.4.latent_ref
  139.6 17.2 %all-gather.2.cloned.1.call-done = bf16[2048,2048]{1,0:T(8,128)(2,1)} async-done(((bf16[32,2048]{1,0:T(8,128)(2,1)}), bf16[2048,2048]{1,0:T(8,128)(2,1)}) %all-gather.2.cloned.1.call-update) | async-done | bytes 8388624 | tf_op jit(solution)/shard_map/all_gather | solution.py:429
  156.8 35.2 %shard_map.117 = (bf16[128,8192]{1,0:T(8,128)(2,1)}, bf16[128,4096]{1,0:T(8,128)(2,1)}) custom-call(s32[4]{0:T(128)S(1)} %pad_add_fusion.where_ref, bf16[1024,576]{1,0:T(8,128)(2,1)S(1)} %constant_dynamic-update-slice_fusion.4.latent_ref, bf16[16,4,32,2048]{3,2,1,0:T(8,128)(2,1)} %bitcast.18, bf16[128,12288]{1,0:T(8,128)(2,1)} %mine_ref, ...), custom_call_target="tpu_custom_call" | custom-call | flops 3489660928 | bytes 14680064 | tf_op jit(solution)/shard_map/pallas_call | solution.py:258
  192.0 11.5 %collective-permute-start.15 = (bf16[128,4096]{1,0:T(8,128)(2,1)}, bf16[128,4096]{1,0:T(8,128)(2,1)S(1)}, u32[]{:S(2)}, u32[]{:S(2)}) collective-permute-start(bf16[128,4096]{1,0:T(8,128)(2,1)} %get-tuple-element.34), channel_id=1, source_target_pairs={{0,1},{1,0},{2,3},{3,2},{4,5},{5,4},{6,7},{7,6},{8,9},{9,8},{10,11... | collective-permute-start | bytes 3145736 | tf_op jit(solution)/shard_map/ppermute | solution.py:374
  203.5 4.2 %shard_map.119 = bf16[128,3584]{1,0:T(8,128)(2,1)} custom-call(f32[512,128]{1,0:T(8,128)S(1)} %copy-done.12, bf16[512,3584]{1,0:T(8,128)(2,1)} %bitcast.12.rows_ref), custom_call_target="tpu_custom_call" | custom-call | flops 1409286144 | bytes 4587520 | tf_op jit(solution)/shard_map/pallas_call | solution.py:110
  207.8 2.2 shard_map.118
  (49 shorter events, 0.2 us)
Async XLA Ops:
  7.2 1.0 copy-start
  7.2 149.6 %all-gather.2.cloned.1.call-start = ((), (), s32[]{:S(2)}) async-start(), calls=%async_computation.2 | async-start | bytes 8519680 | tf_op jit(solution)/shard_map/all_gather | solution.py:429
  8.1 6.9 %collective-permute-start.2 = (bf16[1,112,576]{2,1,0:T(8,128)(2,1)S(1)}, bf16[1,112,576]{2,1,0:T(8,128)(2,1)S(1)}, u32[]{:S(2)}, u32[]{:S(2)}) collective-permute-start(bf16[1,112,576]{2,1,0:T(8,128)(2,1)S(1)} %dynamic-slice_bitcast_fusion), channel_id=1, source_target_pairs={{0,96},{1,25},{8,104},{9,1},{16,112},{17,9},{24,120},{25,17},{32,0... | collective-permute-start | bytes 387080 | tf_op jit(solution)/shard_map/ppermute | solution.py:393
  8.7 6.4 %collective-permute-start.1 = (bf16[1,112,576]{2,1,0:T(8,128)(2,1)S(1)}, bf16[1,112,576]{2,1,0:T(8,128)(2,1)S(1)}, u32[]{:S(2)}, u32[]{:S(2)}) collective-permute-start(bf16[1,112,576]{2,1,0:T(8,128)(2,1)S(1)} %dynamic-slice_bitcast_fusion), channel_id=1, source_target_pairs={{0,64},{1,17},{8,72},{9,25},{16,80},{17,1},{24,88},{25,9},{32,96},... | collective-permute-start | bytes 387080 | tf_op jit(solution)/shard_map/ppermute | solution.py:393
  9.3 6.4 %collective-permute-start = (bf16[1,112,576]{2,1,0:T(8,128)(2,1)S(1)}, bf16[1,112,576]{2,1,0:T(8,128)(2,1)S(1)}, u32[]{:S(2)}, u32[]{:S(2)}) collective-permute-start(bf16[1,112,576]{2,1,0:T(8,128)(2,1)S(1)} %dynamic-slice_bitcast_fusion), channel_id=1, source_target_pairs={{0,32},{1,9},{8,40},{9,17},{16,48},{17,25},{24,56},{25,1},{32,64},... | collective-permute-start | bytes 387080 | tf_op jit(solution)/shard_map/ppermute | solution.py:393
  15.9 15.8 %collective-permute-start.3 = (bf16[4,112,576]{2,1,0:T(8,128)(2,1)S(1)}, bf16[4,112,576]{2,1,0:T(8,128)(2,1)S(1)}, u32[]{:S(2)}, u32[]{:S(2)}) collective-permute-start(bf16[4,112,576]{2,1,0:T(8,128)(2,1)S(1)} %pad_maximum_fusion.1), channel_id=1, source_target_pairs={{0,8},{1,33},{8,16},{9,41},{16,24},{17,49},{24,0},{25,57},{32,40},... | collective-permute-start | bytes 1548296 | tf_op jit(solution)/shard_map/ppermute | solution.py:393
  17.3 14.4 %collective-permute-start.4 = (bf16[4,112,576]{2,1,0:T(8,128)(2,1)S(1)}, bf16[4,112,576]{2,1,0:T(8,128)(2,1)S(1)}, u32[]{:S(2)}, u32[]{:S(2)}) collective-permute-start(bf16[4,112,576]{2,1,0:T(8,128)(2,1)S(1)} %pad_maximum_fusion.1), channel_id=1, source_target_pairs={{0,24},{1,97},{8,0},{9,105},{16,8},{17,113},{24,16},{25,121},{32,5... | collective-permute-start | bytes 1548296 | tf_op jit(solution)/shard_map/ppermute | solution.py:393
  17.4 14.3 %collective-permute-start.5 = (bf16[4,112,576]{2,1,0:T(8,128)(2,1)S(1)}, bf16[4,112,576]{2,1,0:T(8,128)(2,1)S(1)}, u32[]{:S(2)}, u32[]{:S(2)}) collective-permute-start(bf16[4,112,576]{2,1,0:T(8,128)(2,1)S(1)} %pad_maximum_fusion.1), channel_id=1, source_target_pairs={{0,16},{1,65},{8,24},{9,73},{16,0},{17,81},{24,8},{25,89},{32,48},... | collective-permute-start | bytes 1548296 | tf_op jit(solution)/shard_map/ppermute | solution.py:393
  19.2 1.2 copy-start.6
  20.4 0.7 copy-start.9
  21.1 0.7 copy-start.10
  24.4 1.8 copy-start.3
  26.2 11.0 %copy-start.11 = (f32[512,128]{1,0:T(8,128)}, f32[512,128]{1,0:T(8,128)S(1)}, u32[]{:S(2)}) copy-start(f32[512,128]{1,0:T(8,128)S(1)} %get-tuple-element.36.gate_ref) | copy-start | bytes 786436
  31.7 1.0 copy-start.21
  31.7 0.8 copy-start.19
  32.6 4.0 %copy-start.22 = (bf16[4,112,576]{2,1,0:T(8,128)(2,1)}, bf16[4,112,576]{2,1,0:T(8,128)(2,1)S(1)}, u32[]{:S(2)}) copy-start(bf16[4,112,576]{2,1,0:T(8,128)(2,1)S(1)} %collective-permute-done.5) | copy-start | bytes 1548292
  32.7 31.2 %collective-permute-start.10 = (bf16[1,3584,512]{2,1,0:T(8,128)(2,1)}, bf16[1,3584,512]{2,1,0:T(8,128)(2,1)}, u32[]{:S(2)}, u32[]{:S(2)}) collective-permute-start(bf16[1,3584,512]{2,1,0:T(8,128)(2,1)} %gate0), channel_id=1, source_target_pairs={{0,1},{1,0},{2,3},{3,2},{4,5},{5,4},{6,7},{7,6},{8,9},{9,8},{10,11... | collective-permute-start | bytes 11010056 | tf_op jit(solution)/shard_map/ppermute | solution.py:374
  36.5 58.1 %collective-permute-start.11 = (bf16[1,3584,512]{2,1,0:T(8,128)(2,1)}, bf16[1,3584,512]{2,1,0:T(8,128)(2,1)}, u32[]{:S(2)}, u32[]{:S(2)}) collective-permute-start(bf16[1,3584,512]{2,1,0:T(8,128)(2,1)} %up0), channel_id=1, source_target_pairs={{0,1},{1,0},{2,3},{3,2},{4,5},{5,4},{6,7},{7,6},{8,9},{9,8},{10,11... | collective-permute-start | bytes 11010056 | tf_op jit(solution)/shard_map/ppermute | solution.py:374
  37.2 57.4 %collective-permute-start.12 = (bf16[1,512,3584]{2,1,0:T(8,128)(2,1)}, bf16[1,512,3584]{2,1,0:T(8,128)(2,1)}, u32[]{:S(2)}, u32[]{:S(2)}) collective-permute-start(bf16[1,512,3584]{2,1,0:T(8,128)(2,1)} %down0), channel_id=1, source_target_pairs={{0,1},{1,0},{2,3},{3,2},{4,5},{5,4},{6,7},{7,6},{8,9},{9,8},{10,11... | collective-permute-start | bytes 11010056 | tf_op jit(solution)/shard_map/ppermute | solution.py:374
  37.2 57.4 %all-to-all-start = ((bf16[64,8,3584]{2,1,0:T(8,128)(2,1)}), bf16[64,8,3584]{2,1,0:T(8,128)(2,1)}, u32[]{:S(2)}, u32[]{:S(2)}) async-start(bf16[64,8,3584]{2,1,0:T(8,128)(2,1)} %bitcast.14), calls=%async_computation | async-start | bytes 7340032 | tf_op jit(solution)/shard_map/all_to_all | solution.py:406
  46.9 1.4 copy-start.23
  46.9 1.5 copy-start.20
  47.0 9.5 %copy-start.7 = (bf16[128,3584]{1,0:T(8,128)(2,1)S(1)}, bf16[128,3584]{1,0:T(8,128)(2,1)}, u32[]{:S(2)}) copy-start(bf16[128,3584]{1,0:T(8,128)(2,1)} %hidden_ref.3) | copy-start | bytes 2752516
  47.0 9.5 %copy-start.8 = (f32[512]{0:T(512)S(1)}, f32[512]{0:T(512)}, u32[]{:S(2)}) copy-start(f32[512]{0:T(512)} %param.12) | copy-start | bytes 6148
  48.5 8.0 %collective-permute-start.6 = (bf16[16,112,576]{2,1,0:T(8,128)(2,1)S(1)}, bf16[16,112,576]{2,1,0:T(8,128)(2,1)}, u32[]{:S(2)}, u32[]{:S(2)}) collective-permute-start(bf16[16,112,576]{2,1,0:T(8,128)(2,1)S(1)} %constant_dynamic-update-slice_fusion.mine_ref), channel_id=1, source_target_pairs={{0,1},{1,0},{2,3},{3,2},{4,5},{5,4},{6,7},{7,6},{8,9},{9,8},{10,11... | collective-permute-start | bytes 6193160 | tf_op jit(solution)/shard_map/ppermute | solution.py:374
  61.5 54.0 %copy-start.4 = (bf16[128,576]{1,0:T(8,128)(2,1)}, bf16[128,576]{1,0:T(8,128)(2,1)S(1)}, u32[]{:S(2)}) copy-start(bf16[128,576]{1,0:T(8,128)(2,1)S(1)} %shard_map.114) | copy-start | bytes 442372
  61.5 53.9 %collective-permute-start.7 = (bf16[128,576]{1,0:T(8,128)(2,1)S(1)}, bf16[128,576]{1,0:T(8,128)(2,1)S(1)}, u32[]{:S(2)}, u32[]{:S(2)}) collective-permute-start(bf16[128,576]{1,0:T(8,128)(2,1)S(1)} %shard_map.114), channel_id=1, source_target_pairs={{0,2},{2,4},{4,6},{6,0},{1,3},{3,5},{5,7},{7,1},{8,10},{10,12},{12... | collective-permute-start | bytes 442376 | tf_op jit(solution)/shard_map/ppermute | solution.py:379
  61.6 53.8 %collective-permute-start.8 = (bf16[128,576]{1,0:T(8,128)(2,1)S(1)}, bf16[128,576]{1,0:T(8,128)(2,1)S(1)}, u32[]{:S(2)}, u32[]{:S(2)}) collective-permute-start(bf16[128,576]{1,0:T(8,128)(2,1)S(1)} %shard_map.114), channel_id=1, source_target_pairs={{0,4},{2,6},{4,0},{6,2},{1,5},{3,7},{5,1},{7,3},{8,12},{10,14},{12... | collective-permute-start | bytes 442376 | tf_op jit(solution)/shard_map/ppermute | solution.py:379
  63.9 51.6 %collective-permute-start.9 = (bf16[128,576]{1,0:T(8,128)(2,1)S(1)}, bf16[128,576]{1,0:T(8,128)(2,1)}, u32[]{:S(2)}, u32[]{:S(2)}) collective-permute-start(bf16[128,576]{1,0:T(8,128)(2,1)S(1)} %shard_map.114), channel_id=1, source_target_pairs={{0,6},{2,0},{4,2},{6,4},{1,7},{3,1},{5,3},{7,5},{8,14},{10,8},{12,... | collective-permute-start | bytes 442376 | tf_op jit(solution)/shard_map/ppermute | solution.py:379
  115.4 0.7 copy-start.13
  115.4 0.7 copy-start.16
  116.2 11.4 %copy-start.2 = (bf16[128,12288]{1,0:T(8,128)(2,1)S(1)}, bf16[128,12288]{1,0:T(8,128)(2,1)}, u32[]{:S(2)}) copy-start(bf16[128,12288]{1,0:T(8,128)(2,1)} %mine_ref) | copy-start | bytes 9437188
  116.2 87.4 %all-to-all-start.1 = ((bf16[64,8,3584]{2,1,0:T(8,128)(2,1)}), bf16[64,8,3584]{2,1,0:T(8,128)(2,1)}, u32[]{:S(2)}, u32[]{:S(2)}) async-start(bf16[64,8,3584]{2,1,0:T(8,128)(2,1)} %bitcast.19), calls=%async_computation.1 | async-start | bytes 7340032 | tf_op jit(solution)/shard_map/all_to_all | solution.py:406
  127.6 4.3 %copy-start.5 = (bf16[128,576]{1,0:T(8,128)(2,1)S(1)}, bf16[128,576]{1,0:T(8,128)(2,1)}, u32[]{:S(2)}) copy-start(bf16[128,576]{1,0:T(8,128)(2,1)} %copy-done.4) | copy-start | bytes 442372
  127.6 4.3 %copy-start.14 = (bf16[128,576]{1,0:T(8,128)(2,1)S(1)}, bf16[128,576]{1,0:T(8,128)(2,1)}, u32[]{:S(2)}) copy-start(bf16[128,576]{1,0:T(8,128)(2,1)} %copy-done.13) | copy-start | bytes 442372
  127.6 4.3 %copy-start.17 = (bf16[128,576]{1,0:T(8,128)(2,1)S(1)}, bf16[128,576]{1,0:T(8,128)(2,1)}, u32[]{:S(2)}) copy-start(bf16[128,576]{1,0:T(8,128)(2,1)} %copy-done.16) | copy-start | bytes 442372
  129.9 4.1 %copy-start.15 = (bf16[128,576]{1,0:T(8,128)(2,1)S(1)}, bf16[128,576]{1,0:T(8,128)(2,1)}, u32[]{:S(2)}) copy-start(bf16[128,576]{1,0:T(8,128)(2,1)} %copy-done.13) | copy-start | bytes 442372
  129.9 4.1 %copy-start.18 = (bf16[128,576]{1,0:T(8,128)(2,1)S(1)}, bf16[128,576]{1,0:T(8,128)(2,1)}, u32[]{:S(2)}) copy-start(bf16[128,576]{1,0:T(8,128)(2,1)} %copy-done.16) | copy-start | bytes 442372
  129.9 9.6 %collective-permute-start.14 = (bf16[128,6144]{1,0:T(8,128)(2,1)}, bf16[128,6144]{1,0:T(8,128)(2,1)S(1)}, u32[]{:S(2)}, u32[]{:S(2)}) collective-permute-start(bf16[128,6144]{1,0:T(8,128)(2,1)} %shard_map.116), channel_id=1, source_target_pairs={{0,1},{1,0},{2,3},{3,2},{4,5},{5,4},{6,7},{7,6},{8,9},{9,8},{10,11... | collective-permute-start | bytes 4718600 | tf_op jit(solution)/shard_map/ppermute | solution.py:374
  133.9 2.3 %collective-permute-start.13 = (bf16[512,576]{0,1:T(8,128)(2,1)}, bf16[512,576]{0,1:T(8,128)(2,1)}, u32[]{:S(2)}, u32[]{:S(2)}) collective-permute-start(bf16[512,576]{0,1:T(8,128)(2,1)} %copy.16), channel_id=1, source_target_pairs={{0,1},{1,0},{2,3},{3,2},{4,5},{5,4},{6,7},{7,6},{8,9},{9,8},{10,11... | collective-permute-start | bytes 1769480 | tf_op jit(solution)/shard_map/ppermute | solution.py:374
  156.8 46.8 %copy-start.12 = (f32[512,128]{1,0:T(8,128)S(1)}, f32[512,128]{1,0:T(8,128)}, u32[]{:S(2)}) copy-start(f32[512,128]{1,0:T(8,128)} %copy-done.11) | copy-start | bytes 786436
  192.0 15.8 %collective-permute-start.15 = (bf16[128,4096]{1,0:T(8,128)(2,1)}, bf16[128,4096]{1,0:T(8,128)(2,1)S(1)}, u32[]{:S(2)}, u32[]{:S(2)}) collective-permute-start(bf16[128,4096]{1,0:T(8,128)(2,1)} %get-tuple-element.34), channel_id=1, source_target_pairs={{0,1},{1,0},{2,3},{3,2},{4,5},{5,4},{6,7},{7,6},{8,9},{9,8},{10,11... | collective-permute-start | bytes 3145736 | tf_op jit(solution)/shard_map/ppermute | solution.py:374
  207.8 2.2 copy-start.1
Sparse Core Ops, SparseCore 0:
  10.9 145.8 all-gather.1

commit v3 on v2

--- a/solution.py
+++ b/solution.py
@@ -91,15 +91,13 @@
 
     @pl.when(pl.program_id(0) == 0)
     def _():
-        rest = gate_ref[...]
+        rest = gate_ref[...].T
         for term in range(3):
             part = rest.astype(BF16)
-            terms[:, term * tokens : (term + 1) * tokens] = part
+            terms[term * tokens : (term + 1) * tokens, :] = part
             rest = rest - part.astype(F32)
 
-    total = lax.dot_general(
-        terms[...], rows_ref[...], (((0,), (0,)), ((), ())), preferred_element_type=F32
-    )
+    total = jnp.dot(terms[...], rows_ref[...], preferred_element_type=F32)
     out_ref[...] = (total[:tokens] + total[tokens : 2 * tokens] + total[2 * tokens :]).astype(BF16)
 
 
@@ -117,7 +115,7 @@
         ],
         out_specs=pl.BlockSpec((tokens, block), lambda j: (0, j)),
         out_shape=jax.ShapeDtypeStruct((tokens, width), BF16),
-        scratch_shapes=[pltpu.VMEM((slots, 3 * tokens), BF16)],
+        scratch_shapes=[pltpu.VMEM((3 * tokens, slots), BF16)],
     )(gate, rows)
 
 
@@ -440,6 +438,7 @@
     arrived = exchange(rows)
     mine_weight = spread(pieces)
     other = tuple(swap(array) for array in own)
+    other_queries = swap(other_groups(where, queries, 2 * chips))
 
     position = (2 * chip + core) * tokens + jnp.arange(tokens, dtype=jnp.int32)
     cosine, sine = rotation(position)
@@ -450,15 +449,14 @@
 
     results = experts(arrived, own, other)
     pieces, results = lax.optimization_barrier((pieces, results))
-    returned = exchange(results)
-
     line = jnp.concatenate(pieces, axis=0)
     sequence = jnp.concatenate([line, swap(line)], axis=0)
-
-    other_queries = swap(other_groups(where, queries, 2 * chips))
+    sequence, results = lax.optimization_barrier((sequence, results))
+    returned = exchange(results)
 
     whole, send = attend(where, sequence, kv_all, queries, other_queries)
     attention = merge(where, swap(send), whole, chips)
+    attention, returned = lax.optimization_barrier((attention, returned))
     routed = combine(gate, returned)
     return (attention, routed)
 

time: 217 us -> 195 us (0.90)
  the two profiles are of different devices: /device:TPU:95 before, /device:TPU:0 now
where the time goes in v3:
time: 195 us
  Pallas kernels  71.4 us (37%)
  waiting for transfers between devices  66.2 us (34%)
  starting transfers between devices  32.3 us (17%)
  between operations  14.3 us (7%)
  local copies, waits for them, and re-layouts  10 us (5%)
    all_to_all x2, waiting for transfers between devices, exchange(): return lax.all_to_all(rows, CHIPS, split_axis=0, concat_axis=0, tiled=True)  35.3 us
    pallas_call x1, Pallas kernels, attend(): call(attention_kernel, vmem=48, cost=(flops // 4, 2 * (LAT * heads * KV +...  35.2 us
    pallas_call x1, Pallas kernels, experts(): call(functools.partial(expert_kernel, steps=steps), vmem=56, cost=(12 * c...  21.1 us
    ppermute x7, waiting for transfers between devices, swap(): return lax.ppermute(array, 'c', [(0, 1), (1, 0)])  16.2 us
    all_to_all x2, starting transfers between devices, exchange(): return lax.all_to_all(rows, CHIPS, split_axis=0, concat_axis=0, tiled=True)  14.7 us
    ppermute x6, waiting for transfers between devices, turn(): return lax.ppermute(array, ('z', 'y', 'c'), pairs)  14 us
    ppermute x6, starting transfers between devices, turn(): return lax.ppermute(array, ('z', 'y', 'c'), pairs)  10.7 us
    unnamed x41, local copies, waits for them, and re-layouts  9.27 us
  transfers between devices with their start and end apart: 19, of which 10 were waited for; matrix products, arithmetic and copies ran while one was open for 1% of the time, Pallas kernels for 34%

profile of v3, /device:TPU:0, one launch (start us, length us, event | category | flops | bytes accessed | tf_op | source)
XLA Modules:
  0.0 194.9 jit_solution(1258838923510870177)
XLA Ops:
  7.2 0.0 copy-start
  7.2 0.0 all-gather.2.cloned.1.call-start
  7.2 0.7 all-gather.2.cloned.1.call-update
  7.9 0.2 copy-done
  8.1 4.2 %collective-permute-start.2 = (bf16[1,112,576]{2,1,0:T(8,128)(2,1)S(1)}, bf16[1,112,576]{2,1,0:T(8,128)(2,1)S(1)}, u32[]{:S(2)}, u32[]{:S(2)}) collective-permute-start(bf16[1,112,576]{2,1,0:T(8,128)(2,1)S(1)} %dynamic-slice_bitcast_fusion), channel_id=1, source_target_pairs={{0,96},{1,25},{8,104},{9,1},{16,112},{17,9},{24,120},{25,17},{32,0... | collective-permute-start | bytes 387080 | tf_op jit(solution)/shard_map/ppermute | solution.py:391
  12.3 1.3 collective-permute-start
  13.6 2.9 %collective-permute-done.2 = bf16[1,112,576]{2,1,0:T(8,128)(2,1)S(1)} collective-permute-done((bf16[1,112,576]{2,1,0:T(8,128)(2,1)S(1)}, bf16[1,112,576]{2,1,0:T(8,128)(2,1)S(1)}, u32[]{:S(2)}, u32[]{:S(2)}) %collective-permute-start.2) | collective-permute-done | bytes 129056 | tf_op jit(solution)/shard_map/ppermute | solution.py:391
  16.5 2.5 %collective-permute-done.1 = bf16[1,112,576]{2,1,0:T(8,128)(2,1)S(1)} collective-permute-done((bf16[1,112,576]{2,1,0:T(8,128)(2,1)S(1)}, bf16[1,112,576]{2,1,0:T(8,128)(2,1)S(1)}, u32[]{:S(2)}, u32[]{:S(2)}) %collective-permute-start.1) | collective-permute-done | bytes 129056 | tf_op jit(solution)/shard_map/ppermute | solution.py:391
  19.0 1.1 collective-permute-done
  20.2 0.1 pad_maximum_fusion.1
  20.3 1.6 collective-permute-start.3
  21.9 1.7 collective-permute-start.4
  23.6 2.0 %collective-permute-start.5 = (bf16[4,112,576]{2,1,0:T(8,128)(2,1)S(1)}, bf16[4,112,576]{2,1,0:T(8,128)(2,1)S(1)}, u32[]{:S(2)}, u32[]{:S(2)}) collective-permute-start(bf16[4,112,576]{2,1,0:T(8,128)(2,1)S(1)} %pad_maximum_fusion.1), channel_id=1, source_target_pairs={{0,16},{1,65},{8,24},{9,73},{16,0},{17,81},{24,8},{25,89},{32,48},... | collective-permute-start | bytes 1548296 | tf_op jit(solution)/shard_map/ppermute | solution.py:391
  25.6 1.2 copy-done.6
  26.8 0.7 copy-done.9
  27.5 0.7 copy-done.10
  28.1 2.7 %shard_map.113 = (bf16[512,3584]{1,0:T(8,128)(2,1)S(1)}, f32[512,128]{1,0:T(8,128)S(1)}) custom-call(s32[8,128]{1,0:T(8,128)S(1)} %bitcast.16, f32[8,128]{1,0:T(8,128)S(1)} %bitcast.17, bf16[128,3584]{1,0:T(8,128)(2,1)S(1)} %copy-done.6), custom_call_target="tpu_custom_call" | custom-call | flops 469762048 | bytes 4587520 | tf_op jit(solution)/shard_map/pallas_call | solution.py:68
  30.8 1.8 copy-done.3
  32.6 0.0 collective-permute-done.3
  32.6 0.0 collective-permute-done.4
  32.6 0.0 copy-start.13
  32.6 7.5 %collective-permute-done.5 = bf16[4,112,576]{2,1,0:T(8,128)(2,1)S(1)} collective-permute-done((bf16[4,112,576]{2,1,0:T(8,128)(2,1)S(1)}, bf16[4,112,576]{2,1,0:T(8,128)(2,1)S(1)}, u32[]{:S(2)}, u32[]{:S(2)}) %collective-permute-start.5) | collective-permute-done | bytes 516128 | tf_op jit(solution)/shard_map/ppermute | solution.py:391
  40.1 0.8 copy-done.15
  40.9 0.5 collective-permute-start.11
  41.4 0.0 collective-permute-start.12
  41.4 7.1 %all-to-all-start = ((bf16[64,8,3584]{2,1,0:T(8,128)(2,1)}), bf16[64,8,3584]{2,1,0:T(8,128)(2,1)}, u32[]{:S(2)}, u32[]{:S(2)}) async-start(bf16[64,8,3584]{2,1,0:T(8,128)(2,1)} %bitcast.14), calls=%async_computation | async-start | bytes 7340032 | tf_op jit(solution)/shard_map/all_to_all | solution.py:404
  48.5 0.0 copy-start.16
  48.5 0.0 copy-start.14
  48.5 0.1 constant_dynamic-update-slice_fusion.3
  48.6 0.0 copy-start.7
  48.6 0.0 copy-start.8
  48.6 1.3 constant_dynamic-update-slice_fusion.2
  49.9 0.1 constant_dynamic-update-slice_fusion.1
  50.0 0.1 constant_dynamic-update-slice_fusion.mine_ref
  50.1 0.3 collective-permute-start.6
  50.4 0.1 pad_add_fusion.where_ref
  50.5 0.3 fusion
  50.8 0.1 pad_maximum_fusion.2
  50.9 8.4 %collective-permute-done.6.other_ref = bf16[16,112,576]{2,1,0:T(8,128)(2,1)} collective-permute-done((bf16[16,112,576]{2,1,0:T(8,128)(2,1)S(1)}, bf16[16,112,576]{2,1,0:T(8,128)(2,1)}, u32[]{:S(2)}, u32[]{:S(2)}) %collective-permute-start.6) | collective-permute-done | bytes 2064416 | tf_op jit(solution)/shard_map/ppermute | solution.py:372
  59.3 5.0 %shard_map.114 = bf16[128,576]{1,0:T(8,128)(2,1)S(1)} custom-call(s32[4]{0:T(128)S(1)} %pad_add_fusion.where_ref, bf16[128,3584]{1,0:T(8,128)(2,1)S(1)} %copy-done.7, bf16[16,112,576]{2,1,0:T(8,128)(2,1)S(1)} %constant_dynamic-update-slice_fusion.mine_ref, bf16[16,112,576]{2,1,0:T(8,128)(2,1)} %collective-permute-done.6.other_ref, f32[1,512]{1,0:T(1,128)S(1)} %bitcast.15, ...), custom_call_target="tpu_custom_call" | custom-call | flops 528482304 | bytes 4128768 | tf_op jit(solution)/shard_map/pallas_call | solution.py:334
  64.3 1.6 collective-permute-start.7
  65.8 2.7 %collective-permute-start.8 = (bf16[128,576]{1,0:T(8,128)(2,1)S(1)}, bf16[128,576]{1,0:T(8,128)(2,1)S(1)}, u32[]{:S(2)}, u32[]{:S(2)}) collective-permute-start(bf16[128,576]{1,0:T(8,128)(2,1)S(1)} %shard_map.114), channel_id=1, source_target_pairs={{0,4},{2,6},{4,0},{6,2},{1,5},{3,7},{5,1},{7,3},{8,12},{10,14},{12... | collective-permute-start | bytes 442376 | tf_op jit(solution)/shard_map/ppermute | solution.py:377
  68.6 1.4 collective-permute-start.9
  70.0 32.6 %all-to-all-done = bf16[64,8,3584]{2,1,0:T(8,128)(2,1)} async-done(((bf16[64,8,3584]{2,1,0:T(8,128)(2,1)}), bf16[64,8,3584]{2,1,0:T(8,128)(2,1)}, u32[]{:S(2)}, u32[]{:S(2)}) %all-to-all-start) | async-done | bytes 3670048 | tf_op jit(solution)/shard_map/all_to_all | solution.py:404
  102.7 21.1 %shard_map.115 = bf16[512,3584]{1,0:T(8,128)(2,1)} custom-call(bf16[512,3584]{1,0:T(8,128)(2,1)} %bitcast.9.rows_ref, bf16[1,3584,512]{2,1,0:T(8,128)(2,1)} %gate0, bf16[1,3584,512]{2,1,0:T(8,128)(2,1)} %up0, bf16[1,512,3584]{2,1,0:T(8,128)(2,1)} %down0, bf16[1,3584,512]{2,1,0:T(8,128)(2,1)} %collective-permute-done.10.gate1, ...), custom_call_target="tpu_custom_call" | custom-call | flops 11274289152 | bytes 29360128 | tf_op jit(solution)/shard_map/pallas_call | solution.py:174
  123.8 0.1 pad_maximum_fusion
  123.8 0.3 copy.16
  124.1 0.1 collective-permute-start.13
  124.3 1.9 collective-permute-done.13
  126.2 0.3 copy.17
  126.5 0.1 constant_dynamic-update-slice_fusion.4.latent_ref
  126.6 0.0 copy-start.4
  126.6 1.0 copy-done.4
  127.6 7.6 %all-to-all-start.1 = ((bf16[64,8,3584]{2,1,0:T(8,128)(2,1)}), bf16[64,8,3584]{2,1,0:T(8,128)(2,1)}, u32[]{:S(2)}, u32[]{:S(2)}) async-start(bf16[64,8,3584]{2,1,0:T(8,128)(2,1)} %bitcast.19), calls=%async_computation.1 | async-start | bytes 7340032 | tf_op jit(solution)/shard_map/all_to_all | solution.py:404
  135.3 1.0 shard_map.116
  136.3 0.1 collective-permute-start.14
  136.4 3.4 %collective-permute-done.14.other_ref = bf16[128,6144]{1,0:T(8,128)(2,1)S(1)} collective-permute-done((bf16[128,6144]{1,0:T(8,128)(2,1)S(1)}, bf16[128,6144]{1,0:T(8,128)(2,1)S(1)}, u32[]{:S(2)}, u32[]{:S(2)}) %collective-permute-start.14) | collective-permute-done | bytes 1572896 | tf_op jit(solution)/shard_map/ppermute | solution.py:372
  139.8 1.3 copy-done.5
  141.1 35.2 %shard_map.117 = (bf16[128,8192]{1,0:T(8,128)(2,1)}, bf16[128,4096]{1,0:T(8,128)(2,1)S(1)}) custom-call(s32[4]{0:T(128)S(1)} %pad_add_fusion.where_ref, bf16[1024,576]{1,0:T(8,128)(2,1)S(1)} %copy-done.5, bf16[16,4,32,2048]{3,2,1,0:T(8,128)(2,1)} %bitcast.18, bf16[128,12288]{1,0:T(8,128)(2,1)} %mine_ref, bf16[128,6144]{1,0:T(8,128)(2,1)S(1)} %collective-permute-done.14.other_ref), custom_call_target="tpu_custom_call" | custom-call | flops 3489660928 | bytes 14680064 | tf_op jit(solution)/shard_map/pallas_call | solution.py:256
  176.4 0.1 collective-permute-start.15
  176.5 2.5 %collective-permute-done.15.part_ref = bf16[128,4096]{1,0:T(8,128)(2,1)S(1)} collective-permute-done((bf16[128,4096]{1,0:T(8,128)(2,1)S(1)}, bf16[128,4096]{1,0:T(8,128)(2,1)S(1)}, u32[]{:S(2)}, u32[]{:S(2)}) %collective-permute-start.15) | collective-permute-done | bytes 1048608 | tf_op jit(solution)/shard_map/ppermute | solution.py:372
  179.0 2.2 %shard_map.118 = bf16[128,8192]{1,0:T(8,128)(2,1)} custom-call(s32[4]{0:T(128)S(1)} %pad_add_fusion.where_ref, bf16[128,4096]{1,0:T(8,128)(2,1)S(1)} %collective-permute-done.15.part_ref, bf16[128,8192]{1,0:T(8,128)(2,1)} %get-tuple-element.41.whole_ref), custom_call_target="tpu_custom_call", output_to_operand_aliasing={{}: (2, {})} | custom-call | bytes 2097152 | tf_op jit(solution)/shard_map/pallas_call | solution.py:284
  181.2 2.6 %all-to-all-done.1 = bf16[64,8,3584]{2,1,0:T(8,128)(2,1)} async-done(((bf16[64,8,3584]{2,1,0:T(8,128)(2,1)}), bf16[64,8,3584]{2,1,0:T(8,128)(2,1)}, u32[]{:S(2)}, u32[]{:S(2)}) %all-to-all-start.1) | async-done | bytes 3670048 | tf_op jit(solution)/shard_map/all_to_all | solution.py:404
  183.8 4.2 %shard_map.119 = bf16[128,3584]{1,0:T(8,128)(2,1)} custom-call(f32[512,128]{1,0:T(8,128)S(1)} %copy-done.12, bf16[512,3584]{1,0:T(8,128)(2,1)} %bitcast.12.rows_ref), custom_call_target="tpu_custom_call" | custom-call | flops 1409286144 | bytes 4587520 | tf_op jit(solution)/shard_map/pallas_call | solution.py:108
  (35 shorter events, 0.2 us)
Async XLA Ops:
  7.2 1.0 copy-start
  7.2 132.6 %all-gather.2.cloned.1.call-start = ((), (), s32[]{:S(2)}) async-start(), calls=%async_computation.2 | async-start | bytes 8519680 | tf_op jit(solution)/shard_map/all_gather | solution.py:427
  8.1 8.4 %collective-permute-start.2 = (bf16[1,112,576]{2,1,0:T(8,128)(2,1)S(1)}, bf16[1,112,576]{2,1,0:T(8,128)(2,1)S(1)}, u32[]{:S(2)}, u32[]{:S(2)}) collective-permute-start(bf16[1,112,576]{2,1,0:T(8,128)(2,1)S(1)} %dynamic-slice_bitcast_fusion), channel_id=1, source_target_pairs={{0,96},{1,25},{8,104},{9,1},{16,112},{17,9},{24,120},{25,17},{32,0... | collective-permute-start | bytes 387080 | tf_op jit(solution)/shard_map/ppermute | solution.py:391
  12.3 6.7 %collective-permute-start.1 = (bf16[1,112,576]{2,1,0:T(8,128)(2,1)S(1)}, bf16[1,112,576]{2,1,0:T(8,128)(2,1)S(1)}, u32[]{:S(2)}, u32[]{:S(2)}) collective-permute-start(bf16[1,112,576]{2,1,0:T(8,128)(2,1)S(1)} %dynamic-slice_bitcast_fusion), channel_id=1, source_target_pairs={{0,64},{1,17},{8,72},{9,25},{16,80},{17,1},{24,88},{25,9},{32,96},... | collective-permute-start | bytes 387080 | tf_op jit(solution)/shard_map/ppermute | solution.py:391
  12.3 7.8 %collective-permute-start = (bf16[1,112,576]{2,1,0:T(8,128)(2,1)S(1)}, bf16[1,112,576]{2,1,0:T(8,128)(2,1)S(1)}, u32[]{:S(2)}, u32[]{:S(2)}) collective-permute-start(bf16[1,112,576]{2,1,0:T(8,128)(2,1)S(1)} %dynamic-slice_bitcast_fusion), channel_id=1, source_target_pairs={{0,32},{1,9},{8,40},{9,17},{16,48},{17,25},{24,56},{25,1},{32,64},... | collective-permute-start | bytes 387080 | tf_op jit(solution)/shard_map/ppermute | solution.py:391
  20.3 12.3 %collective-permute-start.3 = (bf16[4,112,576]{2,1,0:T(8,128)(2,1)S(1)}, bf16[4,112,576]{2,1,0:T(8,128)(2,1)}, u32[]{:S(2)}, u32[]{:S(2)}) collective-permute-start(bf16[4,112,576]{2,1,0:T(8,128)(2,1)S(1)} %pad_maximum_fusion.1), channel_id=1, source_target_pairs={{0,8},{1,33},{8,16},{9,41},{16,24},{17,49},{24,0},{25,57},{32,40},... | collective-permute-start | bytes 1548296 | tf_op jit(solution)/shard_map/ppermute | solution.py:391
  21.9 10.7 %collective-permute-start.4 = (bf16[4,112,576]{2,1,0:T(8,128)(2,1)S(1)}, bf16[4,112,576]{2,1,0:T(8,128)(2,1)S(1)}, u32[]{:S(2)}, u32[]{:S(2)}) collective-permute-start(bf16[4,112,576]{2,1,0:T(8,128)(2,1)S(1)} %pad_maximum_fusion.1), channel_id=1, source_target_pairs={{0,24},{1,97},{8,0},{9,105},{16,8},{17,113},{24,16},{25,121},{32,5... | collective-permute-start | bytes 1548296 | tf_op jit(solution)/shard_map/ppermute | solution.py:391
  23.6 16.5 %collective-permute-start.5 = (bf16[4,112,576]{2,1,0:T(8,128)(2,1)S(1)}, bf16[4,112,576]{2,1,0:T(8,128)(2,1)S(1)}, u32[]{:S(2)}, u32[]{:S(2)}) collective-permute-start(bf16[4,112,576]{2,1,0:T(8,128)(2,1)S(1)} %pad_maximum_fusion.1), channel_id=1, source_target_pairs={{0,16},{1,65},{8,24},{9,73},{16,0},{17,81},{24,8},{25,89},{32,48},... | collective-permute-start | bytes 1548296 | tf_op jit(solution)/shard_map/ppermute | solution.py:391
  25.6 1.2 copy-start.6
  26.8 0.7 copy-start.9
  27.5 0.7 copy-start.10
  30.8 1.8 copy-start.3
  32.6 8.8 %copy-start.11 = (f32[512,128]{1,0:T(8,128)}, f32[512,128]{1,0:T(8,128)S(1)}, u32[]{:S(2)}) copy-start(f32[512,128]{1,0:T(8,128)S(1)} %get-tuple-element.44.gate_ref) | copy-start | bytes 786436
  32.6 7.5 %copy-start.13 = (bf16[4,112,576]{2,1,0:T(8,128)(2,1)}, bf16[4,112,576]{2,1,0:T(8,128)(2,1)S(1)}, u32[]{:S(2)}) copy-start(bf16[4,112,576]{2,1,0:T(8,128)(2,1)S(1)} %collective-permute-done.4) | copy-start | bytes 1548292
  40.1 0.8 copy-start.15
  40.9 27.7 %collective-permute-start.10 = (bf16[1,3584,512]{2,1,0:T(8,128)(2,1)}, bf16[1,3584,512]{2,1,0:T(8,128)(2,1)}, u32[]{:S(2)}, u32[]{:S(2)}) collective-permute-start(bf16[1,3584,512]{2,1,0:T(8,128)(2,1)} %gate0), channel_id=1, source_target_pairs={{0,1},{1,0},{2,3},{3,2},{4,5},{5,4},{6,7},{7,6},{8,9},{9,8},{10,11... | collective-permute-start | bytes 11010056 | tf_op jit(solution)/shard_map/ppermute | solution.py:372
  40.9 61.7 %collective-permute-start.11 = (bf16[1,3584,512]{2,1,0:T(8,128)(2,1)}, bf16[1,3584,512]{2,1,0:T(8,128)(2,1)}, u32[]{:S(2)}, u32[]{:S(2)}) collective-permute-start(bf16[1,3584,512]{2,1,0:T(8,128)(2,1)} %up0), channel_id=1, source_target_pairs={{0,1},{1,0},{2,3},{3,2},{4,5},{5,4},{6,7},{7,6},{8,9},{9,8},{10,11... | collective-permute-start | bytes 11010056 | tf_op jit(solution)/shard_map/ppermute | solution.py:372
  41.4 61.2 %collective-permute-start.12 = (bf16[1,512,3584]{2,1,0:T(8,128)(2,1)}, bf16[1,512,3584]{2,1,0:T(8,128)(2,1)}, u32[]{:S(2)}, u32[]{:S(2)}) collective-permute-start(bf16[1,512,3584]{2,1,0:T(8,128)(2,1)} %down0), channel_id=1, source_target_pairs={{0,1},{1,0},{2,3},{3,2},{4,5},{5,4},{6,7},{7,6},{8,9},{9,8},{10,11... | collective-permute-start | bytes 11010056 | tf_op jit(solution)/shard_map/ppermute | solution.py:372
  41.4 61.2 %all-to-all-start = ((bf16[64,8,3584]{2,1,0:T(8,128)(2,1)}), bf16[64,8,3584]{2,1,0:T(8,128)(2,1)}, u32[]{:S(2)}, u32[]{:S(2)}) async-start(bf16[64,8,3584]{2,1,0:T(8,128)(2,1)} %bitcast.14), calls=%async_computation | async-start | bytes 7340032 | tf_op jit(solution)/shard_map/all_to_all | solution.py:404
  48.5 1.4 copy-start.16
  48.5 1.5 copy-start.14
  48.6 10.7 %copy-start.7 = (bf16[128,3584]{1,0:T(8,128)(2,1)S(1)}, bf16[128,3584]{1,0:T(8,128)(2,1)}, u32[]{:S(2)}) copy-start(bf16[128,3584]{1,0:T(8,128)(2,1)} %hidden_ref.3) | copy-start | bytes 2752516
  48.6 10.7 %copy-start.8 = (f32[512]{0:T(512)S(1)}, f32[512]{0:T(512)}, u32[]{:S(2)}) copy-start(f32[512]{0:T(512)} %param.12) | copy-start | bytes 6148
  50.1 9.2 %collective-permute-start.6 = (bf16[16,112,576]{2,1,0:T(8,128)(2,1)S(1)}, bf16[16,112,576]{2,1,0:T(8,128)(2,1)}, u32[]{:S(2)}, u32[]{:S(2)}) collective-permute-start(bf16[16,112,576]{2,1,0:T(8,128)(2,1)S(1)} %constant_dynamic-update-slice_fusion.mine_ref), channel_id=1, source_target_pairs={{0,1},{1,0},{2,3},{3,2},{4,5},{5,4},{6,7},{7,6},{8,9},{9,8},{10,11... | collective-permute-start | bytes 6193160 | tf_op jit(solution)/shard_map/ppermute | solution.py:372
  64.3 59.5 %collective-permute-start.7 = (bf16[128,576]{1,0:T(8,128)(2,1)S(1)}, bf16[128,576]{1,0:T(8,128)(2,1)S(1)}, u32[]{:S(2)}, u32[]{:S(2)}) collective-permute-start(bf16[128,576]{1,0:T(8,128)(2,1)S(1)} %shard_map.114), channel_id=1, source_target_pairs={{0,2},{2,4},{4,6},{6,0},{1,3},{3,5},{5,7},{7,1},{8,10},{10,12},{12... | collective-permute-start | bytes 442376 | tf_op jit(solution)/shard_map/ppermute | solution.py:377
  65.8 57.9 %collective-permute-start.8 = (bf16[128,576]{1,0:T(8,128)(2,1)S(1)}, bf16[128,576]{1,0:T(8,128)(2,1)S(1)}, u32[]{:S(2)}, u32[]{:S(2)}) collective-permute-start(bf16[128,576]{1,0:T(8,128)(2,1)S(1)} %shard_map.114), channel_id=1, source_target_pairs={{0,4},{2,6},{4,0},{6,2},{1,5},{3,7},{5,1},{7,3},{8,12},{10,14},{12... | collective-permute-start | bytes 442376 | tf_op jit(solution)/shard_map/ppermute | solution.py:377
  68.6 55.2 %collective-permute-start.9 = (bf16[128,576]{1,0:T(8,128)(2,1)S(1)}, bf16[128,576]{1,0:T(8,128)(2,1)S(1)}, u32[]{:S(2)}, u32[]{:S(2)}) collective-permute-start(bf16[128,576]{1,0:T(8,128)(2,1)S(1)} %shard_map.114), channel_id=1, source_target_pairs={{0,6},{2,0},{4,2},{6,4},{1,7},{3,1},{5,3},{7,5},{8,14},{10,8},{12,... | collective-permute-start | bytes 442376 | tf_op jit(solution)/shard_map/ppermute | solution.py:377
  124.1 2.1 %collective-permute-start.13 = (bf16[512,576]{0,1:T(8,128)(2,1)S(1)}, bf16[512,576]{0,1:T(8,128)(2,1)S(1)}, u32[]{:S(2)}, u32[]{:S(2)}) collective-permute-start(bf16[512,576]{0,1:T(8,128)(2,1)S(1)} %copy.16), channel_id=1, source_target_pairs={{0,1},{1,0},{2,3},{3,2},{4,5},{5,4},{6,7},{7,6},{8,9},{9,8},{10,11... | collective-permute-start | bytes 1769480 | tf_op jit(solution)/shard_map/ppermute | solution.py:372
  126.6 1.1 copy-start.4
  127.6 7.7 %copy-start.2 = (bf16[128,12288]{1,0:T(8,128)(2,1)S(1)}, bf16[128,12288]{1,0:T(8,128)(2,1)}, u32[]{:S(2)}) copy-start(bf16[128,12288]{1,0:T(8,128)(2,1)} %mine_ref) | copy-start | bytes 9437188
  127.6 56.2 %all-to-all-start.1 = ((bf16[64,8,3584]{2,1,0:T(8,128)(2,1)}), bf16[64,8,3584]{2,1,0:T(8,128)(2,1)}, u32[]{:S(2)}, u32[]{:S(2)}) async-start(bf16[64,8,3584]{2,1,0:T(8,128)(2,1)} %bitcast.19), calls=%async_computation.1 | async-start | bytes 7340032 | tf_op jit(solution)/shard_map/all_to_all | solution.py:404
  136.3 3.5 %collective-permute-start.14 = (bf16[128,6144]{1,0:T(8,128)(2,1)S(1)}, bf16[128,6144]{1,0:T(8,128)(2,1)S(1)}, u32[]{:S(2)}, u32[]{:S(2)}) collective-permute-start(bf16[128,6144]{1,0:T(8,128)(2,1)S(1)} %shard_map.116), channel_id=1, source_target_pairs={{0,1},{1,0},{2,3},{3,2},{4,5},{5,4},{6,7},{7,6},{8,9},{9,8},{10,11... | collective-permute-start | bytes 4718600 | tf_op jit(solution)/shard_map/ppermute | solution.py:372
  139.8 1.3 copy-start.5
  176.4 2.7 %collective-permute-start.15 = (bf16[128,4096]{1,0:T(8,128)(2,1)S(1)}, bf16[128,4096]{1,0:T(8,128)(2,1)S(1)}, u32[]{:S(2)}, u32[]{:S(2)}) collective-permute-start(bf16[128,4096]{1,0:T(8,128)(2,1)S(1)} %get-tuple-element.40), channel_id=1, source_target_pairs={{0,1},{1,0},{2,3},{3,2},{4,5},{5,4},{6,7},{7,6},{8,9},{9,8},{10,11... | collective-permute-start | bytes 3145736 | tf_op jit(solution)/shard_map/ppermute | solution.py:372
  179.0 4.8 %copy-start.12 = (f32[512,128]{1,0:T(8,128)S(1)}, f32[512,128]{1,0:T(8,128)}, u32[]{:S(2)}) copy-start(f32[512,128]{1,0:T(8,128)} %copy-done.11) | copy-start | bytes 786436
  183.8 4.2 %copy-start.1 = (bf16[224,576]{1,0:T(8,128)(2,1)S(1)}, bf16[224,576]{1,0:T(8,128)(2,1)}, u32[]{:S(2)}) copy-start(bf16[224,576]{1,0:T(8,128)(2,1)} %param.11) | copy-start | bytes 774148
Sparse Core Ops, SparseCore 0:
  10.9 124.0 all-gather.1

commit v4 on v3

--- a/solution.py
+++ b/solution.py
@@ -193,8 +193,8 @@
     @pl.when(pl.program_id(0) == 0)
     def _():
         core, chip = where_ref[0], where_ref[1]
-        row = lax.broadcasted_iota(jnp.int32, (2 * tokens, length), 0)
-        col = lax.broadcasted_iota(jnp.int32, (2 * tokens, length), 1)
+        row = lax.broadcasted_iota(jnp.int32, (length, 2 * tokens), 1)
+        col = lax.broadcasted_iota(jnp.int32, (length, 2 * tokens), 0)
         row_core = jnp.where(row < tokens, core, 1 - core)
         row_at = (2 * chip + row_core) * tokens + row % tokens
         block = col // tokens
@@ -205,23 +205,26 @@
 
     compressed = latent_ref[:, :LAT]
     rope = latent_ref[:, LAT:]
-    weight = kv_ref[...].reshape(LAT, 2 * KV)
+    group = kv_ref.shape[3] // KV
+    weight = kv_ref[...].reshape(LAT, group * KV)
     keyval = jnp.dot(compressed, weight, preferred_element_type=F32).astype(BF16)
     factor = math.log2(math.e) / math.sqrt(HEAD)
-    for head in range(2):
+    for head in range(group):
         keys = jnp.concatenate([keyval[:, head * KV : head * KV + NOPE], rope], axis=1)
         values = keyval[:, head * KV + NOPE : (head + 1) * KV]
         span = slice(head * HEAD, (head + 1) * HEAD)
         query = jnp.concatenate([mine_ref[:, span], other_ref[:, span]], axis=0)
         score = lax.dot_general(
-            query, keys, (((1,), (1,)), ((), ())), preferred_element_type=F32
+            keys, query, (((1,), (1,)), ((), ())), preferred_element_type=F32
         )
         score = score + bias[...]
-        top = jnp.max(score, axis=1, keepdims=True)
+        top = jnp.max(score, axis=0, keepdims=True)
         weights = jnp.exp2((score - top) * factor)
-        inverse = 1.0 / jnp.sum(weights, axis=1, keepdims=True)
+        inverse = 1.0 / jnp.sum(weights, axis=0, keepdims=True)
         probs = (weights * inverse).astype(BF16)
-        result = jnp.dot(probs, values, preferred_element_type=F32).astype(BF16)
+        result = lax.dot_general(
+            probs, values, (((0,), (0,)), ((), ())), preferred_element_type=F32
+        ).astype(BF16)
         span = slice(head * VDIM, (head + 1) * VDIM)
         out_ref[:, span] = result[:tokens]
         send_ref[:, span] = result[tokens:]
@@ -231,26 +234,26 @@
     tokens = mine.shape[0]
     length = latent.shape[0]
     nodes, chips, rows, columns = kv_weight.shape
-    pairs = columns // (2 * KV)
-    heads = 2 * pairs * chips
+    group = columns // KV
+    heads = group * chips
     spec = pltpu.PrefetchScalarGridSpec(
         num_scalar_prefetch=1,
-        grid=(chips * pairs,),
+        grid=(chips,),
         in_specs=[
             pl.BlockSpec((length, LAT + ROPE), lambda i, w: (0, 0)),
-            pl.BlockSpec((nodes, 1, rows, 2 * KV), lambda i, w: (0, i // pairs, 0, i % pairs)),
+            pl.BlockSpec((nodes, 1, rows, group * KV), lambda i, w: (0, i, 0, 0)),
             pl.BlockSpec(
-                (tokens, 2 * HEAD), lambda i, w: (0, (2 * (i // pairs) + w[0]) * pairs + i % pairs)
+                (tokens, group * HEAD), lambda i, w: (0, 2 * i + w[0])
             ),
-            pl.BlockSpec((tokens, 2 * HEAD), lambda i, w: (0, i)),
+            pl.BlockSpec((tokens, group * HEAD), lambda i, w: (0, i)),
         ],
         out_specs=[
             pl.BlockSpec(
-                (tokens, 2 * VDIM), lambda i, w: (0, (2 * (i // pairs) + w[0]) * pairs + i % pairs)
+                (tokens, group * VDIM), lambda i, w: (0, 2 * i + w[0])
             ),
-            pl.BlockSpec((tokens, 2 * VDIM), lambda i, w: (0, i)),
-        ],
-        scratch_shapes=[pltpu.VMEM((2 * tokens, length), F32)],
+            pl.BlockSpec((tokens, group * VDIM), lambda i, w: (0, i)),
+        ],
+        scratch_shapes=[pltpu.VMEM((length, 2 * tokens), F32)],
     )
     flops = 2 * heads * length * (LAT * KV + 2 * tokens * (HEAD + VDIM))
     return call(
@@ -451,7 +454,6 @@
     pieces, results = lax.optimization_barrier((pieces, results))
     line = jnp.concatenate(pieces, axis=0)
     sequence = jnp.concatenate([line, swap(line)], axis=0)
-    sequence, results = lax.optimization_barrier((sequence, results))
     returned = exchange(results)
 
     whole, send = attend(where, sequence, kv_all, queries, other_queries)

time: 195 us -> 213 us (1.092)
  the two profiles are of different devices: /device:TPU:0 before, /device:TPU:95 now
where the time goes in v4:
time: 213 us; the launch traced here: 212 us
  waiting for transfers between devices  68.5 us (32%)
  Pallas kernels  65.2 us (31%)
  starting transfers between devices  49.1 us (23%)
  between operations  14.3 us (7%)
  local copies, waits for them, and re-layouts  13.2 us (6%)
    all_to_all x2, waiting for transfers between devices, exchange(): return lax.all_to_all(rows, CHIPS, split_axis=0, concat_axis=0, tiled=True)  30.8 us
    pallas_call x1, Pallas kernels, attend(): call(attention_kernel, vmem=48, cost=(flops // 4, 2 * (LAT * heads * KV +...  28.1 us
    all_to_all x2, starting transfers between devices, exchange(): return lax.all_to_all(rows, CHIPS, split_axis=0, concat_axis=0, tiled=True)  21.1 us
    pallas_call x1, Pallas kernels, experts(): call(functools.partial(expert_kernel, steps=steps), vmem=56, cost=(12 * c...  20.8 us
    ppermute x7, starting transfers between devices, swap(): return lax.ppermute(array, 'c', [(0, 1), (1, 0)])  19.2 us
    all_gather x1, waiting for transfers between devices, shards(): kv_all = lax.all_gather(kv_weight, CHIPS, axis=0, tiled=True)  17.2 us
    ppermute x6, waiting for transfers between devices, turn(): return lax.ppermute(array, ('z', 'y', 'c'), pairs)  10 us
    ppermute x7, waiting for transfers between devices, swap(): return lax.ppermute(array, 'c', [(0, 1), (1, 0)])  9.82 us
  transfers between devices with their start and end apart: 19, of which 8 were waited for; matrix products, arithmetic and copies ran while one was open for 4% of the time, Pallas kernels for 29%

profile of v4, /device:TPU:95, one launch (start us, length us, event | category | flops | bytes accessed | tf_op | source)
XLA Modules:
  0.0 211.9 jit_solution(2903314674472462499)
XLA Ops:
  7.2 0.0 copy-start
  7.2 0.0 all-gather.2.cloned.1.call-start
  7.2 0.7 all-gather.2.cloned.1.call-update
  7.9 0.2 copy-done
  8.1 0.5 collective-permute-start.2
  8.7 0.7 collective-permute-start.1
  9.3 1.9 collective-permute-start
  11.2 3.8 %collective-permute-done.2 = bf16[1,112,576]{2,1,0:T(8,128)(2,1)S(1)} collective-permute-done((bf16[1,112,576]{2,1,0:T(8,128)(2,1)S(1)}, bf16[1,112,576]{2,1,0:T(8,128)(2,1)S(1)}, u32[]{:S(2)}, u32[]{:S(2)}) %collective-permute-start.2) | collective-permute-done | bytes 129056 | tf_op jit(solution)/shard_map/ppermute | solution.py:394
  15.1 0.7 collective-permute-done
  15.8 0.1 pad_maximum_fusion.1
  15.9 1.4 collective-permute-start.3
  17.3 0.1 collective-permute-start.4
  17.4 1.7 collective-permute-start.5
  19.2 1.2 copy-done.6
  20.4 0.7 copy-done.9
  21.1 0.7 copy-done.10
  21.7 2.7 %shard_map.113 = (bf16[512,3584]{1,0:T(8,128)(2,1)S(1)}, f32[512,128]{1,0:T(8,128)S(1)}) custom-call(s32[8,128]{1,0:T(8,128)S(1)} %bitcast.16, f32[8,128]{1,0:T(8,128)S(1)} %bitcast.17, bf16[128,3584]{1,0:T(8,128)(2,1)S(1)} %copy-done.6), custom_call_target="tpu_custom_call" | custom-call | flops 469762048 | bytes 4587520 | tf_op jit(solution)/shard_map/pallas_call | solution.py:68
  24.4 1.8 copy-done.3
  26.2 5.5 %collective-permute-done.3 = bf16[4,112,576]{2,1,0:T(8,128)(2,1)S(1)} collective-permute-done((bf16[4,112,576]{2,1,0:T(8,128)(2,1)S(1)}, bf16[4,112,576]{2,1,0:T(8,128)(2,1)S(1)}, u32[]{:S(2)}, u32[]{:S(2)}) %collective-permute-start.3) | collective-permute-done | bytes 516128 | tf_op jit(solution)/shard_map/ppermute | solution.py:394
  31.7 0.0 collective-permute-done.4
  31.7 0.0 collective-permute-done.5
  31.7 0.8 copy-done.19
  32.6 0.1 copy-done.21
  32.7 3.8 %collective-permute-start.10 = (bf16[1,3584,512]{2,1,0:T(8,128)(2,1)}, bf16[1,3584,512]{2,1,0:T(8,128)(2,1)}, u32[]{:S(2)}, u32[]{:S(2)}) collective-permute-start(bf16[1,3584,512]{2,1,0:T(8,128)(2,1)} %gate0), channel_id=1, source_target_pairs={{0,1},{1,0},{2,3},{3,2},{4,5},{5,4},{6,7},{7,6},{8,9},{9,8},{10,11... | collective-permute-start | bytes 11010056 | tf_op jit(solution)/shard_map/ppermute | solution.py:375
  36.5 0.7 collective-permute-start.11
  37.2 9.7 %all-to-all-start = ((bf16[64,8,3584]{2,1,0:T(8,128)(2,1)}), bf16[64,8,3584]{2,1,0:T(8,128)(2,1)}, u32[]{:S(2)}, u32[]{:S(2)}) async-start(bf16[64,8,3584]{2,1,0:T(8,128)(2,1)} %bitcast.14), calls=%async_computation | async-start | bytes 7340032 | tf_op jit(solution)/shard_map/all_to_all | solution.py:407
  46.9 0.0 copy-start.23
  46.9 0.1 constant_dynamic-update-slice_fusion.3
  47.0 0.0 copy-start.7
  47.0 0.0 copy-start.8
  47.0 1.3 constant_dynamic-update-slice_fusion.2
  48.3 0.1 constant_dynamic-update-slice_fusion.1
  48.4 0.1 constant_dynamic-update-slice_fusion.mine_ref
  48.5 1.2 collective-permute-start.6
  49.7 0.1 pad_add_fusion.where_ref
  49.7 0.3 fusion
  50.1 0.1 pad_maximum_fusion.2
  50.2 6.3 %collective-permute-done.6.other_ref = bf16[16,112,576]{2,1,0:T(8,128)(2,1)} collective-permute-done((bf16[16,112,576]{2,1,0:T(8,128)(2,1)S(1)}, bf16[16,112,576]{2,1,0:T(8,128)(2,1)}, u32[]{:S(2)}, u32[]{:S(2)}) %collective-permute-start.6) | collective-permute-done | bytes 2064416 | tf_op jit(solution)/shard_map/ppermute | solution.py:375
  56.5 5.0 %shard_map.114 = bf16[128,576]{1,0:T(8,128)(2,1)S(1)} custom-call(s32[4]{0:T(128)S(1)} %pad_add_fusion.where_ref, bf16[128,3584]{1,0:T(8,128)(2,1)S(1)} %copy-done.7, bf16[16,112,576]{2,1,0:T(8,128)(2,1)S(1)} %constant_dynamic-update-slice_fusion.mine_ref, bf16[16,112,576]{2,1,0:T(8,128)(2,1)} %collective-permute-done.6.other_ref, f32[1,512]{1,0:T(1,128)S(1)} %bitcast.15, ...), custom_call_target="tpu_custom_call" | custom-call | flops 528482304 | bytes 4128768 | tf_op jit(solution)/shard_map/pallas_call | solution.py:337
  61.4 0.0 copy-start.4
  61.5 0.1 collective-permute-start.7
  61.6 2.3 %collective-permute-start.8 = (bf16[128,576]{1,0:T(8,128)(2,1)S(1)}, bf16[128,576]{1,0:T(8,128)(2,1)S(1)}, u32[]{:S(2)}, u32[]{:S(2)}) collective-permute-start(bf16[128,576]{1,0:T(8,128)(2,1)S(1)} %shard_map.114), channel_id=1, source_target_pairs={{0,4},{2,6},{4,0},{6,2},{1,5},{3,7},{5,1},{7,3},{8,12},{10,14},{12... | collective-permute-start | bytes 442376 | tf_op jit(solution)/shard_map/ppermute | solution.py:380
  63.9 0.0 collective-permute-start.9
  63.9 30.8 %all-to-all-done = bf16[64,8,3584]{2,1,0:T(8,128)(2,1)} async-done(((bf16[64,8,3584]{2,1,0:T(8,128)(2,1)}), bf16[64,8,3584]{2,1,0:T(8,128)(2,1)}, u32[]{:S(2)}, u32[]{:S(2)}) %all-to-all-start) | async-done | bytes 3670048 | tf_op jit(solution)/shard_map/all_to_all | solution.py:407
  94.6 20.8 %shard_map.115 = bf16[512,3584]{1,0:T(8,128)(2,1)} custom-call(bf16[512,3584]{1,0:T(8,128)(2,1)} %bitcast.9.rows_ref, bf16[1,3584,512]{2,1,0:T(8,128)(2,1)} %gate0, bf16[1,3584,512]{2,1,0:T(8,128)(2,1)} %up0, bf16[1,512,3584]{2,1,0:T(8,128)(2,1)} %down0, bf16[1,3584,512]{2,1,0:T(8,128)(2,1)} %collective-permute-done.10.gate1, ...), custom_call_target="tpu_custom_call" | custom-call | flops 11274289152 | bytes 29360128 | tf_op jit(solution)/shard_map/pallas_call | solution.py:174
  115.5 0.6 copy-done.13
  116.1 0.1 copy-done.16
  116.2 11.4 %all-to-all-start.1 = ((bf16[64,8,3584]{2,1,0:T(8,128)(2,1)}), bf16[64,8,3584]{2,1,0:T(8,128)(2,1)}, u32[]{:S(2)}, u32[]{:S(2)}) async-start(bf16[64,8,3584]{2,1,0:T(8,128)(2,1)} %bitcast.19), calls=%async_computation.1 | async-start | bytes 7340032 | tf_op jit(solution)/shard_map/all_to_all | solution.py:407
  127.6 0.0 copy-start.5
  127.6 2.3 %shard_map.116 = bf16[128,6144]{1,0:T(8,128)(2,1)} custom-call(s32[4]{0:T(128)S(1)} %pad_add_fusion.where_ref, bf16[128,12288]{1,0:T(8,128)(2,1)S(1)} %copy-done.2), custom_call_target="tpu_custom_call" | custom-call | bytes 3145728 | tf_op jit(solution)/shard_map/pallas_call | solution.py:366
  129.9 1.9 collective-permute-start.14
  131.9 1.0 pad_maximum_fusion
  132.8 1.1 copy.16
  133.9 0.1 collective-permute-start.13
  134.1 0.9 constant_dynamic-update-slice_fusion.5
  135.0 1.2 collective-permute-done.13
  136.3 2.1 %copy.17 = bf16[512,576]{1,0:T(8,128)(2,1)} copy(bf16[512,576]{0,1:T(8,128)(2,1)} %collective-permute-done.13) | data formatting | bytes 1179648 | tf_op jit(solution)/shard_map/ppermute | solution.py:375
  138.4 1.2 constant_dynamic-update-slice_fusion.4.latent_ref
  139.6 17.2 %all-gather.2.cloned.1.call-done = bf16[2048,2048]{1,0:T(8,128)(2,1)} async-done(((bf16[32,2048]{1,0:T(8,128)(2,1)}), bf16[2048,2048]{1,0:T(8,128)(2,1)}) %all-gather.2.cloned.1.call-update) | async-done | bytes 8388624 | tf_op jit(solution)/shard_map/all_gather | solution.py:430
  156.8 28.1 %shard_map.117 = (bf16[128,8192]{1,0:T(8,128)(2,1)}, bf16[128,4096]{1,0:T(8,128)(2,1)S(1)}) custom-call(s32[4]{0:T(128)S(1)} %pad_add_fusion.where_ref, bf16[1024,576]{1,0:T(8,128)(2,1)S(1)} %constant_dynamic-update-slice_fusion.4.latent_ref, bf16[16,4,32,2048]{3,2,1,0:T(8,128)(2,1)} %bitcast.18, bf16[128,12288]{1,0:T(8,128)(2,1)} %mine_ref, ...), custom_call_target="tpu_custom_call" | custom-call | flops 3489660928 | bytes 14680064 | tf_op jit(solution)/shard_map/pallas_call | solution.py:259
  184.8 11.6 %collective-permute-start.15 = (bf16[128,4096]{1,0:T(8,128)(2,1)S(1)}, bf16[128,4096]{1,0:T(8,128)(2,1)S(1)}, u32[]{:S(2)}, u32[]{:S(2)}) collective-permute-start(bf16[128,4096]{1,0:T(8,128)(2,1)S(1)} %get-tuple-element.36), channel_id=1, source_target_pairs={{0,1},{1,0},{2,3},{3,2},{4,5},{5,4},{6,7},{7,6},{8,9},{9,8},{10,11... | collective-permute-start | bytes 3145736 | tf_op jit(solution)/shard_map/ppermute | solution.py:375
  196.4 2.3 %collective-permute-done.15.part_ref = bf16[128,4096]{1,0:T(8,128)(2,1)S(1)} collective-permute-done((bf16[128,4096]{1,0:T(8,128)(2,1)S(1)}, bf16[128,4096]{1,0:T(8,128)(2,1)S(1)}, u32[]{:S(2)}, u32[]{:S(2)}) %collective-permute-start.15) | collective-permute-done | bytes 1048608 | tf_op jit(solution)/shard_map/ppermute | solution.py:375
  198.7 2.2 %shard_map.118 = bf16[128,8192]{1,0:T(8,128)(2,1)} custom-call(s32[4]{0:T(128)S(1)} %pad_add_fusion.where_ref, bf16[128,4096]{1,0:T(8,128)(2,1)S(1)} %collective-permute-done.15.part_ref, bf16[128,8192]{1,0:T(8,128)(2,1)} %get-tuple-element.37.whole_ref), custom_call_target="tpu_custom_call", output_to_operand_aliasing={{}: (2, {})} | custom-call | bytes 2097152 | tf_op jit(solution)/shard_map/pallas_call | solution.py:287
  200.8 4.2 %shard_map.119 = bf16[128,3584]{1,0:T(8,128)(2,1)} custom-call(f32[512,128]{1,0:T(8,128)S(1)} %copy-done.12, bf16[512,3584]{1,0:T(8,128)(2,1)} %bitcast.12.rows_ref), custom_call_target="tpu_custom_call" | custom-call | flops 1409286144 | bytes 4587520 | tf_op jit(solution)/shard_map/pallas_call | solution.py:108
  (49 shorter events, 0.2 us)
Async XLA Ops:
  7.2 1.0 copy-start
  7.2 149.6 %all-gather.2.cloned.1.call-start = ((), (), s32[]{:S(2)}) async-start(), calls=%async_computation.2 | async-start | bytes 8519680 | tf_op jit(solution)/shard_map/all_gather | solution.py:430
  8.1 6.9 %collective-permute-start.2 = (bf16[1,112,576]{2,1,0:T(8,128)(2,1)S(1)}, bf16[1,112,576]{2,1,0:T(8,128)(2,1)S(1)}, u32[]{:S(2)}, u32[]{:S(2)}) collective-permute-start(bf16[1,112,576]{2,1,0:T(8,128)(2,1)S(1)} %dynamic-slice_bitcast_fusion), channel_id=1, source_target_pairs={{0,96},{1,25},{8,104},{9,1},{16,112},{17,9},{24,120},{25,17},{32,0... | collective-permute-start | bytes 387080 | tf_op jit(solution)/shard_map/ppermute | solution.py:394
  8.7 6.4 %collective-permute-start.1 = (bf16[1,112,576]{2,1,0:T(8,128)(2,1)S(1)}, bf16[1,112,576]{2,1,0:T(8,128)(2,1)S(1)}, u32[]{:S(2)}, u32[]{:S(2)}) collective-permute-start(bf16[1,112,576]{2,1,0:T(8,128)(2,1)S(1)} %dynamic-slice_bitcast_fusion), channel_id=1, source_target_pairs={{0,64},{1,17},{8,72},{9,25},{16,80},{17,1},{24,88},{25,9},{32,96},... | collective-permute-start | bytes 387080 | tf_op jit(solution)/shard_map/ppermute | solution.py:394
  9.3 6.4 %collective-permute-start = (bf16[1,112,576]{2,1,0:T(8,128)(2,1)S(1)}, bf16[1,112,576]{2,1,0:T(8,128)(2,1)S(1)}, u32[]{:S(2)}, u32[]{:S(2)}) collective-permute-start(bf16[1,112,576]{2,1,0:T(8,128)(2,1)S(1)} %dynamic-slice_bitcast_fusion), channel_id=1, source_target_pairs={{0,32},{1,9},{8,40},{9,17},{16,48},{17,25},{24,56},{25,1},{32,64},... | collective-permute-start | bytes 387080 | tf_op jit(solution)/shard_map/ppermute | solution.py:394
  15.9 15.8 %collective-permute-start.3 = (bf16[4,112,576]{2,1,0:T(8,128)(2,1)S(1)}, bf16[4,112,576]{2,1,0:T(8,128)(2,1)S(1)}, u32[]{:S(2)}, u32[]{:S(2)}) collective-permute-start(bf16[4,112,576]{2,1,0:T(8,128)(2,1)S(1)} %pad_maximum_fusion.1), channel_id=1, source_target_pairs={{0,8},{1,33},{8,16},{9,41},{16,24},{17,49},{24,0},{25,57},{32,40},... | collective-permute-start | bytes 1548296 | tf_op jit(solution)/shard_map/ppermute | solution.py:394
  17.3 14.4 %collective-permute-start.4 = (bf16[4,112,576]{2,1,0:T(8,128)(2,1)S(1)}, bf16[4,112,576]{2,1,0:T(8,128)(2,1)S(1)}, u32[]{:S(2)}, u32[]{:S(2)}) collective-permute-start(bf16[4,112,576]{2,1,0:T(8,128)(2,1)S(1)} %pad_maximum_fusion.1), channel_id=1, source_target_pairs={{0,24},{1,97},{8,0},{9,105},{16,8},{17,113},{24,16},{25,121},{32,5... | collective-permute-start | bytes 1548296 | tf_op jit(solution)/shard_map/ppermute | solution.py:394
  17.4 14.3 %collective-permute-start.5 = (bf16[4,112,576]{2,1,0:T(8,128)(2,1)S(1)}, bf16[4,112,576]{2,1,0:T(8,128)(2,1)S(1)}, u32[]{:S(2)}, u32[]{:S(2)}) collective-permute-start(bf16[4,112,576]{2,1,0:T(8,128)(2,1)S(1)} %pad_maximum_fusion.1), channel_id=1, source_target_pairs={{0,16},{1,65},{8,24},{9,73},{16,0},{17,81},{24,8},{25,89},{32,48},... | collective-permute-start | bytes 1548296 | tf_op jit(solution)/shard_map/ppermute | solution.py:394
  19.2 1.2 copy-start.6
  20.4 0.7 copy-start.9
  21.1 0.7 copy-start.10
  24.4 1.8 copy-start.3
  26.2 11.0 %copy-start.11 = (f32[512,128]{1,0:T(8,128)}, f32[512,128]{1,0:T(8,128)S(1)}, u32[]{:S(2)}) copy-start(f32[512,128]{1,0:T(8,128)S(1)} %get-tuple-element.40.gate_ref) | copy-start | bytes 786436
  31.7 1.0 copy-start.21
  31.7 0.8 copy-start.19
  32.6 4.0 %copy-start.22 = (bf16[4,112,576]{2,1,0:T(8,128)(2,1)}, bf16[4,112,576]{2,1,0:T(8,128)(2,1)S(1)}, u32[]{:S(2)}) copy-start(bf16[4,112,576]{2,1,0:T(8,128)(2,1)S(1)} %collective-permute-done.5) | copy-start | bytes 1548292
  32.7 31.2 %collective-permute-start.10 = (bf16[1,3584,512]{2,1,0:T(8,128)(2,1)}, bf16[1,3584,512]{2,1,0:T(8,128)(2,1)}, u32[]{:S(2)}, u32[]{:S(2)}) collective-permute-start(bf16[1,3584,512]{2,1,0:T(8,128)(2,1)} %gate0), channel_id=1, source_target_pairs={{0,1},{1,0},{2,3},{3,2},{4,5},{5,4},{6,7},{7,6},{8,9},{9,8},{10,11... | collective-permute-start | bytes 11010056 | tf_op jit(solution)/shard_map/ppermute | solution.py:375
  36.5 58.1 %collective-permute-start.11 = (bf16[1,3584,512]{2,1,0:T(8,128)(2,1)}, bf16[1,3584,512]{2,1,0:T(8,128)(2,1)}, u32[]{:S(2)}, u32[]{:S(2)}) collective-permute-start(bf16[1,3584,512]{2,1,0:T(8,128)(2,1)} %up0), channel_id=1, source_target_pairs={{0,1},{1,0},{2,3},{3,2},{4,5},{5,4},{6,7},{7,6},{8,9},{9,8},{10,11... | collective-permute-start | bytes 11010056 | tf_op jit(solution)/shard_map/ppermute | solution.py:375
  37.2 57.4 %collective-permute-start.12 = (bf16[1,512,3584]{2,1,0:T(8,128)(2,1)}, bf16[1,512,3584]{2,1,0:T(8,128)(2,1)}, u32[]{:S(2)}, u32[]{:S(2)}) collective-permute-start(bf16[1,512,3584]{2,1,0:T(8,128)(2,1)} %down0), channel_id=1, source_target_pairs={{0,1},{1,0},{2,3},{3,2},{4,5},{5,4},{6,7},{7,6},{8,9},{9,8},{10,11... | collective-permute-start | bytes 11010056 | tf_op jit(solution)/shard_map/ppermute | solution.py:375
  37.2 57.4 %all-to-all-start = ((bf16[64,8,3584]{2,1,0:T(8,128)(2,1)}), bf16[64,8,3584]{2,1,0:T(8,128)(2,1)}, u32[]{:S(2)}, u32[]{:S(2)}) async-start(bf16[64,8,3584]{2,1,0:T(8,128)(2,1)} %bitcast.14), calls=%async_computation | async-start | bytes 7340032 | tf_op jit(solution)/shard_map/all_to_all | solution.py:407
  46.9 1.4 copy-start.23
  46.9 1.5 copy-start.20
  47.0 9.5 %copy-start.7 = (bf16[128,3584]{1,0:T(8,128)(2,1)S(1)}, bf16[128,3584]{1,0:T(8,128)(2,1)}, u32[]{:S(2)}) copy-start(bf16[128,3584]{1,0:T(8,128)(2,1)} %hidden_ref.3) | copy-start | bytes 2752516
  47.0 9.5 %copy-start.8 = (f32[512]{0:T(512)S(1)}, f32[512]{0:T(512)}, u32[]{:S(2)}) copy-start(f32[512]{0:T(512)} %param.12) | copy-start | bytes 6148
  48.5 8.0 %collective-permute-start.6 = (bf16[16,112,576]{2,1,0:T(8,128)(2,1)S(1)}, bf16[16,112,576]{2,1,0:T(8,128)(2,1)}, u32[]{:S(2)}, u32[]{:S(2)}) collective-permute-start(bf16[16,112,576]{2,1,0:T(8,128)(2,1)S(1)} %constant_dynamic-update-slice_fusion.mine_ref), channel_id=1, source_target_pairs={{0,1},{1,0},{2,3},{3,2},{4,5},{5,4},{6,7},{7,6},{8,9},{9,8},{10,11... | collective-permute-start | bytes 6193160 | tf_op jit(solution)/shard_map/ppermute | solution.py:375
  61.4 54.0 %copy-start.4 = (bf16[128,576]{1,0:T(8,128)(2,1)}, bf16[128,576]{1,0:T(8,128)(2,1)S(1)}, u32[]{:S(2)}) copy-start(bf16[128,576]{1,0:T(8,128)(2,1)S(1)} %shard_map.114) | copy-start | bytes 442372
  61.5 54.0 %collective-permute-start.7 = (bf16[128,576]{1,0:T(8,128)(2,1)S(1)}, bf16[128,576]{1,0:T(8,128)(2,1)S(1)}, u32[]{:S(2)}, u32[]{:S(2)}) collective-permute-start(bf16[128,576]{1,0:T(8,128)(2,1)S(1)} %shard_map.114), channel_id=1, source_target_pairs={{0,2},{2,4},{4,6},{6,0},{1,3},{3,5},{5,7},{7,1},{8,10},{10,12},{12... | collective-permute-start | bytes 442376 | tf_op jit(solution)/shard_map/ppermute | solution.py:380
  61.6 53.8 %collective-permute-start.8 = (bf16[128,576]{1,0:T(8,128)(2,1)S(1)}, bf16[128,576]{1,0:T(8,128)(2,1)S(1)}, u32[]{:S(2)}, u32[]{:S(2)}) collective-permute-start(bf16[128,576]{1,0:T(8,128)(2,1)S(1)} %shard_map.114), channel_id=1, source_target_pairs={{0,4},{2,6},{4,0},{6,2},{1,5},{3,7},{5,1},{7,3},{8,12},{10,14},{12... | collective-permute-start | bytes 442376 | tf_op jit(solution)/shard_map/ppermute | solution.py:380
  63.9 51.6 %collective-permute-start.9 = (bf16[128,576]{1,0:T(8,128)(2,1)S(1)}, bf16[128,576]{1,0:T(8,128)(2,1)}, u32[]{:S(2)}, u32[]{:S(2)}) collective-permute-start(bf16[128,576]{1,0:T(8,128)(2,1)S(1)} %shard_map.114), channel_id=1, source_target_pairs={{0,6},{2,0},{4,2},{6,4},{1,7},{3,1},{5,3},{7,5},{8,14},{10,8},{12,... | collective-permute-start | bytes 442376 | tf_op jit(solution)/shard_map/ppermute | solution.py:380
  115.4 0.7 copy-start.13
  115.4 0.7 copy-start.16
  116.2 11.4 %copy-start.2 = (bf16[128,12288]{1,0:T(8,128)(2,1)S(1)}, bf16[128,12288]{1,0:T(8,128)(2,1)}, u32[]{:S(2)}) copy-start(bf16[128,12288]{1,0:T(8,128)(2,1)} %mine_ref) | copy-start | bytes 9437188
  116.2 84.7 %all-to-all-start.1 = ((bf16[64,8,3584]{2,1,0:T(8,128)(2,1)}), bf16[64,8,3584]{2,1,0:T(8,128)(2,1)}, u32[]{:S(2)}, u32[]{:S(2)}) async-start(bf16[64,8,3584]{2,1,0:T(8,128)(2,1)} %bitcast.19), calls=%async_computation.1 | async-start | bytes 7340032 | tf_op jit(solution)/shard_map/all_to_all | solution.py:407
  127.6 4.3 %copy-start.5 = (bf16[128,576]{1,0:T(8,128)(2,1)S(1)}, bf16[128,576]{1,0:T(8,128)(2,1)}, u32[]{:S(2)}) copy-start(bf16[128,576]{1,0:T(8,128)(2,1)} %copy-done.4) | copy-start | bytes 442372
  127.6 4.3 %copy-start.14 = (bf16[128,576]{1,0:T(8,128)(2,1)S(1)}, bf16[128,576]{1,0:T(8,128)(2,1)}, u32[]{:S(2)}) copy-start(bf16[128,576]{1,0:T(8,128)(2,1)} %copy-done.13) | copy-start | bytes 442372
  127.6 4.3 %copy-start.17 = (bf16[128,576]{1,0:T(8,128)(2,1)S(1)}, bf16[128,576]{1,0:T(8,128)(2,1)}, u32[]{:S(2)}) copy-start(bf16[128,576]{1,0:T(8,128)(2,1)} %copy-done.16) | copy-start | bytes 442372
  129.9 4.1 %copy-start.15 = (bf16[128,576]{1,0:T(8,128)(2,1)S(1)}, bf16[128,576]{1,0:T(8,128)(2,1)}, u32[]{:S(2)}) copy-start(bf16[128,576]{1,0:T(8,128)(2,1)} %copy-done.13) | copy-start | bytes 442372
  129.9 4.1 %copy-start.18 = (bf16[128,576]{1,0:T(8,128)(2,1)S(1)}, bf16[128,576]{1,0:T(8,128)(2,1)}, u32[]{:S(2)}) copy-start(bf16[128,576]{1,0:T(8,128)(2,1)} %copy-done.16) | copy-start | bytes 442372
  129.9 9.6 %collective-permute-start.14 = (bf16[128,6144]{1,0:T(8,128)(2,1)}, bf16[128,6144]{1,0:T(8,128)(2,1)S(1)}, u32[]{:S(2)}, u32[]{:S(2)}) collective-permute-start(bf16[128,6144]{1,0:T(8,128)(2,1)} %shard_map.116), channel_id=1, source_target_pairs={{0,1},{1,0},{2,3},{3,2},{4,5},{5,4},{6,7},{7,6},{8,9},{9,8},{10,11... | collective-permute-start | bytes 4718600 | tf_op jit(solution)/shard_map/ppermute | solution.py:375
  133.9 2.3 %collective-permute-start.13 = (bf16[512,576]{0,1:T(8,128)(2,1)}, bf16[512,576]{0,1:T(8,128)(2,1)}, u32[]{:S(2)}, u32[]{:S(2)}) collective-permute-start(bf16[512,576]{0,1:T(8,128)(2,1)} %copy.16), channel_id=1, source_target_pairs={{0,1},{1,0},{2,3},{3,2},{4,5},{5,4},{6,7},{7,6},{8,9},{9,8},{10,11... | collective-permute-start | bytes 1769480 | tf_op jit(solution)/shard_map/ppermute | solution.py:375
  184.8 13.8 %collective-permute-start.15 = (bf16[128,4096]{1,0:T(8,128)(2,1)S(1)}, bf16[128,4096]{1,0:T(8,128)(2,1)S(1)}, u32[]{:S(2)}, u32[]{:S(2)}) collective-permute-start(bf16[128,4096]{1,0:T(8,128)(2,1)S(1)} %get-tuple-element.36), channel_id=1, source_target_pairs={{0,1},{1,0},{2,3},{3,2},{4,5},{5,4},{6,7},{7,6},{8,9},{9,8},{10,11... | collective-permute-start | bytes 3145736 | tf_op jit(solution)/shard_map/ppermute | solution.py:375
  198.7 2.2 %copy-start.12 = (f32[512,128]{1,0:T(8,128)S(1)}, f32[512,128]{1,0:T(8,128)}, u32[]{:S(2)}) copy-start(f32[512,128]{1,0:T(8,128)} %copy-done.11) | copy-start | bytes 786436
  200.8 4.3 %copy-start.1 = (bf16[224,576]{1,0:T(8,128)(2,1)S(1)}, bf16[224,576]{1,0:T(8,128)(2,1)}, u32[]{:S(2)}) copy-start(bf16[224,576]{1,0:T(8,128)(2,1)} %param.11) | copy-start | bytes 774148
Sparse Core Ops, SparseCore 0:
  10.9 145.8 all-gather.1

commit v5 on v4

--- a/solution.py
+++ b/solution.py
@@ -454,6 +454,7 @@
     pieces, results = lax.optimization_barrier((pieces, results))
     line = jnp.concatenate(pieces, axis=0)
     sequence = jnp.concatenate([line, swap(line)], axis=0)
+    sequence, results = lax.optimization_barrier((sequence, results))
     returned = exchange(results)
 
     whole, send = attend(where, sequence, kv_all, queries, other_queries)

time: 213 us -> 195 us (0.915)
  the two profiles are of different devices: /device:TPU:95 before, /device:TPU:0 now
where the time goes in v5:
time: 195 us
  waiting for transfers between devices  73.2 us (38%)
  Pallas kernels  64.2 us (33%)
  starting transfers between devices  32.5 us (17%)
  between operations  14.3 us (7%)
  local copies, waits for them, and re-layouts  10 us (5%)
    all_to_all x2, waiting for transfers between devices, exchange(): return lax.all_to_all(rows, CHIPS, split_axis=0, concat_axis=0, tiled=True)  42.2 us
    pallas_call x1, Pallas kernels, attend(): call(attention_kernel, vmem=48, cost=(flops // 4, 2 * (LAT * heads * KV +...  28.1 us
    pallas_call x1, Pallas kernels, experts(): call(functools.partial(expert_kernel, steps=steps), vmem=56, cost=(12 * c...  21.1 us
    ppermute x7, waiting for transfers between devices, swap(): return lax.ppermute(array, 'c', [(0, 1), (1, 0)])  16.2 us
    all_to_all x2, starting transfers between devices, exchange(): return lax.all_to_all(rows, CHIPS, split_axis=0, concat_axis=0, tiled=True)  14.7 us
    ppermute x6, waiting for transfers between devices, turn(): return lax.ppermute(array, ('z', 'y', 'c'), pairs)  14 us
    ppermute x6, starting transfers between devices, turn(): return lax.ppermute(array, ('z', 'y', 'c'), pairs)  10.7 us
    unnamed x41, local copies, waits for them, and re-layouts  9.27 us
  transfers between devices with their start and end apart: 19, of which 10 were waited for; matrix products, arithmetic and copies ran while one was open for 1% of the time, Pallas kernels for 31%

profile of v5, /device:TPU:0, one launch (start us, length us, event | category | flops | bytes accessed | tf_op | source)
XLA Modules:
  0.0 194.9 jit_solution(7715648227788702806)
XLA Ops:
  7.2 0.0 copy-start
  7.2 0.0 all-gather.2.cloned.1.call-start
  7.2 0.7 all-gather.2.cloned.1.call-update
  7.9 0.2 copy-done
  8.1 4.2 %collective-permute-start.2 = (bf16[1,112,576]{2,1,0:T(8,128)(2,1)S(1)}, bf16[1,112,576]{2,1,0:T(8,128)(2,1)S(1)}, u32[]{:S(2)}, u32[]{:S(2)}) collective-permute-start(bf16[1,112,576]{2,1,0:T(8,128)(2,1)S(1)} %dynamic-slice_bitcast_fusion), channel_id=1, source_target_pairs={{0,96},{1,25},{8,104},{9,1},{16,112},{17,9},{24,120},{25,17},{32,0... | collective-permute-start | bytes 387080 | tf_op jit(solution)/shard_map/ppermute | solution.py:394
  12.3 1.3 collective-permute-start
  13.6 2.9 %collective-permute-done.2 = bf16[1,112,576]{2,1,0:T(8,128)(2,1)S(1)} collective-permute-done((bf16[1,112,576]{2,1,0:T(8,128)(2,1)S(1)}, bf16[1,112,576]{2,1,0:T(8,128)(2,1)S(1)}, u32[]{:S(2)}, u32[]{:S(2)}) %collective-permute-start.2) | collective-permute-done | bytes 129056 | tf_op jit(solution)/shard_map/ppermute | solution.py:394
  16.5 2.5 %collective-permute-done.1 = bf16[1,112,576]{2,1,0:T(8,128)(2,1)S(1)} collective-permute-done((bf16[1,112,576]{2,1,0:T(8,128)(2,1)S(1)}, bf16[1,112,576]{2,1,0:T(8,128)(2,1)S(1)}, u32[]{:S(2)}, u32[]{:S(2)}) %collective-permute-start.1) | collective-permute-done | bytes 129056 | tf_op jit(solution)/shard_map/ppermute | solution.py:394
  19.0 1.1 collective-permute-done
  20.2 0.1 pad_maximum_fusion.1
  20.3 1.6 collective-permute-start.3
  21.9 1.7 collective-permute-start.4
  23.6 2.0 %collective-permute-start.5 = (bf16[4,112,576]{2,1,0:T(8,128)(2,1)S(1)}, bf16[4,112,576]{2,1,0:T(8,128)(2,1)S(1)}, u32[]{:S(2)}, u32[]{:S(2)}) collective-permute-start(bf16[4,112,576]{2,1,0:T(8,128)(2,1)S(1)} %pad_maximum_fusion.1), channel_id=1, source_target_pairs={{0,16},{1,65},{8,24},{9,73},{16,0},{17,81},{24,8},{25,89},{32,48},... | collective-permute-start | bytes 1548296 | tf_op jit(solution)/shard_map/ppermute | solution.py:394
  25.6 1.2 copy-done.6
  26.8 0.7 copy-done.9
  27.5 0.7 copy-done.10
  28.1 2.7 %shard_map.113 = (bf16[512,3584]{1,0:T(8,128)(2,1)S(1)}, f32[512,128]{1,0:T(8,128)S(1)}) custom-call(s32[8,128]{1,0:T(8,128)S(1)} %bitcast.16, f32[8,128]{1,0:T(8,128)S(1)} %bitcast.17, bf16[128,3584]{1,0:T(8,128)(2,1)S(1)} %copy-done.6), custom_call_target="tpu_custom_call" | custom-call | flops 469762048 | bytes 4587520 | tf_op jit(solution)/shard_map/pallas_call | solution.py:68
  30.8 1.8 copy-done.3
  32.6 0.0 collective-permute-done.3
  32.6 0.0 collective-permute-done.4
  32.6 0.0 copy-start.13
  32.6 7.5 %collective-permute-done.5 = bf16[4,112,576]{2,1,0:T(8,128)(2,1)S(1)} collective-permute-done((bf16[4,112,576]{2,1,0:T(8,128)(2,1)S(1)}, bf16[4,112,576]{2,1,0:T(8,128)(2,1)S(1)}, u32[]{:S(2)}, u32[]{:S(2)}) %collective-permute-start.5) | collective-permute-done | bytes 516128 | tf_op jit(solution)/shard_map/ppermute | solution.py:394
  40.1 0.8 copy-done.15
  40.9 0.5 collective-permute-start.11
  41.4 0.0 collective-permute-start.12
  41.4 7.1 %all-to-all-start = ((bf16[64,8,3584]{2,1,0:T(8,128)(2,1)}), bf16[64,8,3584]{2,1,0:T(8,128)(2,1)}, u32[]{:S(2)}, u32[]{:S(2)}) async-start(bf16[64,8,3584]{2,1,0:T(8,128)(2,1)} %bitcast.14), calls=%async_computation | async-start | bytes 7340032 | tf_op jit(solution)/shard_map/all_to_all | solution.py:407
  48.5 0.0 copy-start.16
  48.5 0.0 copy-start.14
  48.5 0.1 constant_dynamic-update-slice_fusion.3
  48.6 0.0 copy-start.7
  48.6 0.0 copy-start.8
  48.6 1.3 constant_dynamic-update-slice_fusion.2
  49.9 0.1 constant_dynamic-update-slice_fusion.1
  50.0 0.1 constant_dynamic-update-slice_fusion.mine_ref
  50.1 0.3 collective-permute-start.6
  50.4 0.1 pad_add_fusion.where_ref
  50.5 0.3 fusion
  50.8 0.1 pad_maximum_fusion.2
  50.9 8.4 %collective-permute-done.6.other_ref = bf16[16,112,576]{2,1,0:T(8,128)(2,1)} collective-permute-done((bf16[16,112,576]{2,1,0:T(8,128)(2,1)S(1)}, bf16[16,112,576]{2,1,0:T(8,128)(2,1)}, u32[]{:S(2)}, u32[]{:S(2)}) %collective-permute-start.6) | collective-permute-done | bytes 2064416 | tf_op jit(solution)/shard_map/ppermute | solution.py:375
  59.3 5.0 %shard_map.114 = bf16[128,576]{1,0:T(8,128)(2,1)S(1)} custom-call(s32[4]{0:T(128)S(1)} %pad_add_fusion.where_ref, bf16[128,3584]{1,0:T(8,128)(2,1)S(1)} %copy-done.7, bf16[16,112,576]{2,1,0:T(8,128)(2,1)S(1)} %constant_dynamic-update-slice_fusion.mine_ref, bf16[16,112,576]{2,1,0:T(8,128)(2,1)} %collective-permute-done.6.other_ref, f32[1,512]{1,0:T(1,128)S(1)} %bitcast.15, ...), custom_call_target="tpu_custom_call" | custom-call | flops 528482304 | bytes 4128768 | tf_op jit(solution)/shard_map/pallas_call | solution.py:337
  64.3 1.6 collective-permute-start.7
  65.8 2.7 %collective-permute-start.8 = (bf16[128,576]{1,0:T(8,128)(2,1)S(1)}, bf16[128,576]{1,0:T(8,128)(2,1)S(1)}, u32[]{:S(2)}, u32[]{:S(2)}) collective-permute-start(bf16[128,576]{1,0:T(8,128)(2,1)S(1)} %shard_map.114), channel_id=1, source_target_pairs={{0,4},{2,6},{4,0},{6,2},{1,5},{3,7},{5,1},{7,3},{8,12},{10,14},{12... | collective-permute-start | bytes 442376 | tf_op jit(solution)/shard_map/ppermute | solution.py:380
  68.6 1.4 collective-permute-start.9
  70.0 32.6 %all-to-all-done = bf16[64,8,3584]{2,1,0:T(8,128)(2,1)} async-done(((bf16[64,8,3584]{2,1,0:T(8,128)(2,1)}), bf16[64,8,3584]{2,1,0:T(8,128)(2,1)}, u32[]{:S(2)}, u32[]{:S(2)}) %all-to-all-start) | async-done | bytes 3670048 | tf_op jit(solution)/shard_map/all_to_all | solution.py:407
  102.7 21.1 %shard_map.115 = bf16[512,3584]{1,0:T(8,128)(2,1)} custom-call(bf16[512,3584]{1,0:T(8,128)(2,1)} %bitcast.9.rows_ref, bf16[1,3584,512]{2,1,0:T(8,128)(2,1)} %gate0, bf16[1,3584,512]{2,1,0:T(8,128)(2,1)} %up0, bf16[1,512,3584]{2,1,0:T(8,128)(2,1)} %down0, bf16[1,3584,512]{2,1,0:T(8,128)(2,1)} %collective-permute-done.10.gate1, ...), custom_call_target="tpu_custom_call" | custom-call | flops 11274289152 | bytes 29360128 | tf_op jit(solution)/shard_map/pallas_call | solution.py:174
  123.8 0.1 pad_maximum_fusion
  123.8 0.3 copy.16
  124.1 0.1 collective-permute-start.13
  124.3 1.9 collective-permute-done.13
  126.2 0.3 copy.17
  126.5 0.1 constant_dynamic-update-slice_fusion.4.latent_ref
  126.6 0.0 copy-start.4
  126.6 1.0 copy-done.4
  127.6 7.6 %all-to-all-start.1 = ((bf16[64,8,3584]{2,1,0:T(8,128)(2,1)}), bf16[64,8,3584]{2,1,0:T(8,128)(2,1)}, u32[]{:S(2)}, u32[]{:S(2)}) async-start(bf16[64,8,3584]{2,1,0:T(8,128)(2,1)} %bitcast.19), calls=%async_computation.1 | async-start | bytes 7340032 | tf_op jit(solution)/shard_map/all_to_all | solution.py:407
  135.3 1.0 shard_map.116
  136.3 0.3 collective-permute-start.14
  136.6 3.4 %collective-permute-done.14.other_ref = bf16[128,6144]{1,0:T(8,128)(2,1)S(1)} collective-permute-done((bf16[128,6144]{1,0:T(8,128)(2,1)S(1)}, bf16[128,6144]{1,0:T(8,128)(2,1)S(1)}, u32[]{:S(2)}, u32[]{:S(2)}) %collective-permute-start.14) | collective-permute-done | bytes 1572896 | tf_op jit(solution)/shard_map/ppermute | solution.py:375
  140.0 1.3 copy-done.5
  141.3 28.1 %shard_map.117 = (bf16[128,8192]{1,0:T(8,128)(2,1)}, bf16[128,4096]{1,0:T(8,128)(2,1)S(1)}) custom-call(s32[4]{0:T(128)S(1)} %pad_add_fusion.where_ref, bf16[1024,576]{1,0:T(8,128)(2,1)S(1)} %copy-done.5, bf16[16,4,32,2048]{3,2,1,0:T(8,128)(2,1)} %bitcast.18, bf16[128,12288]{1,0:T(8,128)(2,1)} %mine_ref, bf16[128,6144]{1,0:T(8,128)(2,1)S(1)} %collective-permute-done.14.other_ref), custom_call_target="tpu_custom_call" | custom-call | flops 3489660928 | bytes 14680064 | tf_op jit(solution)/shard_map/pallas_call | solution.py:259
  169.4 0.1 collective-permute-start.15
  169.5 2.5 %collective-permute-done.15.part_ref = bf16[128,4096]{1,0:T(8,128)(2,1)S(1)} collective-permute-done((bf16[128,4096]{1,0:T(8,128)(2,1)S(1)}, bf16[128,4096]{1,0:T(8,128)(2,1)S(1)}, u32[]{:S(2)}, u32[]{:S(2)}) %collective-permute-start.15) | collective-permute-done | bytes 1048608 | tf_op jit(solution)/shard_map/ppermute | solution.py:375
  172.1 2.2 %shard_map.118 = bf16[128,8192]{1,0:T(8,128)(2,1)} custom-call(s32[4]{0:T(128)S(1)} %pad_add_fusion.where_ref, bf16[128,4096]{1,0:T(8,128)(2,1)S(1)} %collective-permute-done.15.part_ref, bf16[128,8192]{1,0:T(8,128)(2,1)} %get-tuple-element.41.whole_ref), custom_call_target="tpu_custom_call", output_to_operand_aliasing={{}: (2, {})} | custom-call | bytes 2097152 | tf_op jit(solution)/shard_map/pallas_call | solution.py:287
  174.2 9.6 %all-to-all-done.1 = bf16[64,8,3584]{2,1,0:T(8,128)(2,1)} async-done(((bf16[64,8,3584]{2,1,0:T(8,128)(2,1)}), bf16[64,8,3584]{2,1,0:T(8,128)(2,1)}, u32[]{:S(2)}, u32[]{:S(2)}) %all-to-all-start.1) | async-done | bytes 3670048 | tf_op jit(solution)/shard_map/all_to_all | solution.py:407
  183.8 4.2 %shard_map.119 = bf16[128,3584]{1,0:T(8,128)(2,1)} custom-call(f32[512,128]{1,0:T(8,128)S(1)} %copy-done.12, bf16[512,3584]{1,0:T(8,128)(2,1)} %bitcast.12.rows_ref), custom_call_target="tpu_custom_call" | custom-call | flops 1409286144 | bytes 4587520 | tf_op jit(solution)/shard_map/pallas_call | solution.py:108
  (35 shorter events, 0.2 us)
Async XLA Ops:
  7.2 1.0 copy-start
  7.2 132.8 %all-gather.2.cloned.1.call-start = ((), (), s32[]{:S(2)}) async-start(), calls=%async_computation.2 | async-start | bytes 8519680 | tf_op jit(solution)/shard_map/all_gather | solution.py:430
  8.1 8.4 %collective-permute-start.2 = (bf16[1,112,576]{2,1,0:T(8,128)(2,1)S(1)}, bf16[1,112,576]{2,1,0:T(8,128)(2,1)S(1)}, u32[]{:S(2)}, u32[]{:S(2)}) collective-permute-start(bf16[1,112,576]{2,1,0:T(8,128)(2,1)S(1)} %dynamic-slice_bitcast_fusion), channel_id=1, source_target_pairs={{0,96},{1,25},{8,104},{9,1},{16,112},{17,9},{24,120},{25,17},{32,0... | collective-permute-start | bytes 387080 | tf_op jit(solution)/shard_map/ppermute | solution.py:394
  12.3 6.7 %collective-permute-start.1 = (bf16[1,112,576]{2,1,0:T(8,128)(2,1)S(1)}, bf16[1,112,576]{2,1,0:T(8,128)(2,1)S(1)}, u32[]{:S(2)}, u32[]{:S(2)}) collective-permute-start(bf16[1,112,576]{2,1,0:T(8,128)(2,1)S(1)} %dynamic-slice_bitcast_fusion), channel_id=1, source_target_pairs={{0,64},{1,17},{8,72},{9,25},{16,80},{17,1},{24,88},{25,9},{32,96},... | collective-permute-start | bytes 387080 | tf_op jit(solution)/shard_map/ppermute | solution.py:394
  12.3 7.8 %collective-permute-start = (bf16[1,112,576]{2,1,0:T(8,128)(2,1)S(1)}, bf16[1,112,576]{2,1,0:T(8,128)(2,1)S(1)}, u32[]{:S(2)}, u32[]{:S(2)}) collective-permute-start(bf16[1,112,576]{2,1,0:T(8,128)(2,1)S(1)} %dynamic-slice_bitcast_fusion), channel_id=1, source_target_pairs={{0,32},{1,9},{8,40},{9,17},{16,48},{17,25},{24,56},{25,1},{32,64},... | collective-permute-start | bytes 387080 | tf_op jit(solution)/shard_map/ppermute | solution.py:394
  20.3 12.3 %collective-permute-start.3 = (bf16[4,112,576]{2,1,0:T(8,128)(2,1)S(1)}, bf16[4,112,576]{2,1,0:T(8,128)(2,1)}, u32[]{:S(2)}, u32[]{:S(2)}) collective-permute-start(bf16[4,112,576]{2,1,0:T(8,128)(2,1)S(1)} %pad_maximum_fusion.1), channel_id=1, source_target_pairs={{0,8},{1,33},{8,16},{9,41},{16,24},{17,49},{24,0},{25,57},{32,40},... | collective-permute-start | bytes 1548296 | tf_op jit(solution)/shard_map/ppermute | solution.py:394
  21.9 10.7 %collective-permute-start.4 = (bf16[4,112,576]{2,1,0:T(8,128)(2,1)S(1)}, bf16[4,112,576]{2,1,0:T(8,128)(2,1)S(1)}, u32[]{:S(2)}, u32[]{:S(2)}) collective-permute-start(bf16[4,112,576]{2,1,0:T(8,128)(2,1)S(1)} %pad_maximum_fusion.1), channel_id=1, source_target_pairs={{0,24},{1,97},{8,0},{9,105},{16,8},{17,113},{24,16},{25,121},{32,5... | collective-permute-start | bytes 1548296 | tf_op jit(solution)/shard_map/ppermute | solution.py:394
  23.6 16.5 %collective-permute-start.5 = (bf16[4,112,576]{2,1,0:T(8,128)(2,1)S(1)}, bf16[4,112,576]{2,1,0:T(8,128)(2,1)S(1)}, u32[]{:S(2)}, u32[]{:S(2)}) collective-permute-start(bf16[4,112,576]{2,1,0:T(8,128)(2,1)S(1)} %pad_maximum_fusion.1), channel_id=1, source_target_pairs={{0,16},{1,65},{8,24},{9,73},{16,0},{17,81},{24,8},{25,89},{32,48},... | collective-permute-start | bytes 1548296 | tf_op jit(solution)/shard_map/ppermute | solution.py:394
  25.6 1.2 copy-start.6
  26.8 0.7 copy-start.9
  27.5 0.7 copy-start.10
  30.8 1.8 copy-start.3
  32.6 8.8 %copy-start.11 = (f32[512,128]{1,0:T(8,128)}, f32[512,128]{1,0:T(8,128)S(1)}, u32[]{:S(2)}) copy-start(f32[512,128]{1,0:T(8,128)S(1)} %get-tuple-element.44.gate_ref) | copy-start | bytes 786436
  32.6 7.5 %copy-start.13 = (bf16[4,112,576]{2,1,0:T(8,128)(2,1)}, bf16[4,112,576]{2,1,0:T(8,128)(2,1)S(1)}, u32[]{:S(2)}) copy-start(bf16[4,112,576]{2,1,0:T(8,128)(2,1)S(1)} %collective-permute-done.4) | copy-start | bytes 1548292
  40.1 0.8 copy-start.15
  40.9 27.7 %collective-permute-start.10 = (bf16[1,3584,512]{2,1,0:T(8,128)(2,1)}, bf16[1,3584,512]{2,1,0:T(8,128)(2,1)}, u32[]{:S(2)}, u32[]{:S(2)}) collective-permute-start(bf16[1,3584,512]{2,1,0:T(8,128)(2,1)} %gate0), channel_id=1, source_target_pairs={{0,1},{1,0},{2,3},{3,2},{4,5},{5,4},{6,7},{7,6},{8,9},{9,8},{10,11... | collective-permute-start | bytes 11010056 | tf_op jit(solution)/shard_map/ppermute | solution.py:375
  40.9 61.7 %collective-permute-start.11 = (bf16[1,3584,512]{2,1,0:T(8,128)(2,1)}, bf16[1,3584,512]{2,1,0:T(8,128)(2,1)}, u32[]{:S(2)}, u32[]{:S(2)}) collective-permute-start(bf16[1,3584,512]{2,1,0:T(8,128)(2,1)} %up0), channel_id=1, source_target_pairs={{0,1},{1,0},{2,3},{3,2},{4,5},{5,4},{6,7},{7,6},{8,9},{9,8},{10,11... | collective-permute-start | bytes 11010056 | tf_op jit(solution)/shard_map/ppermute | solution.py:375
  41.4 61.2 %collective-permute-start.12 = (bf16[1,512,3584]{2,1,0:T(8,128)(2,1)}, bf16[1,512,3584]{2,1,0:T(8,128)(2,1)}, u32[]{:S(2)}, u32[]{:S(2)}) collective-permute-start(bf16[1,512,3584]{2,1,0:T(8,128)(2,1)} %down0), channel_id=1, source_target_pairs={{0,1},{1,0},{2,3},{3,2},{4,5},{5,4},{6,7},{7,6},{8,9},{9,8},{10,11... | collective-permute-start | bytes 11010056 | tf_op jit(solution)/shard_map/ppermute | solution.py:375
  41.4 61.2 %all-to-all-start = ((bf16[64,8,3584]{2,1,0:T(8,128)(2,1)}), bf16[64,8,3584]{2,1,0:T(8,128)(2,1)}, u32[]{:S(2)}, u32[]{:S(2)}) async-start(bf16[64,8,3584]{2,1,0:T(8,128)(2,1)} %bitcast.14), calls=%async_computation | async-start | bytes 7340032 | tf_op jit(solution)/shard_map/all_to_all | solution.py:407
  48.5 1.4 copy-start.16
  48.5 1.5 copy-start.14
  48.6 10.7 %copy-start.7 = (bf16[128,3584]{1,0:T(8,128)(2,1)S(1)}, bf16[128,3584]{1,0:T(8,128)(2,1)}, u32[]{:S(2)}) copy-start(bf16[128,3584]{1,0:T(8,128)(2,1)} %hidden_ref.3) | copy-start | bytes 2752516
  48.6 10.7 %copy-start.8 = (f32[512]{0:T(512)S(1)}, f32[512]{0:T(512)}, u32[]{:S(2)}) copy-start(f32[512]{0:T(512)} %param.12) | copy-start | bytes 6148
  50.1 9.2 %collective-permute-start.6 = (bf16[16,112,576]{2,1,0:T(8,128)(2,1)S(1)}, bf16[16,112,576]{2,1,0:T(8,128)(2,1)}, u32[]{:S(2)}, u32[]{:S(2)}) collective-permute-start(bf16[16,112,576]{2,1,0:T(8,128)(2,1)S(1)} %constant_dynamic-update-slice_fusion.mine_ref), channel_id=1, source_target_pairs={{0,1},{1,0},{2,3},{3,2},{4,5},{5,4},{6,7},{7,6},{8,9},{9,8},{10,11... | collective-permute-start | bytes 6193160 | tf_op jit(solution)/shard_map/ppermute | solution.py:375
  64.3 59.5 %collective-permute-start.7 = (bf16[128,576]{1,0:T(8,128)(2,1)S(1)}, bf16[128,576]{1,0:T(8,128)(2,1)S(1)}, u32[]{:S(2)}, u32[]{:S(2)}) collective-permute-start(bf16[128,576]{1,0:T(8,128)(2,1)S(1)} %shard_map.114), channel_id=1, source_target_pairs={{0,2},{2,4},{4,6},{6,0},{1,3},{3,5},{5,7},{7,1},{8,10},{10,12},{12... | collective-permute-start | bytes 442376 | tf_op jit(solution)/shard_map/ppermute | solution.py:380
  65.8 57.9 %collective-permute-start.8 = (bf16[128,576]{1,0:T(8,128)(2,1)S(1)}, bf16[128,576]{1,0:T(8,128)(2,1)S(1)}, u32[]{:S(2)}, u32[]{:S(2)}) collective-permute-start(bf16[128,576]{1,0:T(8,128)(2,1)S(1)} %shard_map.114), channel_id=1, source_target_pairs={{0,4},{2,6},{4,0},{6,2},{1,5},{3,7},{5,1},{7,3},{8,12},{10,14},{12... | collective-permute-start | bytes 442376 | tf_op jit(solution)/shard_map/ppermute | solution.py:380
  68.6 55.2 %collective-permute-start.9 = (bf16[128,576]{1,0:T(8,128)(2,1)S(1)}, bf16[128,576]{1,0:T(8,128)(2,1)S(1)}, u32[]{:S(2)}, u32[]{:S(2)}) collective-permute-start(bf16[128,576]{1,0:T(8,128)(2,1)S(1)} %shard_map.114), channel_id=1, source_target_pairs={{0,6},{2,0},{4,2},{6,4},{1,7},{3,1},{5,3},{7,5},{8,14},{10,8},{12,... | collective-permute-start | bytes 442376 | tf_op jit(solution)/shard_map/ppermute | solution.py:380
  124.1 2.1 %collective-permute-start.13 = (bf16[512,576]{0,1:T(8,128)(2,1)S(1)}, bf16[512,576]{0,1:T(8,128)(2,1)S(1)}, u32[]{:S(2)}, u32[]{:S(2)}) collective-permute-start(bf16[512,576]{0,1:T(8,128)(2,1)S(1)} %copy.16), channel_id=1, source_target_pairs={{0,1},{1,0},{2,3},{3,2},{4,5},{5,4},{6,7},{7,6},{8,9},{9,8},{10,11... | collective-permute-start | bytes 1769480 | tf_op jit(solution)/shard_map/ppermute | solution.py:375
  126.6 1.1 copy-start.4
  127.6 7.7 %copy-start.2 = (bf16[128,12288]{1,0:T(8,128)(2,1)S(1)}, bf16[128,12288]{1,0:T(8,128)(2,1)}, u32[]{:S(2)}) copy-start(bf16[128,12288]{1,0:T(8,128)(2,1)} %mine_ref) | copy-start | bytes 9437188
  127.6 56.2 %all-to-all-start.1 = ((bf16[64,8,3584]{2,1,0:T(8,128)(2,1)}), bf16[64,8,3584]{2,1,0:T(8,128)(2,1)}, u32[]{:S(2)}, u32[]{:S(2)}) async-start(bf16[64,8,3584]{2,1,0:T(8,128)(2,1)} %bitcast.19), calls=%async_computation.1 | async-start | bytes 7340032 | tf_op jit(solution)/shard_map/all_to_all | solution.py:407
  136.3 3.7 %collective-permute-start.14 = (bf16[128,6144]{1,0:T(8,128)(2,1)S(1)}, bf16[128,6144]{1,0:T(8,128)(2,1)S(1)}, u32[]{:S(2)}, u32[]{:S(2)}) collective-permute-start(bf16[128,6144]{1,0:T(8,128)(2,1)S(1)} %shard_map.116), channel_id=1, source_target_pairs={{0,1},{1,0},{2,3},{3,2},{4,5},{5,4},{6,7},{7,6},{8,9},{9,8},{10,11... | collective-permute-start | bytes 4718600 | tf_op jit(solution)/shard_map/ppermute | solution.py:375
  140.0 1.3 copy-start.5
  169.4 2.7 %collective-permute-start.15 = (bf16[128,4096]{1,0:T(8,128)(2,1)S(1)}, bf16[128,4096]{1,0:T(8,128)(2,1)S(1)}, u32[]{:S(2)}, u32[]{:S(2)}) collective-permute-start(bf16[128,4096]{1,0:T(8,128)(2,1)S(1)} %get-tuple-element.40), channel_id=1, source_target_pairs={{0,1},{1,0},{2,3},{3,2},{4,5},{5,4},{6,7},{7,6},{8,9},{9,8},{10,11... | collective-permute-start | bytes 3145736 | tf_op jit(solution)/shard_map/ppermute | solution.py:375
  172.1 11.8 %copy-start.12 = (f32[512,128]{1,0:T(8,128)S(1)}, f32[512,128]{1,0:T(8,128)}, u32[]{:S(2)}) copy-start(f32[512,128]{1,0:T(8,128)} %copy-done.11) | copy-start | bytes 786436
  183.8 4.2 %copy-start.1 = (bf16[224,576]{1,0:T(8,128)(2,1)S(1)}, bf16[224,576]{1,0:T(8,128)(2,1)}, u32[]{:S(2)}) copy-start(bf16[224,576]{1,0:T(8,128)(2,1)} %param.11) | copy-start | bytes 774148
Sparse Core Ops, SparseCore 0:
  10.9 124.0 all-gather.1

commit v6 on v5

--- a/solution.py
+++ b/solution.py
@@ -57,7 +57,11 @@
         )
         kept = (named > 0.5) & (earlier.astype(jnp.int32) == row % CAP)
         pick[...] = jnp.where(kept, 1.0, 0.0).astype(BF16)
-        gate_ref[...] = jnp.where(kept, weight, 0.0)
+        rest = jnp.where(kept, weight, 0.0).T
+        for term in range(3):
+            part = rest.astype(BF16)
+            gate_ref[term * tokens : (term + 1) * tokens, :] = part
+            rest = rest - part.astype(F32)
 
     rows_ref[...] = jnp.dot(pick[...], hidden_ref[...], preferred_element_type=F32).astype(BF16)
 
@@ -76,46 +80,37 @@
         ],
         out_specs=[
             pl.BlockSpec((slots, block), lambda j: (0, j)),
-            pl.BlockSpec((slots, tokens), lambda j: (0, 0)),
+            pl.BlockSpec((3 * tokens, slots), lambda j: (0, 0)),
         ],
         out_shape=[
             jax.ShapeDtypeStruct((slots, width), BF16),
-            jax.ShapeDtypeStruct((slots, tokens), F32),
+            jax.ShapeDtypeStruct((3 * tokens, slots), BF16),
         ],
         scratch_shapes=[pltpu.VMEM((slots, tokens), BF16)],
     )(ids, weights, hidden)
 
 
-def combine_kernel(gate_ref, rows_ref, out_ref, terms):
+def combine_kernel(gate_ref, rows_ref, out_ref):
     tokens = out_ref.shape[0]
-
-    @pl.when(pl.program_id(0) == 0)
-    def _():
-        rest = gate_ref[...].T
-        for term in range(3):
-            part = rest.astype(BF16)
-            terms[term * tokens : (term + 1) * tokens, :] = part
-            rest = rest - part.astype(F32)
-
-    total = jnp.dot(terms[...], rows_ref[...], preferred_element_type=F32)
+    total = jnp.dot(gate_ref[...], rows_ref[...], preferred_element_type=F32)
     out_ref[...] = (total[:tokens] + total[tokens : 2 * tokens] + total[2 * tokens :]).astype(BF16)
 
 
 def combine(gate, rows):
-    slots, tokens = gate.shape
+    terms, slots = gate.shape
+    tokens = terms // 3
     width = rows.shape[1]
     block = 1792
     return call(
         combine_kernel,
-        cost=(6 * slots * tokens * width, 2 * (slots + tokens) * width),
+        cost=(2 * slots * terms * width, 2 * (slots + tokens) * width),
         grid=(width // block,),
         in_specs=[
-            pl.BlockSpec((slots, tokens), lambda j: (0, 0)),
+            pl.BlockSpec((terms, slots), lambda j: (0, 0)),
             pl.BlockSpec((slots, block), lambda j: (0, j)),
         ],
         out_specs=pl.BlockSpec((tokens, block), lambda j: (0, j)),
         out_shape=jax.ShapeDtypeStruct((tokens, width), BF16),
-        scratch_shapes=[pltpu.VMEM((3 * tokens, slots), BF16)],
     )(gate, rows)
 
 

time: 195 us -> 195 us (level)
  no operation moved by 1% of the time
where the time goes in v6:
time: 195 us
  waiting for transfers between devices  72.2 us (37%)
  Pallas kernels  64.5 us (33%)
  starting transfers between devices  32.2 us (17%)
  between operations  14.3 us (7%)
  local copies, waits for them, and re-layouts  10.8 us (6%)
    all_to_all x2, waiting for transfers between devices, exchange(): return lax.all_to_all(rows, CHIPS, split_axis=0, concat_axis=0, tiled=True)  42.3 us
    pallas_call x1, Pallas kernels, attend(): call(attention_kernel, vmem=48, cost=(flops // 4, 2 * (LAT * heads * KV +...  28.1 us
    pallas_call x1, Pallas kernels, experts(): call(functools.partial(expert_kernel, steps=steps), vmem=56, cost=(12 * c...  21.4 us
    ppermute x7, waiting for transfers between devices, swap(): return lax.ppermute(array, 'c', [(0, 1), (1, 0)])  16.1 us
    all_to_all x2, starting transfers between devices, exchange(): return lax.all_to_all(rows, CHIPS, split_axis=0, concat_axis=0, tiled=True)  14.4 us
    ppermute x6, waiting for transfers between devices, turn(): return lax.ppermute(array, ('z', 'y', 'c'), pairs)  13.1 us
    ppermute x6, starting transfers between devices, turn(): return lax.ppermute(array, ('z', 'y', 'c'), pairs)  10.7 us
    unnamed x41, local copies, waits for them, and re-layouts  10 us
  transfers between devices with their start and end apart: 19, of which 10 were waited for; matrix products, arithmetic and copies ran while one was open for 1% of the time, Pallas kernels for 31%

profile of v6, /device:TPU:0, one launch (start us, length us, event | category | flops | bytes accessed | tf_op | source)
XLA Modules:
  0.0 194.7 jit_solution(3153945146975796012)
XLA Ops:
  7.2 0.0 copy-start
  7.2 0.0 all-gather.2.cloned.1.call-start
  7.2 0.7 all-gather.2.cloned.1.call-update
  7.9 0.2 copy-done
  8.1 4.2 %collective-permute-start.2 = (bf16[1,112,576]{2,1,0:T(8,128)(2,1)S(1)}, bf16[1,112,576]{2,1,0:T(8,128)(2,1)S(1)}, u32[]{:S(2)}, u32[]{:S(2)}) collective-permute-start(bf16[1,112,576]{2,1,0:T(8,128)(2,1)S(1)} %dynamic-slice_bitcast_fusion), channel_id=1, source_target_pairs={{0,96},{1,25},{8,104},{9,1},{16,112},{17,9},{24,120},{25,17},{32,0... | collective-permute-start | bytes 387080 | tf_op jit(solution)/shard_map/ppermute | solution.py:389
  12.3 1.3 collective-permute-start
  13.6 2.9 %collective-permute-done.2 = bf16[1,112,576]{2,1,0:T(8,128)(2,1)S(1)} collective-permute-done((bf16[1,112,576]{2,1,0:T(8,128)(2,1)S(1)}, bf16[1,112,576]{2,1,0:T(8,128)(2,1)S(1)}, u32[]{:S(2)}, u32[]{:S(2)}) %collective-permute-start.2) | collective-permute-done | bytes 129056 | tf_op jit(solution)/shard_map/ppermute | solution.py:389
  16.5 2.5 %collective-permute-done.1 = bf16[1,112,576]{2,1,0:T(8,128)(2,1)S(1)} collective-permute-done((bf16[1,112,576]{2,1,0:T(8,128)(2,1)S(1)}, bf16[1,112,576]{2,1,0:T(8,128)(2,1)S(1)}, u32[]{:S(2)}, u32[]{:S(2)}) %collective-permute-start.1) | collective-permute-done | bytes 129056 | tf_op jit(solution)/shard_map/ppermute | solution.py:389
  19.0 1.1 collective-permute-done
  20.2 0.1 pad_maximum_fusion.1
  20.3 1.6 collective-permute-start.3
  21.9 1.7 collective-permute-start.4
  23.6 2.0 %collective-permute-start.5 = (bf16[4,112,576]{2,1,0:T(8,128)(2,1)S(1)}, bf16[4,112,576]{2,1,0:T(8,128)(2,1)S(1)}, u32[]{:S(2)}, u32[]{:S(2)}) collective-permute-start(bf16[4,112,576]{2,1,0:T(8,128)(2,1)S(1)} %pad_maximum_fusion.1), channel_id=1, source_target_pairs={{0,16},{1,65},{8,24},{9,73},{16,0},{17,81},{24,8},{25,89},{32,48},... | collective-permute-start | bytes 1548296 | tf_op jit(solution)/shard_map/ppermute | solution.py:389
  25.6 1.2 copy-done.6
  26.8 0.7 copy-done.9
  27.5 0.7 copy-done.10
  28.1 2.8 %shard_map.113 = (bf16[512,3584]{1,0:T(8,128)(2,1)S(1)}, bf16[384,512]{1,0:T(8,128)(2,1)S(1)}) custom-call(s32[8,128]{1,0:T(8,128)S(1)} %bitcast.16, f32[8,128]{1,0:T(8,128)S(1)} %bitcast.17, bf16[128,3584]{1,0:T(8,128)(2,1)S(1)} %copy-done.6), custom_call_target="tpu_custom_call" | custom-call | flops 469762048 | bytes 4587520 | tf_op jit(solution)/shard_map/pallas_call | solution.py:72
  31.0 1.8 copy-done.3
  32.8 0.8 copy-done.11
  33.6 6.5 %collective-permute-done.5 = bf16[4,112,576]{2,1,0:T(8,128)(2,1)S(1)} collective-permute-done((bf16[4,112,576]{2,1,0:T(8,128)(2,1)S(1)}, bf16[4,112,576]{2,1,0:T(8,128)(2,1)S(1)}, u32[]{:S(2)}, u32[]{:S(2)}) %collective-permute-start.5) | collective-permute-done | bytes 516128 | tf_op jit(solution)/shard_map/ppermute | solution.py:389
  40.1 0.8 copy-done.15
  40.9 0.5 collective-permute-start.11
  41.4 0.0 collective-permute-start.12
  41.4 7.1 %all-to-all-start = ((bf16[64,8,3584]{2,1,0:T(8,128)(2,1)}), bf16[64,8,3584]{2,1,0:T(8,128)(2,1)}, u32[]{:S(2)}, u32[]{:S(2)}) async-start(bf16[64,8,3584]{2,1,0:T(8,128)(2,1)} %bitcast.14), calls=%async_computation | async-start | bytes 7340032 | tf_op jit(solution)/shard_map/all_to_all | solution.py:402
  48.5 0.0 copy-start.16
  48.5 0.0 copy-start.14
  48.5 0.1 constant_dynamic-update-slice_fusion.3
  48.6 0.0 copy-start.7
  48.6 0.0 copy-start.8
  48.6 1.3 constant_dynamic-update-slice_fusion.2
  49.9 0.1 constant_dynamic-update-slice_fusion.1
  50.0 0.1 constant_dynamic-update-slice_fusion.mine_ref
  50.1 0.3 collective-permute-start.6
  50.4 0.1 pad_add_fusion.where_ref
  50.5 0.3 fusion
  50.8 0.1 pad_maximum_fusion.2
  50.9 8.3 %collective-permute-done.6.other_ref = bf16[16,112,576]{2,1,0:T(8,128)(2,1)} collective-permute-done((bf16[16,112,576]{2,1,0:T(8,128)(2,1)S(1)}, bf16[16,112,576]{2,1,0:T(8,128)(2,1)}, u32[]{:S(2)}, u32[]{:S(2)}) %collective-permute-start.6) | collective-permute-done | bytes 2064416 | tf_op jit(solution)/shard_map/ppermute | solution.py:370
  59.2 5.0 %shard_map.114 = bf16[128,576]{1,0:T(8,128)(2,1)S(1)} custom-call(s32[4]{0:T(128)S(1)} %pad_add_fusion.where_ref, bf16[128,3584]{1,0:T(8,128)(2,1)S(1)} %copy-done.7, bf16[16,112,576]{2,1,0:T(8,128)(2,1)S(1)} %constant_dynamic-update-slice_fusion.mine_ref, bf16[16,112,576]{2,1,0:T(8,128)(2,1)} %collective-permute-done.6.other_ref, f32[1,512]{1,0:T(1,128)S(1)} %bitcast.15, ...), custom_call_target="tpu_custom_call" | custom-call | flops 528482304 | bytes 4128768 | tf_op jit(solution)/shard_map/pallas_call | solution.py:332
  64.2 1.6 collective-permute-start.7
  65.9 2.7 %collective-permute-start.8 = (bf16[128,576]{1,0:T(8,128)(2,1)S(1)}, bf16[128,576]{1,0:T(8,128)(2,1)S(1)}, u32[]{:S(2)}, u32[]{:S(2)}) collective-permute-start(bf16[128,576]{1,0:T(8,128)(2,1)S(1)} %shard_map.114), channel_id=1, source_target_pairs={{0,4},{2,6},{4,0},{6,2},{1,5},{3,7},{5,1},{7,3},{8,12},{10,14},{12... | collective-permute-start | bytes 442376 | tf_op jit(solution)/shard_map/ppermute | solution.py:375
  68.6 1.4 collective-permute-start.9
  70.0 32.7 %all-to-all-done = bf16[64,8,3584]{2,1,0:T(8,128)(2,1)} async-done(((bf16[64,8,3584]{2,1,0:T(8,128)(2,1)}), bf16[64,8,3584]{2,1,0:T(8,128)(2,1)}, u32[]{:S(2)}, u32[]{:S(2)}) %all-to-all-start) | async-done | bytes 3670048 | tf_op jit(solution)/shard_map/all_to_all | solution.py:402
  102.7 0.0 collective-permute-done.11.up1
  102.7 0.0 collective-permute-done.12.down1
  102.7 21.4 %shard_map.115 = bf16[512,3584]{1,0:T(8,128)(2,1)} custom-call(bf16[512,3584]{1,0:T(8,128)(2,1)} %bitcast.9.rows_ref, bf16[1,3584,512]{2,1,0:T(8,128)(2,1)} %gate0, bf16[1,3584,512]{2,1,0:T(8,128)(2,1)} %up0, bf16[1,512,3584]{2,1,0:T(8,128)(2,1)} %down0, bf16[1,3584,512]{2,1,0:T(8,128)(2,1)} %collective-permute-done.10.gate1, ...), custom_call_target="tpu_custom_call" | custom-call | flops 11274289152 | bytes 29360128 | tf_op jit(solution)/shard_map/pallas_call | solution.py:169
  124.1 0.1 pad_maximum_fusion
  124.2 0.3 copy.16
  124.5 0.1 collective-permute-start.13
  124.7 1.9 collective-permute-done.13
  126.5 0.3 copy.17
  126.8 0.1 constant_dynamic-update-slice_fusion.4.latent_ref
  126.9 0.0 copy-start.4
  127.0 1.0 copy-done.4
  128.0 7.3 %all-to-all-start.1 = ((bf16[64,8,3584]{2,1,0:T(8,128)(2,1)}), bf16[64,8,3584]{2,1,0:T(8,128)(2,1)}, u32[]{:S(2)}, u32[]{:S(2)}) async-start(bf16[64,8,3584]{2,1,0:T(8,128)(2,1)} %bitcast.19), calls=%async_computation.1 | async-start | bytes 7340032 | tf_op jit(solution)/shard_map/all_to_all | solution.py:402
  135.3 1.0 shard_map.116
  136.3 0.3 collective-permute-start.14
  136.6 3.4 %collective-permute-done.14.other_ref = bf16[128,6144]{1,0:T(8,128)(2,1)S(1)} collective-permute-done((bf16[128,6144]{1,0:T(8,128)(2,1)S(1)}, bf16[128,6144]{1,0:T(8,128)(2,1)S(1)}, u32[]{:S(2)}, u32[]{:S(2)}) %collective-permute-start.14) | collective-permute-done | bytes 1572896 | tf_op jit(solution)/shard_map/ppermute | solution.py:370
  140.0 1.3 copy-done.5
  141.3 28.1 %shard_map.117 = (bf16[128,8192]{1,0:T(8,128)(2,1)}, bf16[128,4096]{1,0:T(8,128)(2,1)S(1)}) custom-call(s32[4]{0:T(128)S(1)} %pad_add_fusion.where_ref, bf16[1024,576]{1,0:T(8,128)(2,1)S(1)} %copy-done.5, bf16[16,4,32,2048]{3,2,1,0:T(8,128)(2,1)} %bitcast.18, bf16[128,12288]{1,0:T(8,128)(2,1)} %mine_ref, bf16[128,6144]{1,0:T(8,128)(2,1)S(1)} %collective-permute-done.14.other_ref), custom_call_target="tpu_custom_call" | custom-call | flops 3489660928 | bytes 14680064 | tf_op jit(solution)/shard_map/pallas_call | solution.py:254
  169.4 0.1 collective-permute-start.15
  169.5 2.5 %collective-permute-done.15.part_ref = bf16[128,4096]{1,0:T(8,128)(2,1)S(1)} collective-permute-done((bf16[128,4096]{1,0:T(8,128)(2,1)S(1)}, bf16[128,4096]{1,0:T(8,128)(2,1)S(1)}, u32[]{:S(2)}, u32[]{:S(2)}) %collective-permute-start.15) | collective-permute-done | bytes 1048608 | tf_op jit(solution)/shard_map/ppermute | solution.py:370
  172.0 2.2 %shard_map.118 = bf16[128,8192]{1,0:T(8,128)(2,1)} custom-call(s32[4]{0:T(128)S(1)} %pad_add_fusion.where_ref, bf16[128,4096]{1,0:T(8,128)(2,1)S(1)} %collective-permute-done.15.part_ref, bf16[128,8192]{1,0:T(8,128)(2,1)} %get-tuple-element.41.whole_ref), custom_call_target="tpu_custom_call", output_to_operand_aliasing={{}: (2, {})} | custom-call | bytes 2097152 | tf_op jit(solution)/shard_map/pallas_call | solution.py:282
  174.2 9.6 %all-to-all-done.1 = bf16[64,8,3584]{2,1,0:T(8,128)(2,1)} async-done(((bf16[64,8,3584]{2,1,0:T(8,128)(2,1)}), bf16[64,8,3584]{2,1,0:T(8,128)(2,1)}, u32[]{:S(2)}, u32[]{:S(2)}) %all-to-all-start.1) | async-done | bytes 3670048 | tf_op jit(solution)/shard_map/all_to_all | solution.py:402
  183.8 4.1 %shard_map.119 = bf16[128,3584]{1,0:T(8,128)(2,1)} custom-call(bf16[384,512]{1,0:T(8,128)(2,1)S(1)} %copy-done.12, bf16[512,3584]{1,0:T(8,128)(2,1)} %bitcast.12.rows_ref), custom_call_target="tpu_custom_call" | custom-call | flops 1409286144 | bytes 4587520 | tf_op jit(solution)/shard_map/pallas_call | solution.py:104
  (35 shorter events, 0.2 us)
Async XLA Ops:
  7.2 1.0 copy-start
  7.2 132.8 %all-gather.2.cloned.1.call-start = ((), (), s32[]{:S(2)}) async-start(), calls=%async_computation.2 | async-start | bytes 8519680 | tf_op jit(solution)/shard_map/all_gather | solution.py:425
  8.1 8.4 %collective-permute-start.2 = (bf16[1,112,576]{2,1,0:T(8,128)(2,1)S(1)}, bf16[1,112,576]{2,1,0:T(8,128)(2,1)S(1)}, u32[]{:S(2)}, u32[]{:S(2)}) collective-permute-start(bf16[1,112,576]{2,1,0:T(8,128)(2,1)S(1)} %dynamic-slice_bitcast_fusion), channel_id=1, source_target_pairs={{0,96},{1,25},{8,104},{9,1},{16,112},{17,9},{24,120},{25,17},{32,0... | collective-permute-start | bytes 387080 | tf_op jit(solution)/shard_map/ppermute | solution.py:389
  12.3 6.7 %collective-permute-start.1 = (bf16[1,112,576]{2,1,0:T(8,128)(2,1)S(1)}, bf16[1,112,576]{2,1,0:T(8,128)(2,1)S(1)}, u32[]{:S(2)}, u32[]{:S(2)}) collective-permute-start(bf16[1,112,576]{2,1,0:T(8,128)(2,1)S(1)} %dynamic-slice_bitcast_fusion), channel_id=1, source_target_pairs={{0,64},{1,17},{8,72},{9,25},{16,80},{17,1},{24,88},{25,9},{32,96},... | collective-permute-start | bytes 387080 | tf_op jit(solution)/shard_map/ppermute | solution.py:389
  12.3 7.8 %collective-permute-start = (bf16[1,112,576]{2,1,0:T(8,128)(2,1)S(1)}, bf16[1,112,576]{2,1,0:T(8,128)(2,1)S(1)}, u32[]{:S(2)}, u32[]{:S(2)}) collective-permute-start(bf16[1,112,576]{2,1,0:T(8,128)(2,1)S(1)} %dynamic-slice_bitcast_fusion), channel_id=1, source_target_pairs={{0,32},{1,9},{8,40},{9,17},{16,48},{17,25},{24,56},{25,1},{32,64},... | collective-permute-start | bytes 387080 | tf_op jit(solution)/shard_map/ppermute | solution.py:389
  20.3 13.3 %collective-permute-start.3 = (bf16[4,112,576]{2,1,0:T(8,128)(2,1)S(1)}, bf16[4,112,576]{2,1,0:T(8,128)(2,1)}, u32[]{:S(2)}, u32[]{:S(2)}) collective-permute-start(bf16[4,112,576]{2,1,0:T(8,128)(2,1)S(1)} %pad_maximum_fusion.1), channel_id=1, source_target_pairs={{0,8},{1,33},{8,16},{9,41},{16,24},{17,49},{24,0},{25,57},{32,40},... | collective-permute-start | bytes 1548296 | tf_op jit(solution)/shard_map/ppermute | solution.py:389
  21.9 11.6 %collective-permute-start.4 = (bf16[4,112,576]{2,1,0:T(8,128)(2,1)S(1)}, bf16[4,112,576]{2,1,0:T(8,128)(2,1)S(1)}, u32[]{:S(2)}, u32[]{:S(2)}) collective-permute-start(bf16[4,112,576]{2,1,0:T(8,128)(2,1)S(1)} %pad_maximum_fusion.1), channel_id=1, source_target_pairs={{0,24},{1,97},{8,0},{9,105},{16,8},{17,113},{24,16},{25,121},{32,5... | collective-permute-start | bytes 1548296 | tf_op jit(solution)/shard_map/ppermute | solution.py:389
  23.6 16.4 %collective-permute-start.5 = (bf16[4,112,576]{2,1,0:T(8,128)(2,1)S(1)}, bf16[4,112,576]{2,1,0:T(8,128)(2,1)S(1)}, u32[]{:S(2)}, u32[]{:S(2)}) collective-permute-start(bf16[4,112,576]{2,1,0:T(8,128)(2,1)S(1)} %pad_maximum_fusion.1), channel_id=1, source_target_pairs={{0,16},{1,65},{8,24},{9,73},{16,0},{17,81},{24,8},{25,89},{32,48},... | collective-permute-start | bytes 1548296 | tf_op jit(solution)/shard_map/ppermute | solution.py:389
  25.6 1.2 copy-start.6
  26.8 0.7 copy-start.9
  27.5 0.7 copy-start.10
  31.0 1.8 copy-start.3
  32.8 0.8 copy-start.11
  33.6 6.5 %copy-start.13 = (bf16[4,112,576]{2,1,0:T(8,128)(2,1)}, bf16[4,112,576]{2,1,0:T(8,128)(2,1)S(1)}, u32[]{:S(2)}) copy-start(bf16[4,112,576]{2,1,0:T(8,128)(2,1)S(1)} %collective-permute-done.4) | copy-start | bytes 1548292
  40.1 0.8 copy-start.15
  40.9 27.7 %collective-permute-start.10 = (bf16[1,3584,512]{2,1,0:T(8,128)(2,1)}, bf16[1,3584,512]{2,1,0:T(8,128)(2,1)}, u32[]{:S(2)}, u32[]{:S(2)}) collective-permute-start(bf16[1,3584,512]{2,1,0:T(8,128)(2,1)} %gate0), channel_id=1, source_target_pairs={{0,1},{1,0},{2,3},{3,2},{4,5},{5,4},{6,7},{7,6},{8,9},{9,8},{10,11... | collective-permute-start | bytes 11010056 | tf_op jit(solution)/shard_map/ppermute | solution.py:370
  40.9 61.8 %collective-permute-start.11 = (bf16[1,3584,512]{2,1,0:T(8,128)(2,1)}, bf16[1,3584,512]{2,1,0:T(8,128)(2,1)}, u32[]{:S(2)}, u32[]{:S(2)}) collective-permute-start(bf16[1,3584,512]{2,1,0:T(8,128)(2,1)} %up0), channel_id=1, source_target_pairs={{0,1},{1,0},{2,3},{3,2},{4,5},{5,4},{6,7},{7,6},{8,9},{9,8},{10,11... | collective-permute-start | bytes 11010056 | tf_op jit(solution)/shard_map/ppermute | solution.py:370
  41.4 61.3 %collective-permute-start.12 = (bf16[1,512,3584]{2,1,0:T(8,128)(2,1)}, bf16[1,512,3584]{2,1,0:T(8,128)(2,1)}, u32[]{:S(2)}, u32[]{:S(2)}) collective-permute-start(bf16[1,512,3584]{2,1,0:T(8,128)(2,1)} %down0), channel_id=1, source_target_pairs={{0,1},{1,0},{2,3},{3,2},{4,5},{5,4},{6,7},{7,6},{8,9},{9,8},{10,11... | collective-permute-start | bytes 11010056 | tf_op jit(solution)/shard_map/ppermute | solution.py:370
  41.4 61.3 %all-to-all-start = ((bf16[64,8,3584]{2,1,0:T(8,128)(2,1)}), bf16[64,8,3584]{2,1,0:T(8,128)(2,1)}, u32[]{:S(2)}, u32[]{:S(2)}) async-start(bf16[64,8,3584]{2,1,0:T(8,128)(2,1)} %bitcast.14), calls=%async_computation | async-start | bytes 7340032 | tf_op jit(solution)/shard_map/all_to_all | solution.py:402
  48.5 1.4 copy-start.16
  48.5 1.5 copy-start.14
  48.6 10.7 %copy-start.7 = (bf16[128,3584]{1,0:T(8,128)(2,1)S(1)}, bf16[128,3584]{1,0:T(8,128)(2,1)}, u32[]{:S(2)}) copy-start(bf16[128,3584]{1,0:T(8,128)(2,1)} %hidden_ref.3) | copy-start | bytes 2752516
  48.6 10.6 %copy-start.8 = (f32[512]{0:T(512)S(1)}, f32[512]{0:T(512)}, u32[]{:S(2)}) copy-start(f32[512]{0:T(512)} %param.12) | copy-start | bytes 6148
  50.1 9.2 %collective-permute-start.6 = (bf16[16,112,576]{2,1,0:T(8,128)(2,1)S(1)}, bf16[16,112,576]{2,1,0:T(8,128)(2,1)}, u32[]{:S(2)}, u32[]{:S(2)}) collective-permute-start(bf16[16,112,576]{2,1,0:T(8,128)(2,1)S(1)} %constant_dynamic-update-slice_fusion.mine_ref), channel_id=1, source_target_pairs={{0,1},{1,0},{2,3},{3,2},{4,5},{5,4},{6,7},{7,6},{8,9},{9,8},{10,11... | collective-permute-start | bytes 6193160 | tf_op jit(solution)/shard_map/ppermute | solution.py:370
  64.2 59.9 %collective-permute-start.7 = (bf16[128,576]{1,0:T(8,128)(2,1)S(1)}, bf16[128,576]{1,0:T(8,128)(2,1)S(1)}, u32[]{:S(2)}, u32[]{:S(2)}) collective-permute-start(bf16[128,576]{1,0:T(8,128)(2,1)S(1)} %shard_map.114), channel_id=1, source_target_pairs={{0,2},{2,4},{4,6},{6,0},{1,3},{3,5},{5,7},{7,1},{8,10},{10,12},{12... | collective-permute-start | bytes 442376 | tf_op jit(solution)/shard_map/ppermute | solution.py:375
  65.9 58.2 %collective-permute-start.8 = (bf16[128,576]{1,0:T(8,128)(2,1)S(1)}, bf16[128,576]{1,0:T(8,128)(2,1)S(1)}, u32[]{:S(2)}, u32[]{:S(2)}) collective-permute-start(bf16[128,576]{1,0:T(8,128)(2,1)S(1)} %shard_map.114), channel_id=1, source_target_pairs={{0,4},{2,6},{4,0},{6,2},{1,5},{3,7},{5,1},{7,3},{8,12},{10,14},{12... | collective-permute-start | bytes 442376 | tf_op jit(solution)/shard_map/ppermute | solution.py:375
  68.6 55.5 %collective-permute-start.9 = (bf16[128,576]{1,0:T(8,128)(2,1)S(1)}, bf16[128,576]{1,0:T(8,128)(2,1)S(1)}, u32[]{:S(2)}, u32[]{:S(2)}) collective-permute-start(bf16[128,576]{1,0:T(8,128)(2,1)S(1)} %shard_map.114), channel_id=1, source_target_pairs={{0,6},{2,0},{4,2},{6,4},{1,7},{3,1},{5,3},{7,5},{8,14},{10,8},{12,... | collective-permute-start | bytes 442376 | tf_op jit(solution)/shard_map/ppermute | solution.py:375
  124.5 2.1 %collective-permute-start.13 = (bf16[512,576]{0,1:T(8,128)(2,1)S(1)}, bf16[512,576]{0,1:T(8,128)(2,1)S(1)}, u32[]{:S(2)}, u32[]{:S(2)}) collective-permute-start(bf16[512,576]{0,1:T(8,128)(2,1)S(1)} %copy.16), channel_id=1, source_target_pairs={{0,1},{1,0},{2,3},{3,2},{4,5},{5,4},{6,7},{7,6},{8,9},{9,8},{10,11... | collective-permute-start | bytes 1769480 | tf_op jit(solution)/shard_map/ppermute | solution.py:370
  126.9 1.1 copy-start.4
  128.0 7.3 %copy-start.2 = (bf16[128,12288]{1,0:T(8,128)(2,1)S(1)}, bf16[128,12288]{1,0:T(8,128)(2,1)}, u32[]{:S(2)}) copy-start(bf16[128,12288]{1,0:T(8,128)(2,1)} %mine_ref) | copy-start | bytes 9437188
  128.0 55.8 %all-to-all-start.1 = ((bf16[64,8,3584]{2,1,0:T(8,128)(2,1)}), bf16[64,8,3584]{2,1,0:T(8,128)(2,1)}, u32[]{:S(2)}, u32[]{:S(2)}) async-start(bf16[64,8,3584]{2,1,0:T(8,128)(2,1)} %bitcast.19), calls=%async_computation.1 | async-start | bytes 7340032 | tf_op jit(solution)/shard_map/all_to_all | solution.py:402
  136.3 3.7 %collective-permute-start.14 = (bf16[128,6144]{1,0:T(8,128)(2,1)S(1)}, bf16[128,6144]{1,0:T(8,128)(2,1)S(1)}, u32[]{:S(2)}, u32[]{:S(2)}) collective-permute-start(bf16[128,6144]{1,0:T(8,128)(2,1)S(1)} %shard_map.116), channel_id=1, source_target_pairs={{0,1},{1,0},{2,3},{3,2},{4,5},{5,4},{6,7},{7,6},{8,9},{9,8},{10,11... | collective-permute-start | bytes 4718600 | tf_op jit(solution)/shard_map/ppermute | solution.py:370
  140.0 1.3 copy-start.5
  169.4 2.7 %collective-permute-start.15 = (bf16[128,4096]{1,0:T(8,128)(2,1)S(1)}, bf16[128,4096]{1,0:T(8,128)(2,1)S(1)}, u32[]{:S(2)}, u32[]{:S(2)}) collective-permute-start(bf16[128,4096]{1,0:T(8,128)(2,1)S(1)} %get-tuple-element.40), channel_id=1, source_target_pairs={{0,1},{1,0},{2,3},{3,2},{4,5},{5,4},{6,7},{7,6},{8,9},{9,8},{10,11... | collective-permute-start | bytes 3145736 | tf_op jit(solution)/shard_map/ppermute | solution.py:370
  172.0 11.8 %copy-start.12 = (bf16[384,512]{1,0:T(8,128)(2,1)S(1)}, bf16[384,512]{1,0:T(8,128)(2,1)}, u32[]{:S(2)}) copy-start(bf16[384,512]{1,0:T(8,128)(2,1)} %copy-done.11) | copy-start | bytes 1179652
  183.8 4.1 %copy-start.1 = (bf16[224,576]{1,0:T(8,128)(2,1)S(1)}, bf16[224,576]{1,0:T(8,128)(2,1)}, u32[]{:S(2)}) copy-start(bf16[224,576]{1,0:T(8,128)(2,1)} %param.11) | copy-start | bytes 774148
Sparse Core Ops, SparseCore 0:
  10.9 122.8 all-gather.1
